TPU v7x, 32 devices: a whole 2x2x4 slice. The times are simulated.
32 devices in a mesh: dp: 2 (over x), expert: 16 (over z, y, core).
Axes of the slice: x: 2, y: 2, z: 4, core: 2. Of those that a mesh axis runs over, the one named last changes fastest.
Arguments:
- tokens: bfloat16 [2048, 2048], P('expert', 'dp'), may hold values from -6 to 6
- expert_ids: int32 [2048, 8], P('expert'), may hold values from 0 to 15, all different within a row; in each aligned block of 128 rows (0 to 127, 128 to 255, ...) at most 96 rows name the same one
- chosen_probs: float32 [2048, 8], P('expert'), may hold values from 0.05 to 1
- gate_weight: bfloat16 [16, 1536, 2048], P('expert', 'dp'), may hold values from -0.125 to 0.125
- up_weight: bfloat16 [16, 1536, 2048], P('expert', 'dp'), may hold values from -0.125 to 0.125
- down_weight: bfloat16 [16, 1536, 2048], P('expert', 'dp'), may hold values from -0.15625 to 0.15625
Outputs:
- mixed: bfloat16 [2048, 2048], P('expert', 'dp')
Inputs may be any that keep to these rules, and one draw needn't show every extreme that they name: `expert_ids`: each row names 8 different experts; the 128 rows of one device name each expert at most 96 times, a bound that some block reaches.
All inputs are finite; a program needn't handle non-finite values.
Results may differ from a plain program's by a relative error of at most 0.0058.
Values may be sent and summed in bfloat16 or wider, within the bound.
No kernel may reach another device: no remote copies, remote signals or barrier semaphores. Data moves between devices by JAX's collectives and lax.ppermute only.
A program may use at most 128 MiB of HBM per device.

v0:
```python
import jax
import jax.numpy as jnp
from jax import lax
from jax.sharding import PartitionSpec as P


def local(tokens, expert_ids, chosen_probs, gate_weight, up_weight, down_weight):
    n_experts = lax.axis_size("expert")
    tok_rows = expert_ids.shape[0]
    top_count = expert_ids.shape[1]
    capacity = min(
        tok_rows, max(2, (3 * tok_rows * top_count + 2 * n_experts - 1) // (2 * n_experts))
    )
    route = chosen_probs / jnp.sum(chosen_probs, axis=1, keepdims=True)
    flat = expert_ids.reshape(-1)
    onehot = (flat[:, None] == jnp.arange(n_experts, dtype=jnp.int32)[None, :]).astype(jnp.int32)
    slot = jnp.sum(onehot * (jnp.cumsum(onehot, axis=0) - 1), axis=1)
    place = flat * capacity + slot
    tok_index = jnp.arange(tok_rows * top_count, dtype=jnp.int32) // top_count
    source = lax.all_gather(tokens, "dp", axis=1, tiled=True)
    columns_now = source.shape[1]
    buffer = (
        jnp.zeros((n_experts * capacity, columns_now), jnp.bfloat16)
        .at[place]
        .set(source[tok_index])
    )
    outgoing = buffer.reshape(n_experts, capacity, columns_now)
    gate_local = gate_weight[0]
    up_local = up_weight[0]
    down_local = down_weight[0]
    arrived = lax.all_to_all(outgoing, "expert", split_axis=0, concat_axis=0, tiled=True)
    gate = jnp.einsum("snd,fd->snf", arrived, gate_local, preferred_element_type=jnp.float32)
    up = jnp.einsum("snd,fd->snf", arrived, up_local, preferred_element_type=jnp.float32)
    hidden = (jax.nn.silu(gate) * up).astype(jnp.bfloat16)
    produced = jnp.einsum(
        "snf,fd->snd", hidden, down_local, preferred_element_type=jnp.float32
    ).astype(jnp.bfloat16)
    returned = lax.all_to_all(produced, "expert", split_axis=0, concat_axis=0, tiled=True)
    width = returned.shape[2]
    picked = returned.reshape(n_experts * capacity, width)[place]
    weighted = picked.astype(jnp.float32) * route.reshape(-1)[:, None]
    partial_out = jnp.sum(weighted.reshape(tok_rows, top_count, width), axis=1)
    return lax.psum_scatter(partial_out, "dp", scatter_dimension=1, tiled=True).astype(jnp.bfloat16)


def solution(mesh):
    in_specs = (
        P("expert", "dp"),
        P("expert", None),
        P("expert", None),
        P("expert", "dp", None),
        P("expert", "dp", None),
        P("expert", "dp", None),
    )
    out_specs = P("expert", "dp")
    return jax.shard_map(local, mesh=mesh, in_specs=in_specs, out_specs=out_specs, check_vma=False)
```

profile of v0, /device:TPU:0, one launch (start us, length us, event | category | flops | bytes accessed | tf_op | source)
XLA Modules:
  0.0 410.7 jit_solution(5039450729393087225)
XLA Ops:
  6.5 0.0 copy-start
  6.5 0.9 copy.11
  7.5 0.1 eq.29
  7.6 0.1 eq.25
  7.7 0.7 broadcast_multiply_fusion
  8.4 4.5 %reduce-window.6 = s32[16,8,128]{2,1,0:T(8,128)S(1)} reduce-window(s32[16,8,128]{2,1,0:T(8,128)S(1)} %fusion.15, s32[]{:T(128)} %constant.30.clone.1), window={size=1x1x128 pad=0_0x0_0x127_0}, to_apply=%region_0.0 | reduce-window | flops 2080768 | bytes 131076 | tf_op jit(solution)/shard_map/reduce-window
  12.9 0.1 slice.12
  13.0 0.1 copy.13
  13.1 0.1 copy.14
  13.2 0.1 add_add_fusion
  13.3 0.1 copy.10
  13.4 0.1 mul.37
  13.5 11.9 %all_gather.3 = bf16[128,2048]{1,0:T(8,128)(2,1)} all-gather(bf16[128,1024]{1,0:T(8,128)(2,1)} %param.6), channel_id=1, replica_groups=mesh['dp'=2,'expert'=16] {'dp'}, dimensions={1}, use_global_device_ids=true | all-gather | bytes 786432 | tf_op jit(solution)/shard_map/all_gather | solution.py:20
  25.4 24.3 %scatter_custom_fusion = bf16[1536,2048]{1,0:T(8,128)(2,1)} fusion(s32[1024]{0:T(1024)S(1)} %bitcast.44, bf16[128,2048]{1,0:T(8,128)(2,1)} %all_gather.3, s32[1024]{0:T(1024)S(1)} %broadcast_clamp_fusion.1, bf16[]{:T(256)} %constant.28.clone.1), kind=kCustom, calls=%fused_computation.7 | custom fusion | bytes 6291968 | tf_op jit(solution)/shard_map/scatter | solution.py:25
  49.7 0.0 copy-start.3
  49.7 143.4 %all_to_all.10 = bf16[16,96,2048]{2,1,0:T(8,128)(2,1)S(1)} all-to-all(bf16[16,96,2048]{2,1,0:T(8,128)(2,1)} %bitcast.40), channel_id=1, replica_groups=mesh['dp'=2,'expert'=16] {'expert'}, dimensions={0} | all-to-all | bytes 12582912 | tf_op jit(solution)/shard_map/all_to_all | solution.py:31
  193.1 0.0 copy-start.1
  193.1 2.7 copy-done.1
  195.8 0.0 copy-done.3
  195.8 6.7 %fusion.4 = f32[16,96,768]{2,1,0:T(8,128)} fusion(bf16[16,96,2048]{2,1,0:T(8,128)(2,1)S(1)} %all_to_all.10, bf16[1,768,2048]{2,1,0:T(8,128)(2,1)S(1)} %copy-done.3), kind=kOutput, calls=%fused_computation.10 | convolution fusion | flops 4831838208 | bytes 14155776 | tf_op jit(solution)/shard_map/snd,fd->snf/dot_general | solution.py:33
  202.5 0.0 copy-done
  202.5 16.9 %convolution_convert_fusion = bf16[16,96,2048]{2,1,0:T(8,128)(2,1)} fusion(bf16[1,768,2048]{2,1,0:T(8,128)(2,1)S(1)} %copy-done, f32[16,96,768]{2,1,0:T(8,128)} %fusion.4, bf16[16,96,2048]{2,1,0:T(8,128)(2,1)} %copy-done.1, bf16[1,768,2048]{2,1,0:T(8,128)(2,1)} %param.9), kind=kOutput, calls=%fused_computation.6 | convolution fusion | flops 9673900032 | bytes 23592960 | tf_op jit(solution)/shard_map/snf,fd->snd/dot_general | solution.py:35
  219.4 0.0 copy-start.2
  219.4 5.7 %all-to-all-start.1 = ((bf16[16,96,2048]{2,1,0:T(8,128)(2,1)}), bf16[16,96,2048]{2,1,0:T(8,128)(2,1)}, u32[]{:S(2)}, u32[]{:S(2)}) async-start(bf16[16,96,2048]{2,1,0:T(8,128)(2,1)} %convolution_convert_fusion), calls=%async_computation.1 | async-start | bytes 12582912 | tf_op jit(solution)/shard_map/all_to_all | solution.py:38
  225.1 0.3 reduce-scatter.2.cloned.1.call-start
  225.4 0.0 copy-done.2
  225.4 0.1 copy.15
  225.5 113.8 %all-to-all-done.1 = bf16[16,96,2048]{2,1,0:T(8,128)(2,1)} async-done(((bf16[16,96,2048]{2,1,0:T(8,128)(2,1)}), bf16[16,96,2048]{2,1,0:T(8,128)(2,1)}, u32[]{:S(2)}, u32[]{:S(2)}) %all-to-all-start.1) | async-done | bytes 6291488 | tf_op jit(solution)/shard_map/all_to_all | solution.py:38
  339.3 12.4 %gather_fusion = bf16[1024,2048]{1,0:T(8,128)(2,1)} fusion(bf16[1536,2048]{1,0:T(8,128)(2,1)} %bitcast.12, s32[1024]{0:T(1024)S(1)} %broadcast_clamp_fusion), kind=kCustom, calls=%fused_computation.1 | custom fusion | bytes 8392704 | tf_op jit(solution)/shard_map/gather | solution.py:40
  351.7 7.5 %fusion = f32[128,2048]{1,0:T(8,128)} fusion(bf16[1024,2048]{1,0:T(8,128)(2,1)} %gather_fusion, f32[128,8]{1,0:T(8,128)S(1)} %copy.15), kind=kLoop, calls=%fused_computation.4 | loop fusion | flops 6029312 | bytes 5246976 | tf_op jit(solution)/shard_map/reduce_sum | solution.py:42
  359.2 0.0 reduce-scatter.2.cloned.1.call-update
  359.2 42.9 %reduce-scatter.2.cloned.1.call-done = f32[128,1024]{1,0:T(8,128)} async-done(((f32[128,2048]{1,0:T(8,128)}), f32[128,1024]{1,0:T(8,128)}) %reduce-scatter.2.cloned.1.call-update) | async-done | bytes 524304 | tf_op jit(solution)/shard_map/reduce_scatter | solution.py:43
  402.1 1.8 convert_element_type.26
  (10 shorter events, 0.1 us)
Async XLA Ops:
  6.5 195.9 %copy-start = (bf16[1,768,2048]{2,1,0:T(8,128)(2,1)S(1)}, bf16[1,768,2048]{2,1,0:T(8,128)(2,1)}, u32[]{:S(2)}) copy-start(bf16[1,768,2048]{2,1,0:T(8,128)(2,1)} %param.11) | copy-start | bytes 9437188
  49.7 146.1 %copy-start.3 = (bf16[1,768,2048]{2,1,0:T(8,128)(2,1)S(1)}, bf16[1,768,2048]{2,1,0:T(8,128)(2,1)}, u32[]{:S(2)}) copy-start(bf16[1,768,2048]{2,1,0:T(8,128)(2,1)} %param.10) | copy-start | bytes 9437188
  193.1 2.7 copy-start.1
  219.4 5.9 %copy-start.2 = (f32[128,8]{0,1:T(8,128)S(1)}, f32[128,8]{0,1:T(8,128)}, u32[]{:S(2)}) copy-start(f32[128,8]{0,1:T(8,128)} %param.8) | copy-start | bytes 12292
  219.4 119.9 %all-to-all-start.1 = ((bf16[16,96,2048]{2,1,0:T(8,128)(2,1)}), bf16[16,96,2048]{2,1,0:T(8,128)(2,1)}, u32[]{:S(2)}, u32[]{:S(2)}) async-start(bf16[16,96,2048]{2,1,0:T(8,128)(2,1)} %convolution_convert_fusion), calls=%async_computation.1 | async-start | bytes 12582912 | tf_op jit(solution)/shard_map/all_to_all | solution.py:38
  225.1 177.0 %reduce-scatter.2.cloned.1.call-start = ((), (), s32[]{:S(2)}) async-start(), calls=%async_computation.3 | async-start | bytes 1572864 | tf_op jit(solution)/shard_map/reduce_scatter | solution.py:43
Sparse Core Ops, SparseCore 0:
  359.3 42.7 reduce-scatter.1
where the time goes:
time: 411 us
  waiting for transfers between devices  157 us (38%)
  blocking collectives  155 us (38%)
  local copies, waits for them, and re-layouts  41.1 us (10%)
  matrix products  23.6 us (6%)
  other arithmetic  14.6 us (4%)
  between operations  13.5 us (3%)
  starting transfers between devices  5.93 us (1%)
    all_to_all x1, blocking collectives, local(): lax.all_to_all(outgoing, 'expert', split_axis=0, concat_axis=0, tiled=True)  143 us
    all_to_all x1, waiting for transfers between devices, local(): lax.all_to_all(produced, 'expert', split_axis=0, concat_axis=0, tiled=True)  114 us
    reduce_scatter x1, waiting for transfers between devices, local(): lax.psum_scatter(partial_out, 'dp', scatter_dimension=1, tiled=True)  42.9 us
    scatter x1, local copies, waits for them, and re-layouts, local(): buffer = jnp.zeros((n_experts * capacity, columns_now), jnp.bfloat16).at[...  24.3 us
    dot_general x1, matrix products, local(): jnp.einsum('snf,fd->snd', hidden, down_local, preferred_element_type=jnp....  16.9 us
    gather x1, local copies, waits for them, and re-layouts, local(): picked = returned.reshape(n_experts * capacity, width)[place]  12.4 us
    all_gather x1, blocking collectives, local(): source = lax.all_gather(tokens, 'dp', axis=1, tiled=True)  11.9 us
  transfers between devices with their start and end apart: 2, of which 2 were waited for; matrix products, arithmetic and copies ran while one was open for 0% of the time, Pallas kernels for 0%

commit v1 on v0

--- a/solution.py
+++ b/solution.py
@@ -1,10 +1,14 @@
 import jax
 import jax.numpy as jnp
 from jax import lax
+from jax.experimental import pallas as pl
+from jax.experimental.pallas import tpu as pltpu
 from jax.sharding import PartitionSpec as P
 
+CHUNKS = 2
 
-def local(tokens, expert_ids, chosen_probs, gate_weight, up_weight, down_weight):
+
+def exchange(tokens, expert_ids, chosen_probs, gate_weight, up_weight, down_weight):
     n_experts = lax.axis_size("expert")
     tok_rows = expert_ids.shape[0]
     top_count = expert_ids.shape[1]
@@ -43,7 +47,120 @@
     return lax.psum_scatter(partial_out, "dp", scatter_dimension=1, tiled=True).astype(jnp.bfloat16)
 
 
+def swap(value, mask):
+    n = lax.axis_size("expert")
+    return lax.ppermute(value, "expert", [(i, i ^ mask) for i in range(n)])
+
+
+def swap_dp(value):
+    return lax.ppermute(value, "dp", [(0, 1), (1, 0)])
+
+
+def ffn_kernel(n_blocks, half_ref, *refs):
+    xs = refs[:n_blocks]
+    w_ref, gate_ref, up_ref, down_ref = refs[n_blocks:n_blocks + 4]
+    outs = refs[n_blocks + 4:n_blocks * 2 + 4]
+    part = xs[0].shape[2]
+    mine = half_ref[0]
+    here = [pl.ds(pl.multiple_of((mine if s == 0 else 1 - mine) * part, part), part) for s in range(2)]
+    nt = (((1,), (1,)), ((), ()))
+    for b in range(n_blocks):
+        gate = lax.dot_general(xs[b][0], gate_ref[:, here[0]], nt, preferred_element_type=jnp.float32)
+        gate += lax.dot_general(xs[b][1], gate_ref[:, here[1]], nt, preferred_element_type=jnp.float32)
+        up = lax.dot_general(xs[b][0], up_ref[:, here[0]], nt, preferred_element_type=jnp.float32)
+        up += lax.dot_general(xs[b][1], up_ref[:, here[1]], nt, preferred_element_type=jnp.float32)
+        hidden = (gate / (1.0 + jnp.exp(-gate)) * up * w_ref[b]).astype(jnp.bfloat16)
+        for s in range(2):
+            outs[b][s] = jnp.dot(
+                hidden, down_ref[:, here[s]], preferred_element_type=jnp.float32
+            ).astype(jnp.bfloat16)
+
+
+def ffn(xs, weights, gate, up, down, mine):
+    n_blocks = len(xs)
+    rows, part = xs[0].shape[1:]
+    flops = 6 * n_blocks * rows * gate.shape[0] * gate.shape[1]
+    vmem = pl.BlockSpec(memory_space=pltpu.VMEM)
+    return pl.pallas_call(
+        lambda *refs: ffn_kernel(n_blocks, *refs),
+        out_shape=[jax.ShapeDtypeStruct((2, rows, part), jnp.bfloat16)] * n_blocks,
+        in_specs=[pl.BlockSpec(memory_space=pltpu.SMEM)] + [vmem] * (n_blocks + 4),
+        out_specs=[vmem] * n_blocks,
+        compiler_params=pltpu.CompilerParams(vmem_limit_bytes=48 * 2**20),
+        cost_estimate=pl.CostEstimate(
+            flops=flops,
+            bytes_accessed=6 * gate.size + 8 * n_blocks * rows * part,
+            transcendentals=n_blocks * rows * gate.shape[0],
+        ),
+        name="ffn",
+    )(mine, *xs, weights, gate, up, down)
+
+
+def gather_all(tokens, expert_ids, chosen_probs, gate_weight, up_weight, down_weight):
+    n_experts = lax.axis_size("expert")
+    tok_rows, part = tokens.shape
+    me = lax.axis_index("expert")
+    mine = lax.axis_index("dp").reshape(1).astype(jnp.int32)
+    gate, up, down = gate_weight[0], up_weight[0], down_weight[0]
+
+    route = chosen_probs / jnp.sum(chosen_probs, axis=1, keepdims=True)
+    chosen = expert_ids.T[None] == jnp.arange(n_experts, dtype=jnp.int32)[:, None, None]
+    dense = jnp.sum(jnp.where(chosen, route.T[None], 0.0), axis=1)
+    dense = lax.all_to_all(dense, "expert", split_axis=0, concat_axis=0, tiled=True)
+
+    line = [1 << k for k in range(n_experts.bit_length() - 2, 1, -1)]
+    step = tok_rows // CHUNKS
+    finished = []
+    for c in range(CHUNKS):
+        masks = [0]
+        t = tokens[None, c * step:(c + 1) * step]
+        for m in line:
+            t = jnp.concatenate([t, swap(t, m)], axis=0)
+            masks = masks + [k ^ m for k in masks]
+        masks = masks + [k ^ 2 for k in masks]
+        n_slots = len(masks)
+        a, b = t[:, :step // 2], t[:, step // 2:]
+        a = jnp.stack([a, swap_dp(a)])
+        b = jnp.concatenate([b, swap(b, 2)], axis=0)
+        a = jnp.concatenate([a, swap(a, 2)], axis=1)
+        b = jnp.stack([b, swap_dp(b)])
+        a = a.reshape(2, n_slots * step // 2, part)
+        b = b.reshape(2, n_slots * step // 2, part)
+        xs = [a, swap(a, 1), b, swap(b, 1)]
+        weights = []
+        for p in range(2):
+            for core in range(2):
+                rows = slice(c * step + p * step // 2, c * step + (p + 1) * step // 2)
+                order = me ^ jnp.array([k ^ core for k in masks], jnp.int32)
+                weights.append(dense[:, rows][order].reshape(-1, 1))
+        outs = ffn(xs, jnp.stack(weights), gate, up, down, mine)
+        shape = (2, 2, n_slots // 2, step // 2, part)
+        a0, a1, b0, b1 = [o.reshape(shape).astype(jnp.float32) for o in outs]
+
+        def add(keep, got):
+            return keep + got.astype(jnp.float32)
+
+        def send(v):
+            return v.astype(jnp.bfloat16)
+
+        a = add(a0, swap(send(a1), 1))
+        b = add(b0, swap(send(b1), 1))
+        a = add(a[:, 0], swap(send(a[:, 1]), 2))
+        b = add(b[0], swap_dp(send(b[1])))
+        a = add(a[0], swap_dp(send(a[1])))
+        b = add(b[0], swap(send(b[1]), 2))
+        t = jnp.concatenate([a, b], axis=1)
+        for m in reversed(line):
+            n = t.shape[0] // 2
+            t = add(t[:n], swap(send(t[n:]), m))
+        finished.append(t[0].astype(jnp.bfloat16))
+    return jnp.concatenate(finished, axis=0)
+
+
 def solution(mesh):
+    n_dp, n_experts = mesh.shape["dp"], mesh.shape["expert"]
+    powers = n_experts & (n_experts - 1) == 0
+    few = n_dp == 2 and powers and 4 <= n_experts <= 32
     in_specs = (
         P("expert", "dp"),
         P("expert", None),
@@ -52,5 +169,10 @@
         P("expert", "dp", None),
         P("expert", "dp", None),
     )
-    out_specs = P("expert", "dp")
-    return jax.shard_map(local, mesh=mesh, in_specs=in_specs, out_specs=out_specs, check_vma=False)
+    return jax.shard_map(
+        gather_all if few else exchange,
+        mesh=mesh,
+        in_specs=in_specs,
+        out_specs=P("expert", "dp"),
+        check_vma=False,
+    )

time: 411 us -> 166 us (0.40)
  blocking collectives: 155 us -> 0 us
  waiting for transfers between devices: 157 us -> 71.1 us
  starting transfers between devices: 5.93 us -> 42.9 us
  local copies, waits for them, and re-layouts: 41.1 us -> 10.5 us
  Pallas kernels: 0 us -> 30.5 us
  matrix products: 23.6 us -> 0 us
  between operations: 13.5 us -> 0.55 us
  other arithmetic: 14.6 us -> 10.4 us
    all_to_all x1 -> x0, blocking collectives: 143 us -> none  [local(): lax.all_to_all(outgoing, 'expert', split_axis=0, concat_axis=0, tiled=True)]
    all_to_all x1, waiting for transfers between devices: 114 us -> 0.01 us  [gather_all(): lax.all_to_all(dense, 'expert', split_axis=0, concat_axis=0, tiled=True)]
    ppermute x0 -> x32, waiting for transfers between devices: none -> 71.1 us  [the longest x24 42.8 us: swap(): return lax.ppermute(value, 'expert', [(i, i ^ mask) for i in range(n)])]
    reduce_scatter x1 -> x0, waiting for transfers between devices: 42.9 us -> none  [local(): lax.psum_scatter(partial_out, 'dp', scatter_dimension=1, tiled=True)]
    ppermute x0 -> x32, starting transfers between devices: none -> 37 us  [the longest x24 28.2 us: swap(): return lax.ppermute(value, 'expert', [(i, i ^ mask) for i in range(n)])]
    pallas_call x0 -> x2, Pallas kernels: none -> 30.5 us  [ffn(): pl.pallas_call(lambda *refs: ffn_kernel(n_blocks, *refs), out_shape=[jax....]
    scatter x1 -> x0, local copies, waits for them, and re-layouts: 24.3 us -> none  [local(): buffer = jnp.zeros((n_experts * capacity, columns_now), jnp.bfloat16).at[...]
    dot_general x2 -> x0, matrix products: 23.6 us -> none  [the longest x1 16.9 us: local(): jnp.einsum('snf,fd->snd', hidden, down_local, preferred_element_type=jnp....]
  transfers between devices with their start and end apart: 2 -> 33, of which waited for: 2 -> 17; matrix products, arithmetic and copies ran while one was open for 0% -> 10% of each run, Pallas kernels for 0% -> 18%
where the time goes in v1:
time: 166 us
  waiting for transfers between devices  71.1 us (43%)
  starting transfers between devices  42.9 us (26%)
  Pallas kernels  30.5 us (18%)
  local copies, waits for them, and re-layouts  10.5 us (6%)
  other arithmetic  10.4 us (6%)
    ppermute x24, waiting for transfers between devices, swap(): return lax.ppermute(value, 'expert', [(i, i ^ mask) for i in range(n)])  42.8 us
    pallas_call x2, Pallas kernels, ffn(): pl.pallas_call(lambda *refs: ffn_kernel(n_blocks, *refs), out_shape=[jax....  30.5 us
    ppermute x8, waiting for transfers between devices, swap_dp(): return lax.ppermute(value, 'dp', [(0, 1), (1, 0)])  28.3 us
    ppermute x24, starting transfers between devices, swap(): return lax.ppermute(value, 'expert', [(i, i ^ mask) for i in range(n)])  28.2 us
    ppermute x8, starting transfers between devices, swap_dp(): return lax.ppermute(value, 'dp', [(0, 1), (1, 0)])  8.86 us
    all_to_all x1, starting transfers between devices, gather_all(): lax.all_to_all(dense, 'expert', split_axis=0, concat_axis=0, tiled=True)  5.9 us
    gather x8, local copies, waits for them, and re-layouts, gather_all(): weights.append(dense[:, rows][order].reshape(-1, 1))  4.45 us
  transfers between devices with their start and end apart: 33, of which 17 were waited for; matrix products, arithmetic and copies ran while one was open for 10% of the time, Pallas kernels for 18%

profile of v1, /device:TPU:0, one launch (start us, length us, event | category | flops | bytes accessed | tf_op | source)
XLA Modules:
  0.0 166.1 jit_solution(2072105508188828997)
XLA Ops:
  0.0 1.0 slice_bitcast_fusion.9
  1.0 4.1 %collective-permute-start = (bf16[1,64,1024]{2,1,0:T(8,128)(2,1)S(1)}, bf16[1,64,1024]{2,1,0:T(8,128)(2,1)S(1)}, u32[]{:S(2)}, u32[]{:S(2)}) collective-permute-start(bf16[1,64,1024]{2,1,0:T(8,128)(2,1)S(1)} %get-tuple-element.27), channel_id=1, source_target_pairs={{0,8},{1,9},{2,10},{3,11},{4,12},{5,13},{6,14},{7,15},{8,0},{9,1},... | collective-permute-start | bytes 393224 | tf_op jit(solution)/shard_map/ppermute | solution.py:52
  5.1 6.3 %collective-permute-done = bf16[1,64,1024]{2,1,0:T(8,128)(2,1)S(1)} collective-permute-done((bf16[1,64,1024]{2,1,0:T(8,128)(2,1)S(1)}, bf16[1,64,1024]{2,1,0:T(8,128)(2,1)S(1)}, u32[]{:S(2)}, u32[]{:S(2)}) %collective-permute-start) | collective-permute-done | bytes 131104 | tf_op jit(solution)/shard_map/ppermute | solution.py:52
  11.5 0.8 collective-permute-start.1
  12.2 3.4 %collective-permute-start.16 = (bf16[1,64,1024]{2,1,0:T(8,128)(2,1)S(1)}, bf16[1,64,1024]{2,1,0:T(8,128)(2,1)S(1)}, u32[]{:S(2)}, u32[]{:S(2)}) collective-permute-start(bf16[1,64,1024]{2,1,0:T(8,128)(2,1)S(1)} %get-tuple-element.28), channel_id=1, source_target_pairs={{0,8},{1,9},{2,10},{3,11},{4,12},{5,13},{6,14},{7,15},{8,0},{9,1},... | collective-permute-start | bytes 393224 | tf_op jit(solution)/shard_map/ppermute | solution.py:52
  15.6 0.7 reduce_sum.18
  16.3 5.5 %collective-permute-done.1 = bf16[2,64,1024]{2,1,0:T(8,128)(2,1)S(1)} collective-permute-done((bf16[2,64,1024]{2,1,0:T(8,128)(2,1)S(1)}, bf16[2,64,1024]{2,1,0:T(8,128)(2,1)S(1)}, u32[]{:S(2)}, u32[]{:S(2)}) %collective-permute-start.1) | collective-permute-done | bytes 262176 | tf_op jit(solution)/shard_map/ppermute | solution.py:52
  22.0 1.3 collective-permute-start.5
  23.3 1.5 collective-permute-start.2
  25.5 5.9 %all-to-all-start = ((f32[16,1,128]{2,1,0:T(1,128)}), f32[16,1,128]{2,1,0:T(1,128)S(1)}, u32[]{:S(2)}, u32[]{:S(2)}) async-start(f32[16,1,128]{2,1,0:T(1,128)} %bitcast.10), calls=%async_computation | async-start | bytes 16384 | tf_op jit(solution)/shard_map/all_to_all | solution.py:109
  31.4 2.0 %collective-permute-start.17 = (bf16[2,64,1024]{2,1,0:T(8,128)(2,1)S(1)}, bf16[2,64,1024]{2,1,0:T(8,128)(2,1)S(1)}, u32[]{:S(2)}, u32[]{:S(2)}) collective-permute-start(bf16[2,64,1024]{2,1,0:T(8,128)(2,1)S(1)} %pad_maximum_fusion.15), channel_id=1, source_target_pairs={{0,4},{1,5},{2,6},{3,7},{4,0},{5,1},{6,2},{7,3},{8,12},{9,13},{10,... | collective-permute-start | bytes 786440 | tf_op jit(solution)/shard_map/ppermute | solution.py:52
  34.1 1.5 collective-permute-start.3
  35.7 4.6 %collective-permute-done.17 = bf16[2,64,1024]{2,1,0:T(8,128)(2,1)S(1)} collective-permute-done((bf16[2,64,1024]{2,1,0:T(8,128)(2,1)S(1)}, bf16[2,64,1024]{2,1,0:T(8,128)(2,1)S(1)}, u32[]{:S(2)}, u32[]{:S(2)}) %collective-permute-start.17) | collective-permute-done | bytes 262176 | tf_op jit(solution)/shard_map/ppermute | solution.py:52
  40.4 1.7 %collective-permute-start.21 = (bf16[4,32,1024]{2,1,0:T(8,128)(2,1)S(1)}, bf16[4,32,1024]{2,1,0:T(8,128)(2,1)S(1)}, u32[]{:S(2)}, u32[]{:S(2)}) collective-permute-start(bf16[4,32,1024]{2,1,0:T(8,128)(2,1)S(1)} %get-tuple-element.24), channel_id=1, source_target_pairs={{0,2},{1,3},{2,0},{3,1},{4,6},{5,7},{6,4},{7,5},{8,10},{9,11},{10,... | collective-permute-start | bytes 786440 | tf_op jit(solution)/shard_map/ppermute | solution.py:52
  42.6 5.7 %collective-permute-done.6 = bf16[8,32,1024]{2,1,0:T(8,128)(2,1)S(1)} collective-permute-done((bf16[8,32,1024]{2,1,0:T(8,128)(2,1)S(1)}, bf16[8,32,1024]{2,1,0:T(8,128)(2,1)S(1)}, u32[]{:S(2)}, u32[]{:S(2)}) %collective-permute-start.6) | collective-permute-done | bytes 524320 | tf_op jit(solution)/shard_map/ppermute | solution.py:56
  49.2 4.0 %collective-permute-done.21 = bf16[4,32,1024]{2,1,0:T(8,128)(2,1)S(1)} collective-permute-done((bf16[4,32,1024]{2,1,0:T(8,128)(2,1)S(1)}, bf16[4,32,1024]{2,1,0:T(8,128)(2,1)S(1)}, u32[]{:S(2)}, u32[]{:S(2)}) %collective-permute-start.21) | collective-permute-done | bytes 262176 | tf_op jit(solution)/shard_map/ppermute | solution.py:52
  53.3 1.5 collective-permute-start.22
  54.8 0.9 pad_maximum_fusion.11
  55.7 1.5 collective-permute-start.19
  60.1 5.9 %collective-permute-done.22 = bf16[8,32,1024]{2,1,0:T(8,128)(2,1)} collective-permute-done((bf16[8,32,1024]{2,1,0:T(8,128)(2,1)S(1)}, bf16[8,32,1024]{2,1,0:T(8,128)(2,1)}, u32[]{:S(2)}, u32[]{:S(2)}) %collective-permute-start.22) | collective-permute-done | bytes 524320 | tf_op jit(solution)/shard_map/ppermute | solution.py:56
  66.0 2.1 %pad_maximum_fusion.3.refs_3_ = bf16[2,256,1024]{2,1,0:T(8,128)(2,1)} fusion(bf16[1,256,1024]{2,1,0:T(8,128)(2,1)} %bitcast.33, bf16[1,256,1024]{2,1,0:T(8,128)(2,1)S(1)} %bitcast.102), kind=kLoop, calls=%fused_computation.29 | loop fusion | flops 524288 | bytes 2097152 | tf_op jit(solution)/shard_map/stack | solution.py:126
  68.3 1.1 pad_maximum_fusion.2
  69.9 15.6 %ffn.2 = (bf16[2,256,1024]{2,1,0:T(8,128)(2,1)S(1)}, bf16[2,256,1024]{2,1,0:T(8,128)(2,1)S(1)}, bf16[2,256,1024]{2,1,0:T(8,128)(2,1)S(1)}, bf16[2,256,1024]{2,1,0:T(8,128)(2,1)}) custom-call(s32[1]{0:T(128)} %bitcast.refs_0_, bf16[2,256,1024]{2,1,0:T(8,128)(2,1)S(1)} %bitcast.92, bf16[2,256,1024]{2,1,0:T(8,128)(2,1)} %collective-permute-done.4.refs_2_, ...), custom_call_target="tpu_custom_call" | custom-call | flops 9663676416 | bytes 17825792 | tf_op jit(solution)/shard_map/ffn/pallas_call | solution.py:84
  85.5 1.0 copy-done
  86.5 1.0 copy-done.2
  90.3 0.8 stack_reshape.39
  91.1 0.9 pad_maximum_fusion.13.refs_5_
  92.6 14.9 %ffn.3 = (bf16[2,256,1024]{2,1,0:T(8,128)(2,1)S(1)}, bf16[2,256,1024]{2,1,0:T(8,128)(2,1)S(1)}, bf16[2,256,1024]{2,1,0:T(8,128)(2,1)S(1)}, bf16[2,256,1024]{2,1,0:T(8,128)(2,1)S(1)}) custom-call(s32[1]{0:T(128)} %bitcast.refs_0_, bf16[2,256,1024]{2,1,0:T(8,128)(2,1)S(1)} %bitcast.94, bf16[2,256,1024]{2,1,0:T(8,128)(2,1)} %collective-permute-done.20.refs_2_, ...), custom_call_target="tpu_custom_call" | custom-call | flops 9663676416 | bytes 17825792 | tf_op jit(solution)/shard_map/ffn/pallas_call | solution.py:84
  109.1 1.5 collective-permute-start.12
  111.1 1.5 collective-permute-start.9
  113.1 0.7 collective-permute-start.28
  114.3 0.7 collective-permute-start.25
  115.0 9.0 %collective-permute-done.12 = bf16[2,4,32,1024]{3,2,1,0:T(8,128)(2,1)S(1)} collective-permute-done((bf16[2,4,32,1024]{3,2,1,0:T(8,128)(2,1)S(1)}, bf16[2,4,32,1024]{3,2,1,0:T(8,128)(2,1)S(1)}, u32[]{:S(2)}, u32[]{:S(2)}) %collective-permute-start.12) | collective-permute-done | bytes 524320 | tf_op jit(solution)/shard_map/ppermute | solution.py:56
  124.2 1.5 collective-permute-start.13
  126.2 1.2 collective-permute-start.10
  127.5 7.8 %collective-permute-done.28 = bf16[2,4,32,1024]{3,2,1,0:T(8,128)(2,1)S(1)} collective-permute-done((bf16[2,4,32,1024]{3,2,1,0:T(8,128)(2,1)S(1)}, bf16[2,4,32,1024]{3,2,1,0:T(8,128)(2,1)S(1)}, u32[]{:S(2)}, u32[]{:S(2)}) %collective-permute-start.28) | collective-permute-done | bytes 524320 | tf_op jit(solution)/shard_map/ppermute | solution.py:56
  135.4 1.5 collective-permute-start.29
  137.5 1.2 collective-permute-start.26
  138.7 4.2 %collective-permute-done.13 = bf16[4,32,1024]{2,1,0:T(8,128)(2,1)S(1)} collective-permute-done((bf16[4,32,1024]{2,1,0:T(8,128)(2,1)S(1)}, bf16[4,32,1024]{2,1,0:T(8,128)(2,1)S(1)}, u32[]{:S(2)}, u32[]{:S(2)}) %collective-permute-start.13) | collective-permute-done | bytes 262176 | tf_op jit(solution)/shard_map/ppermute | solution.py:52
  143.0 0.8 collective-permute-start.14
  143.8 3.4 %collective-permute-done.29 = bf16[4,32,1024]{2,1,0:T(8,128)(2,1)S(1)} collective-permute-done((bf16[4,32,1024]{2,1,0:T(8,128)(2,1)S(1)}, bf16[4,32,1024]{2,1,0:T(8,128)(2,1)S(1)}, u32[]{:S(2)}, u32[]{:S(2)}) %collective-permute-start.29) | collective-permute-done | bytes 262176 | tf_op jit(solution)/shard_map/ppermute | solution.py:52
  147.4 0.8 collective-permute-start.30
  148.2 1.7 %collective-permute-done.14 = bf16[2,64,1024]{2,1,0:T(8,128)(2,1)S(1)} collective-permute-done((bf16[2,64,1024]{2,1,0:T(8,128)(2,1)S(1)}, bf16[2,64,1024]{2,1,0:T(8,128)(2,1)S(1)}, u32[]{:S(2)}, u32[]{:S(2)}) %collective-permute-start.14) | collective-permute-done | bytes 262176 | tf_op jit(solution)/shard_map/ppermute | solution.py:52
  150.0 2.4 %collective-permute-start.15 = (bf16[1,64,1024]{2,1,0:T(8,128)(2,1)S(1)}, bf16[1,64,1024]{2,1,0:T(8,128)(2,1)S(1)}, u32[]{:S(2)}, u32[]{:S(2)}) collective-permute-start(bf16[1,64,1024]{2,1,0:T(8,128)(2,1)S(1)} %slice.281), channel_id=1, source_target_pairs={{0,8},{1,9},{2,10},{3,11},{4,12},{5,13},{6,14},{7,15},{8,0},{9,1},... | collective-permute-start | bytes 393224 | tf_op jit(solution)/shard_map/ppermute | solution.py:52
  152.4 5.5 %collective-permute-done.30 = bf16[2,64,1024]{2,1,0:T(8,128)(2,1)S(1)} collective-permute-done((bf16[2,64,1024]{2,1,0:T(8,128)(2,1)S(1)}, bf16[2,64,1024]{2,1,0:T(8,128)(2,1)S(1)}, u32[]{:S(2)}, u32[]{:S(2)}) %collective-permute-start.30) | collective-permute-done | bytes 262176 | tf_op jit(solution)/shard_map/ppermute | solution.py:52
  158.0 1.0 collective-permute-start.31
  159.0 6.3 %collective-permute-done.31 = bf16[1,64,1024]{2,1,0:T(8,128)(2,1)S(1)} collective-permute-done((bf16[1,64,1024]{2,1,0:T(8,128)(2,1)S(1)}, bf16[1,64,1024]{2,1,0:T(8,128)(2,1)S(1)}, u32[]{:S(2)}, u32[]{:S(2)}) %collective-permute-start.31) | collective-permute-done | bytes 131104 | tf_op jit(solution)/shard_map/ppermute | solution.py:52
  165.3 0.7 pad_maximum_fusion.16
  (113 shorter events, 14.9 us)
Async XLA Ops:
  0.0 23.3 %copy-start.7 = (f32[128,8]{0,1:T(8,128)S(1)}, f32[128,8]{0,1:T(8,128)}, u32[]{:S(2)}) copy-start(f32[128,8]{0,1:T(8,128)} %param.16) | copy-start | bytes 12292
  0.0 24.8 %copy-start.8 = (s32[128,8]{0,1:T(8,128)S(1)}, s32[128,8]{0,1:T(8,128)}, u32[]{:S(2)}) copy-start(s32[128,8]{0,1:T(8,128)} %param.15) | copy-start | bytes 12292
  1.0 10.4 %collective-permute-start = (bf16[1,64,1024]{2,1,0:T(8,128)(2,1)S(1)}, bf16[1,64,1024]{2,1,0:T(8,128)(2,1)S(1)}, u32[]{:S(2)}, u32[]{:S(2)}) collective-permute-start(bf16[1,64,1024]{2,1,0:T(8,128)(2,1)S(1)} %get-tuple-element.27), channel_id=1, source_target_pairs={{0,8},{1,9},{2,10},{3,11},{4,12},{5,13},{6,14},{7,15},{8,0},{9,1},... | collective-permute-start | bytes 393224 | tf_op jit(solution)/shard_map/ppermute | solution.py:52
  11.5 10.4 %collective-permute-start.1 = (bf16[2,64,1024]{2,1,0:T(8,128)(2,1)S(1)}, bf16[2,64,1024]{2,1,0:T(8,128)(2,1)S(1)}, u32[]{:S(2)}, u32[]{:S(2)}) collective-permute-start(bf16[2,64,1024]{2,1,0:T(8,128)(2,1)S(1)} %pad_maximum_fusion.14), channel_id=1, source_target_pairs={{0,4},{1,5},{2,6},{3,7},{4,0},{5,1},{6,2},{7,3},{8,12},{9,13},{10,... | collective-permute-start | bytes 786440 | tf_op jit(solution)/shard_map/ppermute | solution.py:52
  12.2 19.1 %collective-permute-start.16 = (bf16[1,64,1024]{2,1,0:T(8,128)(2,1)S(1)}, bf16[1,64,1024]{2,1,0:T(8,128)(2,1)S(1)}, u32[]{:S(2)}, u32[]{:S(2)}) collective-permute-start(bf16[1,64,1024]{2,1,0:T(8,128)(2,1)S(1)} %get-tuple-element.28), channel_id=1, source_target_pairs={{0,8},{1,9},{2,10},{3,11},{4,12},{5,13},{6,14},{7,15},{8,0},{9,1},... | collective-permute-start | bytes 393224 | tf_op jit(solution)/shard_map/ppermute | solution.py:52
  21.9 13.8 %copy-start.9 = (s32[8]{0:T(128)S(1)}, s32[8]{0:T(128)}, u32[]{:S(2)}) copy-start(s32[8]{0:T(128)} %constant.19.clone) | copy-start | bytes 100
  21.9 13.8 %copy-start.10 = (s32[8]{0:T(128)S(1)}, s32[8]{0:T(128)}, u32[]{:S(2)}) copy-start(s32[8]{0:T(128)} %constant.20.clone) | copy-start | bytes 100
  22.0 11.4 %collective-permute-start.5 = (bf16[4,32,1024]{2,1,0:T(8,128)(2,1)S(1)}, bf16[4,32,1024]{2,1,0:T(8,128)(2,1)S(1)}, u32[]{:S(2)}, u32[]{:S(2)}) collective-permute-start(bf16[4,32,1024]{2,1,0:T(8,128)(2,1)S(1)} %get-tuple-element.21), channel_id=1, source_target_pairs={{0,2},{1,3},{2,0},{3,1},{4,6},{5,7},{6,4},{7,5},{8,10},{9,11},{10,... | collective-permute-start | bytes 786440 | tf_op jit(solution)/shard_map/ppermute | solution.py:52
  23.3 10.7 %collective-permute-start.2 = (bf16[4,32,1024]{2,1,0:T(8,128)(2,1)S(1)}, bf16[4,32,1024]{2,1,0:T(8,128)(2,1)S(1)}, u32[]{:S(2)}, u32[]{:S(2)}) collective-permute-start(bf16[4,32,1024]{2,1,0:T(8,128)(2,1)S(1)} %get-tuple-element.23), channel_id=1, source_target_pairs={{0,16},{16,0},{1,17},{17,1},{2,18},{18,2},{3,19},{19,3},{4,20},{20... | collective-permute-start | bytes 786440 | tf_op jit(solution)/shard_map/ppermute | solution.py:56
  25.5 31.7 %all-to-all-start = ((f32[16,1,128]{2,1,0:T(1,128)}), f32[16,1,128]{2,1,0:T(1,128)S(1)}, u32[]{:S(2)}, u32[]{:S(2)}) async-start(f32[16,1,128]{2,1,0:T(1,128)} %bitcast.10), calls=%async_computation | async-start | bytes 16384 | tf_op jit(solution)/shard_map/all_to_all | solution.py:109
  31.4 8.8 %collective-permute-start.17 = (bf16[2,64,1024]{2,1,0:T(8,128)(2,1)S(1)}, bf16[2,64,1024]{2,1,0:T(8,128)(2,1)S(1)}, u32[]{:S(2)}, u32[]{:S(2)}) collective-permute-start(bf16[2,64,1024]{2,1,0:T(8,128)(2,1)S(1)} %pad_maximum_fusion.15), channel_id=1, source_target_pairs={{0,4},{1,5},{2,6},{3,7},{4,0},{5,1},{6,2},{7,3},{8,12},{9,13},{10,... | collective-permute-start | bytes 786440 | tf_op jit(solution)/shard_map/ppermute | solution.py:52
  33.5 14.9 %collective-permute-start.6 = (bf16[8,32,1024]{2,1,0:T(8,128)(2,1)S(1)}, bf16[8,32,1024]{2,1,0:T(8,128)(2,1)S(1)}, u32[]{:S(2)}, u32[]{:S(2)}) collective-permute-start(bf16[8,32,1024]{2,1,0:T(8,128)(2,1)S(1)} %pad_maximum_fusion.8), channel_id=1, source_target_pairs={{0,16},{16,0},{1,17},{17,1},{2,18},{18,2},{3,19},{19,3},{4,20},{20... | collective-permute-start | bytes 1572872 | tf_op jit(solution)/shard_map/ppermute | solution.py:56
  34.1 14.9 %collective-permute-start.3 = (bf16[2,4,32,1024]{3,2,1,0:T(8,128)(2,1)S(1)}, bf16[2,4,32,1024]{3,2,1,0:T(8,128)(2,1)S(1)}, u32[]{:S(2)}, u32[]{:S(2)}) collective-permute-start(bf16[2,4,32,1024]{3,2,1,0:T(8,128)(2,1)S(1)} %pad_maximum_fusion.7), channel_id=1, source_target_pairs={{0,2},{1,3},{2,0},{3,1},{4,6},{5,7},{6,4},{7,5},{8,10},{9,11},{10,... | collective-permute-start | bytes 1572872 | tf_op jit(solution)/shard_map/ppermute | solution.py:52
  40.4 12.9 %collective-permute-start.21 = (bf16[4,32,1024]{2,1,0:T(8,128)(2,1)S(1)}, bf16[4,32,1024]{2,1,0:T(8,128)(2,1)S(1)}, u32[]{:S(2)}, u32[]{:S(2)}) collective-permute-start(bf16[4,32,1024]{2,1,0:T(8,128)(2,1)S(1)} %get-tuple-element.24), channel_id=1, source_target_pairs={{0,2},{1,3},{2,0},{3,1},{4,6},{5,7},{6,4},{7,5},{8,10},{9,11},{10,... | collective-permute-start | bytes 786440 | tf_op jit(solution)/shard_map/ppermute | solution.py:52
  42.1 12.8 %collective-permute-start.18 = (bf16[4,32,1024]{2,1,0:T(8,128)(2,1)S(1)}, bf16[4,32,1024]{2,1,0:T(8,128)(2,1)S(1)}, u32[]{:S(2)}, u32[]{:S(2)}) collective-permute-start(bf16[4,32,1024]{2,1,0:T(8,128)(2,1)S(1)} %get-tuple-element.26), channel_id=1, source_target_pairs={{0,16},{16,0},{1,17},{17,1},{2,18},{18,2},{3,19},{19,3},{4,20},{20... | collective-permute-start | bytes 786440 | tf_op jit(solution)/shard_map/ppermute | solution.py:56
  48.4 7.3 %copy-start.4 = (bf16[2,256,1024]{2,1,0:T(8,128)(2,1)}, bf16[2,256,1024]{2,1,0:T(8,128)(2,1)S(1)}, u32[]{:S(2)}) copy-start(bf16[2,256,1024]{2,1,0:T(8,128)(2,1)S(1)} %pad_maximum_fusion.1.refs_3_) | copy-start | bytes 3145732
  48.4 21.4 %collective-permute-start.7 = (bf16[2,256,1024]{2,1,0:T(8,128)(2,1)S(1)}, bf16[2,256,1024]{2,1,0:T(8,128)(2,1)}, u32[]{:S(2)}, u32[]{:S(2)}) collective-permute-start(bf16[2,256,1024]{2,1,0:T(8,128)(2,1)S(1)} %pad_maximum_fusion.1.refs_3_), channel_id=1, source_target_pairs={{0,1},{1,0},{2,3},{3,2},{4,5},{5,4},{6,7},{7,6},{8,9},{9,8},{10,11... | collective-permute-start | bytes 3145736 | tf_op jit(solution)/shard_map/ppermute | solution.py:52
  49.1 20.7 %collective-permute-start.4 = (bf16[2,256,1024]{2,1,0:T(8,128)(2,1)S(1)}, bf16[2,256,1024]{2,1,0:T(8,128)(2,1)}, u32[]{:S(2)}, u32[]{:S(2)}) collective-permute-start(bf16[2,256,1024]{2,1,0:T(8,128)(2,1)S(1)} %bitcast.91), channel_id=1, source_target_pairs={{0,1},{1,0},{2,3},{3,2},{4,5},{5,4},{6,7},{7,6},{8,9},{9,8},{10,11... | collective-permute-start | bytes 3145736 | tf_op jit(solution)/shard_map/ppermute | solution.py:52
  53.3 12.7 %collective-permute-start.22 = (bf16[8,32,1024]{2,1,0:T(8,128)(2,1)S(1)}, bf16[8,32,1024]{2,1,0:T(8,128)(2,1)}, u32[]{:S(2)}, u32[]{:S(2)}) collective-permute-start(bf16[8,32,1024]{2,1,0:T(8,128)(2,1)S(1)} %pad_maximum_fusion.12), channel_id=1, source_target_pairs={{0,16},{16,0},{1,17},{17,1},{2,18},{18,2},{3,19},{19,3},{4,20},{20... | collective-permute-start | bytes 1572872 | tf_op jit(solution)/shard_map/ppermute | solution.py:56
  54.8 2.4 %copy-start.5 = (bf16[4,32,1024]{2,1,0:T(8,128)(2,1)}, bf16[4,32,1024]{2,1,0:T(8,128)(2,1)S(1)}, u32[]{:S(2)}) copy-start(bf16[4,32,1024]{2,1,0:T(8,128)(2,1)S(1)} %collective-permute-done.18) | copy-start | bytes 786436
  55.7 12.6 %collective-permute-start.19 = (bf16[2,4,32,1024]{3,2,1,0:T(8,128)(2,1)}, bf16[2,4,32,1024]{3,2,1,0:T(8,128)(2,1)}, u32[]{:S(2)}, u32[]{:S(2)}) collective-permute-start(bf16[2,4,32,1024]{3,2,1,0:T(8,128)(2,1)} %pad_maximum_fusion.11), channel_id=1, source_target_pairs={{0,2},{1,3},{2,0},{3,1},{4,6},{5,7},{6,4},{7,5},{8,10},{9,11},{10,... | collective-permute-start | bytes 1572872 | tf_op jit(solution)/shard_map/ppermute | solution.py:52
  60.1 8.2 %copy-start.6 = (bf16[4,32,1024]{2,1,0:T(8,128)(2,1)S(1)}, bf16[4,32,1024]{2,1,0:T(8,128)(2,1)}, u32[]{:S(2)}) copy-start(bf16[4,32,1024]{2,1,0:T(8,128)(2,1)} %copy-done.5) | copy-start | bytes 786436
  68.1 24.4 %collective-permute-start.23 = (bf16[2,256,1024]{2,1,0:T(8,128)(2,1)}, bf16[2,256,1024]{2,1,0:T(8,128)(2,1)}, u32[]{:S(2)}, u32[]{:S(2)}) collective-permute-start(bf16[2,256,1024]{2,1,0:T(8,128)(2,1)} %pad_maximum_fusion.3.refs_3_), channel_id=1, source_target_pairs={{0,1},{1,0},{2,3},{3,2},{4,5},{5,4},{6,7},{7,6},{8,9},{9,8},{10,11... | collective-permute-start | bytes 3145736 | tf_op jit(solution)/shard_map/ppermute | solution.py:52
  69.4 23.1 %collective-permute-start.20 = (bf16[2,256,1024]{2,1,0:T(8,128)(2,1)S(1)}, bf16[2,256,1024]{2,1,0:T(8,128)(2,1)}, u32[]{:S(2)}, u32[]{:S(2)}) collective-permute-start(bf16[2,256,1024]{2,1,0:T(8,128)(2,1)S(1)} %bitcast.93), channel_id=1, source_target_pairs={{0,1},{1,0},{2,3},{3,2},{4,5},{5,4},{6,7},{7,6},{8,9},{9,8},{10,11... | collective-permute-start | bytes 3145736 | tf_op jit(solution)/shard_map/ppermute | solution.py:52
  85.5 1.0 copy-start
  86.5 1.0 copy-start.2
  87.5 20.7 %collective-permute-start.11 = (bf16[2,2,4,32,1024]{4,3,2,1,0:T(8,128)(2,1)}, bf16[2,2,4,32,1024]{4,3,2,1,0:T(8,128)(2,1)S(1)}, u32[]{:S(2)}, u32[]{:S(2)}) collective-permute-start(bf16[2,2,4,32,1024]{4,3,2,1,0:T(8,128)(2,1)} %bitcast.22), channel_id=1, source_target_pairs={{0,1},{1,0},{2,3},{3,2},{4,5},{5,4},{6,7},{7,6},{8,9},{9,8},{10,11... | collective-permute-start | bytes 3145736 | tf_op jit(solution)/shard_map/ppermute | solution.py:52
  92.1 18.5 %collective-permute-start.8 = (bf16[2,2,4,32,1024]{4,3,2,0,1:T(8,128)(2,1)S(1)}, bf16[2,2,4,32,1024]{4,3,2,0,1:T(8,128)(2,1)S(1)}, u32[]{:S(2)}, u32[]{:S(2)}) collective-permute-start(bf16[2,2,4,32,1024]{4,3,2,0,1:T(8,128)(2,1)S(1)} %copy.50), channel_id=1, source_target_pairs={{0,1},{1,0},{2,3},{3,2},{4,5},{5,4},{6,7},{7,6},{8,9},{9,8},{10,11... | collective-permute-start | bytes 3145736 | tf_op jit(solution)/shard_map/ppermute | solution.py:52
  107.4 1.2 copy-start.3
  107.5 5.2 %collective-permute-start.27 = (bf16[2,2,4,32,1024]{4,3,2,1,0:T(8,128)(2,1)S(1)}, bf16[2,2,4,32,1024]{4,3,2,1,0:T(8,128)(2,1)S(1)}, u32[]{:S(2)}, u32[]{:S(2)}) collective-permute-start(bf16[2,2,4,32,1024]{4,3,2,1,0:T(8,128)(2,1)S(1)} %bitcast.101), channel_id=1, source_target_pairs={{0,1},{1,0},{2,3},{3,2},{4,5},{5,4},{6,7},{7,6},{8,9},{9,8},{10,11... | collective-permute-start | bytes 3145736 | tf_op jit(solution)/shard_map/ppermute | solution.py:52
  107.8 6.1 %collective-permute-start.24 = (bf16[2,2,4,32,1024]{4,3,2,0,1:T(8,128)(2,1)S(1)}, bf16[2,2,4,32,1024]{4,3,2,0,1:T(8,128)(2,1)S(1)}, u32[]{:S(2)}, u32[]{:S(2)}) collective-permute-start(bf16[2,2,4,32,1024]{4,3,2,0,1:T(8,128)(2,1)S(1)} %copy.56), channel_id=1, source_target_pairs={{0,1},{1,0},{2,3},{3,2},{4,5},{5,4},{6,7},{7,6},{8,9},{9,8},{10,11... | collective-permute-start | bytes 3145736 | tf_op jit(solution)/shard_map/ppermute | solution.py:52
  108.7 2.0 %copy-start.1 = (bf16[2,256,1024]{2,1,0:T(8,128)(2,1)S(1)}, bf16[2,256,1024]{2,1,0:T(8,128)(2,1)}, u32[]{:S(2)}) copy-start(bf16[2,256,1024]{2,1,0:T(8,128)(2,1)} %copy-done) | copy-start | bytes 3145732
  109.1 14.8 %collective-permute-start.12 = (bf16[2,4,32,1024]{3,2,1,0:T(8,128)(2,1)S(1)}, bf16[2,4,32,1024]{3,2,1,0:T(8,128)(2,1)S(1)}, u32[]{:S(2)}, u32[]{:S(2)}) collective-permute-start(bf16[2,4,32,1024]{3,2,1,0:T(8,128)(2,1)S(1)} %fusion.9), channel_id=1, source_target_pairs={{0,16},{16,0},{1,17},{17,1},{2,18},{18,2},{3,19},{19,3},{4,20},{20... | collective-permute-start | bytes 1572872 | tf_op jit(solution)/shard_map/ppermute | solution.py:56
  111.1 14.9 %collective-permute-start.9 = (bf16[2,4,32,1024]{3,2,1,0:T(8,128)(2,1)S(1)}, bf16[2,4,32,1024]{3,2,1,0:T(8,128)(2,1)S(1)}, u32[]{:S(2)}, u32[]{:S(2)}) collective-permute-start(bf16[2,4,32,1024]{3,2,1,0:T(8,128)(2,1)S(1)} %fusion.8), channel_id=1, source_target_pairs={{0,2},{1,3},{2,0},{3,1},{4,6},{5,7},{6,4},{7,5},{8,10},{9,11},{10,... | collective-permute-start | bytes 1572872 | tf_op jit(solution)/shard_map/ppermute | solution.py:52
  113.1 22.1 %collective-permute-start.28 = (bf16[2,4,32,1024]{3,2,1,0:T(8,128)(2,1)S(1)}, bf16[2,4,32,1024]{3,2,1,0:T(8,128)(2,1)S(1)}, u32[]{:S(2)}, u32[]{:S(2)}) collective-permute-start(bf16[2,4,32,1024]{3,2,1,0:T(8,128)(2,1)S(1)} %fusion.11), channel_id=1, source_target_pairs={{0,16},{16,0},{1,17},{17,1},{2,18},{18,2},{3,19},{19,3},{4,20},{20... | collective-permute-start | bytes 1572872 | tf_op jit(solution)/shard_map/ppermute | solution.py:56
  114.3 22.9 %collective-permute-start.25 = (bf16[2,4,32,1024]{3,2,1,0:T(8,128)(2,1)S(1)}, bf16[2,4,32,1024]{3,2,1,0:T(8,128)(2,1)S(1)}, u32[]{:S(2)}, u32[]{:S(2)}) collective-permute-start(bf16[2,4,32,1024]{3,2,1,0:T(8,128)(2,1)S(1)} %fusion.10), channel_id=1, source_target_pairs={{0,2},{1,3},{2,0},{3,1},{4,6},{5,7},{6,4},{7,5},{8,10},{9,11},{10,... | collective-permute-start | bytes 1572872 | tf_op jit(solution)/shard_map/ppermute | solution.py:52
  124.2 18.7 %collective-permute-start.13 = (bf16[4,32,1024]{2,1,0:T(8,128)(2,1)S(1)}, bf16[4,32,1024]{2,1,0:T(8,128)(2,1)S(1)}, u32[]{:S(2)}, u32[]{:S(2)}) collective-permute-start(bf16[4,32,1024]{2,1,0:T(8,128)(2,1)S(1)} %fusion.19), channel_id=1, source_target_pairs={{0,2},{1,3},{2,0},{3,1},{4,6},{5,7},{6,4},{7,5},{8,10},{9,11},{10,... | collective-permute-start | bytes 786440 | tf_op jit(solution)/shard_map/ppermute | solution.py:52
  126.2 16.7 %collective-permute-start.10 = (bf16[4,32,1024]{2,1,0:T(8,128)(2,1)S(1)}, bf16[4,32,1024]{2,1,0:T(8,128)(2,1)S(1)}, u32[]{:S(2)}, u32[]{:S(2)}) collective-permute-start(bf16[4,32,1024]{2,1,0:T(8,128)(2,1)S(1)} %fusion.18), channel_id=1, source_target_pairs={{0,16},{16,0},{1,17},{17,1},{2,18},{18,2},{3,19},{19,3},{4,20},{20... | collective-permute-start | bytes 786440 | tf_op jit(solution)/shard_map/ppermute | solution.py:56
  135.4 11.8 %collective-permute-start.29 = (bf16[4,32,1024]{2,1,0:T(8,128)(2,1)S(1)}, bf16[4,32,1024]{2,1,0:T(8,128)(2,1)S(1)}, u32[]{:S(2)}, u32[]{:S(2)}) collective-permute-start(bf16[4,32,1024]{2,1,0:T(8,128)(2,1)S(1)} %fusion.21), channel_id=1, source_target_pairs={{0,2},{1,3},{2,0},{3,1},{4,6},{5,7},{6,4},{7,5},{8,10},{9,11},{10,... | collective-permute-start | bytes 786440 | tf_op jit(solution)/shard_map/ppermute | solution.py:52
  137.5 9.8 %collective-permute-start.26 = (bf16[4,32,1024]{2,1,0:T(8,128)(2,1)S(1)}, bf16[4,32,1024]{2,1,0:T(8,128)(2,1)S(1)}, u32[]{:S(2)}, u32[]{:S(2)}) collective-permute-start(bf16[4,32,1024]{2,1,0:T(8,128)(2,1)S(1)} %fusion.20), channel_id=1, source_target_pairs={{0,16},{16,0},{1,17},{17,1},{2,18},{18,2},{3,19},{19,3},{4,20},{20... | collective-permute-start | bytes 786440 | tf_op jit(solution)/shard_map/ppermute | solution.py:56
  143.0 6.9 %collective-permute-start.14 = (bf16[2,64,1024]{2,1,0:T(8,128)(2,1)S(1)}, bf16[2,64,1024]{2,1,0:T(8,128)(2,1)S(1)}, u32[]{:S(2)}, u32[]{:S(2)}) collective-permute-start(bf16[2,64,1024]{2,1,0:T(8,128)(2,1)S(1)} %fusion.15), channel_id=1, source_target_pairs={{0,4},{1,5},{2,6},{3,7},{4,0},{5,1},{6,2},{7,3},{8,12},{9,13},{10,... | collective-permute-start | bytes 786440 | tf_op jit(solution)/shard_map/ppermute | solution.py:52
  147.4 10.5 %collective-permute-start.30 = (bf16[2,64,1024]{2,1,0:T(8,128)(2,1)S(1)}, bf16[2,64,1024]{2,1,0:T(8,128)(2,1)S(1)}, u32[]{:S(2)}, u32[]{:S(2)}) collective-permute-start(bf16[2,64,1024]{2,1,0:T(8,128)(2,1)S(1)} %fusion.12), channel_id=1, source_target_pairs={{0,4},{1,5},{2,6},{3,7},{4,0},{5,1},{6,2},{7,3},{8,12},{9,13},{10,... | collective-permute-start | bytes 786440 | tf_op jit(solution)/shard_map/ppermute | solution.py:52
  150.0 9.0 %collective-permute-start.15 = (bf16[1,64,1024]{2,1,0:T(8,128)(2,1)S(1)}, bf16[1,64,1024]{2,1,0:T(8,128)(2,1)S(1)}, u32[]{:S(2)}, u32[]{:S(2)}) collective-permute-start(bf16[1,64,1024]{2,1,0:T(8,128)(2,1)S(1)} %slice.281), channel_id=1, source_target_pairs={{0,8},{1,9},{2,10},{3,11},{4,12},{5,13},{6,14},{7,15},{8,0},{9,1},... | collective-permute-start | bytes 393224 | tf_op jit(solution)/shard_map/ppermute | solution.py:52
  158.0 7.3 %collective-permute-start.31 = (bf16[1,64,1024]{2,1,0:T(8,128)(2,1)S(1)}, bf16[1,64,1024]{2,1,0:T(8,128)(2,1)S(1)}, u32[]{:S(2)}, u32[]{:S(2)}) collective-permute-start(bf16[1,64,1024]{2,1,0:T(8,128)(2,1)S(1)} %slice.280), channel_id=1, source_target_pairs={{0,8},{1,9},{2,10},{3,11},{4,12},{5,13},{6,14},{7,15},{8,0},{9,1},... | collective-permute-start | bytes 393224 | tf_op jit(solution)/shard_map/ppermute | solution.py:52

commit v2 on v0

--- a/solution.py
+++ b/solution.py
@@ -1,10 +1,14 @@
 import jax
 import jax.numpy as jnp
 from jax import lax
+from jax.experimental import pallas as pl
+from jax.experimental.pallas import tpu as pltpu
 from jax.sharding import PartitionSpec as P
 
-
-def local(tokens, expert_ids, chosen_probs, gate_weight, up_weight, down_weight):
+VMEM_MB = 40
+
+
+def exchange(tokens, expert_ids, chosen_probs, gate_weight, up_weight, down_weight):
     n_experts = lax.axis_size("expert")
     tok_rows = expert_ids.shape[0]
     top_count = expert_ids.shape[1]
@@ -43,7 +47,193 @@
     return lax.psum_scatter(partial_out, "dp", scatter_dimension=1, tiled=True).astype(jnp.bfloat16)
 
 
+def swap(value, mask):
+    n = lax.axis_size("expert")
+    return lax.ppermute(value, "expert", [(i, i ^ mask) for i in range(n)])
+
+
+def swap_dp(value):
+    return lax.ppermute(value, "dp", [(0, 1), (1, 0)])
+
+
+def after(value, *events):
+    return lax.optimization_barrier((value, *events))[0]
+
+
+def ffn_kernel(half, z_first, half_ref, *refs):
+    pieces = (refs[0:4], refs[4:8])
+    w_ref, gate_hbm, up_hbm, down_hbm, own_sent, own_kept = refs[8:14]
+    other_sent, other_kept = refs[14:16], refs[16]
+    x_scr, gate_ref, up_ref, down_ref, sems = refs[17:]
+    rows, part = pieces[0][0].shape[2:]
+    lines = pieces[0][0].shape[1]
+    ff = gate_ref.shape[0]
+    copies = []
+    for k, (src, dst) in enumerate(((gate_hbm, gate_ref), (up_hbm, up_ref), (down_hbm, down_ref))):
+        for h in range(2):
+            at = pl.ds(h * (ff // 2), ff // 2)
+            copies.append(pltpu.make_async_copy(src.at[0, at], dst.at[at], sems.at[2 * k + h]))
+    for copy in copies:
+        copy.start()
+    mine = half_ref[0]
+    here = [pl.ds(pl.multiple_of((mine if s == 0 else 1 - mine) * part, part), part) for s in range(2)]
+    nt = (((1,), (1,)), ((), ()))
+    size = lines * rows
+
+    def place(core, y):
+        return (core * 2 + y) * size
+
+    for p in range(2):
+        for core in range(2):
+            for y in range(2):
+                for x in range(2):
+                    first, second = (y, x) if p == 0 else (x, y)
+                    piece = pieces[p][core * 2 + first][second]
+                    x_scr[p, x, pl.ds(place(core, y), size), :] = piece.reshape(size, part)
+
+    def project(p, ref):
+        return sum(
+            lax.dot_general(x_scr[p, s], ref[:, here[s]], nt, preferred_element_type=jnp.float32)
+            for s in range(2)
+        )
+
+    for p in range(2):
+        if p == 0:
+            copies[0].wait()
+            copies[1].wait()
+        gate = project(p, gate_ref)
+        if p == 0:
+            copies[2].wait()
+            copies[3].wait()
+        hidden = (gate / (1.0 + jnp.exp(-gate)) * project(p, up_ref)).astype(jnp.bfloat16)
+        if p == 0:
+            copies[4].wait()
+            copies[5].wait()
+        for x in range(2):
+            out = jnp.dot(hidden, down_ref[:, here[x]], preferred_element_type=jnp.float32)
+            for core in range(2):
+                for y in range(2):
+                    first, second = (y, x) if p == 0 else (x, y)
+                    for z in range(lines):
+                        at = place(core, y) + z * rows
+                        value = out[at:at + rows] * w_ref[core, y, z, 2 * half + p]
+                        at = (z, second) if z_first else (second, z)
+                        if core and first:
+                            other_sent[p][at] = value.astype(jnp.bfloat16)
+                        else:
+                            ref = other_kept if core else (own_kept, own_sent)[first]
+                            ref[(p,) + at] = value.astype(jnp.bfloat16)
+
+
+def ffn(half, z_first, pieces, weights, gate, up, down, mine):
+    rows, part = pieces[0].shape[2:]
+    lines = pieces[0].shape[1]
+    one = (lines, 2, rows, part) if z_first else (2, lines, rows, part)
+    shapes = [(2,) + one, (2,) + one, one, one, (2,) + one]
+    n_rows = 4 * lines * rows
+    vmem = pl.BlockSpec(memory_space=pltpu.VMEM)
+    hbm = pl.BlockSpec(memory_space=pltpu.HBM)
+    return pl.pallas_call(
+        lambda *refs: ffn_kernel(half, z_first, *refs),
+        out_shape=[jax.ShapeDtypeStruct(s, jnp.bfloat16) for s in shapes],
+        in_specs=[pl.BlockSpec(memory_space=pltpu.SMEM)] + [vmem] * 9 + [hbm] * 3,
+        out_specs=[vmem] * 5,
+        scratch_shapes=[
+            pltpu.VMEM((2, 2, n_rows, part), jnp.bfloat16),
+            pltpu.VMEM(gate.shape[1:], jnp.bfloat16),
+            pltpu.VMEM(gate.shape[1:], jnp.bfloat16),
+            pltpu.VMEM(gate.shape[1:], jnp.bfloat16),
+            pltpu.SemaphoreType.DMA((6,)),
+        ],
+        compiler_params=pltpu.CompilerParams(vmem_limit_bytes=VMEM_MB * 2**20),
+        cost_estimate=pl.CostEstimate(flops=10000000000, bytes_accessed=20000000, transcendentals=0),
+        name="ffn",
+    )(mine, *pieces, weights, gate, up, down)
+
+
+def gather_all(tokens, expert_ids, chosen_probs, gate_weight, up_weight, down_weight):
+    n_experts = lax.axis_size("expert")
+    tok_rows, part = tokens.shape
+    me = lax.axis_index("expert")
+    mine = lax.axis_index("dp").reshape(1).astype(jnp.int32)
+    line = [1 << k for k in range(n_experts.bit_length() - 2, 1, -1)]
+    lines = n_experts // 4
+    rows = tok_rows // 4
+    along = {"x": swap_dp, "y": lambda v: swap(v, 2)}
+
+    def add(keep, got):
+        return keep.astype(jnp.float32) + got.astype(jnp.float32)
+
+    def send(v):
+        return v.astype(jnp.bfloat16)
+
+    def line_scatter(t):
+        for m in reversed(line):
+            n = t.shape[0] // 2
+            t = add(t[:n], swap(send(t[n:]), m))
+        return t[0]
+
+    route = chosen_probs / jnp.sum(chosen_probs, axis=1, keepdims=True)
+    chosen = expert_ids.T[None] == jnp.arange(n_experts, dtype=jnp.int32)[:, None, None]
+    dense = jnp.sum(jnp.where(chosen, route.T[None], 0.0), axis=1)
+    dense = lax.all_to_all(dense, "expert", split_axis=0, concat_axis=0, tiled=True)
+    masks = [0]
+    for m in line + [2, 1]:
+        masks = masks + [k ^ m for k in masks]
+    order = me ^ jnp.array(masks, jnp.int32)
+    weights = dense[order].reshape(2, 2, lines, 4, rows, 1)
+
+    def spread(v, *events):
+        gots = []
+        for m in line:
+            gots.append(swap(after(v, *events), m))
+            v = jnp.concatenate([v, gots[-1]], axis=0)
+        a, b = v[None, :, :rows], v[None, :, rows:]
+        gots += [along["x"](a), along["y"](b)]
+        a = jnp.concatenate([a, gots[-2]], axis=0)
+        b = jnp.concatenate([b, gots[-1]], axis=0)
+        return (a, along["y"](a)), (b, along["x"](b)), gots
+
+    a, b, gots = spread(tokens[None, :2 * rows])
+    c, d, late = spread(tokens[None, 2 * rows:], gots[0])
+    a, b = (a[0], after(a[1], weights, *late[-2:])), (b[0], after(b[1], weights, *late[-2:]))
+
+    def run(z_first, a, b, k):
+        pieces = []
+        for last in (a, b):
+            pieces += [*last, *[swap(p, 1) for p in last]]
+        return ffn(k, z_first, pieces, weights, gate_weight, up_weight, down_weight, mine)
+
+    def meet(own_sent, other_sent):
+        sent = [send(add(own_sent[k], swap(other_sent[k], 1))) for k in range(2)]
+        return along["y"](sent[0]), along["x"](sent[1])
+
+    def total(gots, own, other):
+        other = swap(other, 1)
+        return [add(add(own[k], other[k]), gots[k]) for k in range(2)]
+
+    ab = run(True, a, b, 0)
+    ab_gots = meet(ab[0], ab[2:4])
+    c, d = [tuple(after(p, ab[0]) for p in v) for v in (c, d)]
+    cd = run(False, c, d, 1)
+    cd_other = [after(v, *ab_gots) for v in cd[2:4]]
+    cd_gots = meet(cd[0], cd_other)
+    a, b = total(ab_gots, ab[1], ab[4])
+    t = line_scatter(jnp.concatenate([a, b], axis=1))
+    a, b = t[:2], t[2:]
+    a = add(a[0], along["x"](send(a[1])))
+    b = add(b[0], along["y"](send(b[1])))
+    c, d = total(cd_gots, cd[1], cd[4])
+    c = add(c[0], along["x"](send(c[1])))
+    d = add(d[0], along["y"](send(d[1])))
+    t = line_scatter(jnp.concatenate([c, d], axis=1))
+    return jnp.concatenate([a, b, t], axis=0).astype(jnp.bfloat16)
+
+
 def solution(mesh):
+    n_dp, n_experts = mesh.shape["dp"], mesh.shape["expert"]
+    powers = n_experts & (n_experts - 1) == 0
+    few = n_dp == 2 and powers and 4 <= n_experts <= 32
     in_specs = (
         P("expert", "dp"),
         P("expert", None),
@@ -52,5 +242,10 @@
         P("expert", "dp", None),
         P("expert", "dp", None),
     )
-    out_specs = P("expert", "dp")
-    return jax.shard_map(local, mesh=mesh, in_specs=in_specs, out_specs=out_specs, check_vma=False)
+    return jax.shard_map(
+        gather_all if few else exchange,
+        mesh=mesh,
+        in_specs=in_specs,
+        out_specs=P("expert", "dp"),
+        check_vma=False,
+    )

time: 411 us -> 140 us (0.34)
  blocking collectives: 155 us -> 0 us
  waiting for transfers between devices: 157 us -> 57.6 us
  starting transfers between devices: 5.93 us -> 44.4 us
  local copies, waits for them, and re-layouts: 41.1 us -> 4.4 us
  Pallas kernels: 0 us -> 25.6 us
  matrix products: 23.6 us -> 0 us
  between operations: 13.5 us -> 0.33 us
  other arithmetic: 14.6 us -> 6.97 us
    all_to_all x1 -> x0, blocking collectives: 143 us -> none  [local(): lax.all_to_all(outgoing, 'expert', split_axis=0, concat_axis=0, tiled=True)]
    all_to_all x1, waiting for transfers between devices: 114 us -> 0.98 us  [gather_all(): lax.all_to_all(dense, 'expert', split_axis=0, concat_axis=0, tiled=True)]
    ppermute x0 -> x38, waiting for transfers between devices: none -> 56.6 us  [the longest x30 41.9 us: swap(): return lax.ppermute(value, 'expert', [(i, i ^ mask) for i in range(n)])]
    reduce_scatter x1 -> x0, waiting for transfers between devices: 42.9 us -> none  [local(): lax.psum_scatter(partial_out, 'dp', scatter_dimension=1, tiled=True)]
    ppermute x0 -> x38, starting transfers between devices: none -> 40.9 us  [the longest x30 32.4 us: swap(): return lax.ppermute(value, 'expert', [(i, i ^ mask) for i in range(n)])]
    pallas_call x0 -> x2, Pallas kernels: none -> 25.6 us  [ffn(): pl.pallas_call(lambda *refs: ffn_kernel(half, z_first, *refs), out_shape=...]
    scatter x1 -> x0, local copies, waits for them, and re-layouts: 24.3 us -> none  [local(): buffer = jnp.zeros((n_experts * capacity, columns_now), jnp.bfloat16).at[...]
    dot_general x2 -> x0, matrix products: 23.6 us -> none  [the longest x1 16.9 us: local(): jnp.einsum('snf,fd->snd', hidden, down_local, preferred_element_type=jnp....]
  transfers between devices with their start and end apart: 2 -> 39, of which waited for: 2 -> 22; matrix products, arithmetic and copies ran while one was open for 0% -> 5% of each run, Pallas kernels for 0% -> 18%
where the time goes in v2:
time: 140 us; the launch traced here: 139 us
  waiting for transfers between devices  57.6 us (41%)
  starting transfers between devices  44.4 us (32%)
  Pallas kernels  25.6 us (18%)
  other arithmetic  6.97 us (5%)
  local copies, waits for them, and re-layouts  4.4 us (3%)
    ppermute x30, waiting for transfers between devices, swap(): return lax.ppermute(value, 'expert', [(i, i ^ mask) for i in range(n)])  41.9 us
    ppermute x30, starting transfers between devices, swap(): return lax.ppermute(value, 'expert', [(i, i ^ mask) for i in range(n)])  32.4 us
    pallas_call x2, Pallas kernels, ffn(): pl.pallas_call(lambda *refs: ffn_kernel(half, z_first, *refs), out_shape=...  25.6 us
    ppermute x8, waiting for transfers between devices, swap_dp(): return lax.ppermute(value, 'dp', [(0, 1), (1, 0)])  14.7 us
    ppermute x8, starting transfers between devices, swap_dp(): return lax.ppermute(value, 'dp', [(0, 1), (1, 0)])  8.48 us
    all_to_all x1, starting transfers between devices, gather_all(): lax.all_to_all(dense, 'expert', split_axis=0, concat_axis=0, tiled=True)  3.47 us
  transfers between devices with their start and end apart: 39, of which 22 were waited for; matrix products, arithmetic and copies ran while one was open for 5% of the time, Pallas kernels for 18%

profile of v2, /device:TPU:0, one launch (start us, length us, event | category | flops | bytes accessed | tf_op | source)
XLA Modules:
  0.0 139.3 jit_solution(3712582364553253894)
XLA Ops:
  0.0 1.0 slice_bitcast_fusion.9
  1.0 4.1 %collective-permute-start = (bf16[1,64,1024]{2,1,0:T(8,128)(2,1)S(1)}, bf16[1,64,1024]{2,1,0:T(8,128)(2,1)S(1)}, u32[]{:S(2)}, u32[]{:S(2)}) collective-permute-start(bf16[1,64,1024]{2,1,0:T(8,128)(2,1)S(1)} %get-tuple-element.63), channel_id=1, source_target_pairs={{0,8},{1,9},{2,10},{3,11},{4,12},{5,13},{6,14},{7,15},{8,0},{9,1},... | collective-permute-start | bytes 393224 | tf_op jit(solution)/shard_map/ppermute | solution.py:52
  5.1 6.3 %collective-permute-done = bf16[1,64,1024]{2,1,0:T(8,128)(2,1)S(1)} collective-permute-done((bf16[1,64,1024]{2,1,0:T(8,128)(2,1)S(1)}, bf16[1,64,1024]{2,1,0:T(8,128)(2,1)S(1)}, u32[]{:S(2)}, u32[]{:S(2)}) %collective-permute-start) | collective-permute-done | bytes 131104 | tf_op jit(solution)/shard_map/ppermute | solution.py:52
  11.5 0.8 collective-permute-start.1
  12.2 3.4 %collective-permute-start.4 = (bf16[1,64,1024]{2,1,0:T(8,128)(2,1)S(1)}, bf16[1,64,1024]{2,1,0:T(8,128)(2,1)S(1)}, u32[]{:S(2)}, u32[]{:S(2)}) collective-permute-start(bf16[1,64,1024]{2,1,0:T(8,128)(2,1)S(1)} %get-tuple-element.25), channel_id=1, source_target_pairs={{0,8},{1,9},{2,10},{3,11},{4,12},{5,13},{6,14},{7,15},{8,0},{9,1},... | collective-permute-start | bytes 393224 | tf_op jit(solution)/shard_map/ppermute | solution.py:52
  15.6 0.7 reduce_sum.18
  16.3 4.5 %collective-permute-done.4 = bf16[1,64,1024]{2,1,0:T(8,128)(2,1)S(1)} collective-permute-done((bf16[1,64,1024]{2,1,0:T(8,128)(2,1)S(1)}, bf16[1,64,1024]{2,1,0:T(8,128)(2,1)S(1)}, u32[]{:S(2)}, u32[]{:S(2)}) %collective-permute-start.4) | collective-permute-done | bytes 131104 | tf_op jit(solution)/shard_map/ppermute | solution.py:52
  20.8 4.2 %collective-permute-start.5 = (bf16[2,64,1024]{2,1,0:T(8,128)(2,1)S(1)}, bf16[2,64,1024]{2,1,0:T(8,128)(2,1)S(1)}, u32[]{:S(2)}, u32[]{:S(2)}) collective-permute-start(bf16[2,64,1024]{2,1,0:T(8,128)(2,1)S(1)} %pad_maximum_fusion.9), channel_id=1, source_target_pairs={{0,4},{1,5},{2,6},{3,7},{4,0},{5,1},{6,2},{7,3},{8,12},{9,13},{10,... | collective-permute-start | bytes 786440 | tf_op jit(solution)/shard_map/ppermute | solution.py:52
  25.1 1.6 %collective-permute-start.10 = (bf16[1,4,32,1024]{3,2,1,0:T(8,128)(2,1)S(1)}, bf16[1,4,32,1024]{3,2,1,0:T(8,128)(2,1)S(1)}, u32[]{:S(2)}, u32[]{:S(2)}) collective-permute-start(bf16[1,4,32,1024]{3,2,1,0:T(8,128)(2,1)S(1)} %get-tuple-element.57), channel_id=1, source_target_pairs={{0,2},{1,3},{2,0},{3,1},{4,6},{5,7},{6,4},{7,5},{8,10},{9,11},{10,... | collective-permute-start | bytes 786440 | tf_op jit(solution)/shard_map/ppermute | solution.py:52
  26.7 1.5 %collective-permute-start.2 = (bf16[1,4,32,1024]{3,2,1,0:T(8,128)(2,1)S(1)}, bf16[1,4,32,1024]{3,2,1,0:T(8,128)(2,1)S(1)}, u32[]{:S(2)}, u32[]{:S(2)}) collective-permute-start(bf16[1,4,32,1024]{3,2,1,0:T(8,128)(2,1)S(1)} %get-tuple-element.58), channel_id=1, source_target_pairs={{0,16},{16,0},{1,17},{17,1},{2,18},{18,2},{3,19},{19,3},{4,20},{20... | collective-permute-start | bytes 786440 | tf_op jit(solution)/shard_map/ppermute | solution.py:56
  28.2 0.6 select_reduce_fusion
  28.9 3.5 %all-to-all-start = ((f32[16,1,128]{2,1,0:T(1,128)}), f32[16,1,128]{2,1,0:T(1,128)S(1)}, u32[]{:S(2)}, u32[]{:S(2)}) async-start(f32[16,1,128]{2,1,0:T(1,128)} %bitcast.6), calls=%async_computation | async-start | bytes 16384 | tf_op jit(solution)/shard_map/all_to_all | solution.py:179
  32.7 1.6 %collective-permute-start.11 = (bf16[2,4,32,1024]{3,2,1,0:T(8,128)(2,1)S(1)}, bf16[2,4,32,1024]{3,2,1,0:T(8,128)(2,1)S(1)}, u32[]{:S(2)}, u32[]{:S(2)}) collective-permute-start(bf16[2,4,32,1024]{3,2,1,0:T(8,128)(2,1)S(1)} %pad_maximum_fusion.5.refs_5_), channel_id=1, source_target_pairs={{0,16},{16,0},{1,17},{17,1},{2,18},{18,2},{3,19},{19,3},{4,20},{20... | collective-permute-start | bytes 1572872 | tf_op jit(solution)/shard_map/ppermute | solution.py:56
  34.3 1.6 %collective-permute-start.3 = (bf16[2,4,32,1024]{3,2,1,0:T(8,128)(2,1)S(1)}, bf16[2,4,32,1024]{3,2,1,0:T(8,128)(2,1)S(1)}, u32[]{:S(2)}, u32[]{:S(2)}) collective-permute-start(bf16[2,4,32,1024]{3,2,1,0:T(8,128)(2,1)S(1)} %pad_maximum_fusion.3.refs_1_), channel_id=1, source_target_pairs={{0,2},{1,3},{2,0},{3,1},{4,6},{5,7},{6,4},{7,5},{8,10},{9,11},{10,... | collective-permute-start | bytes 1572872 | tf_op jit(solution)/shard_map/ppermute | solution.py:52
  36.0 0.6 collective-permute-start.6
  36.6 1.0 collective-permute-start.7
  37.6 1.0 all-to-all-done
  39.4 12.9 %collective-permute-done.6 = bf16[1,4,32,1024]{3,2,1,0:T(8,128)(2,1)S(1)} collective-permute-done((bf16[1,4,32,1024]{3,2,1,0:T(8,128)(2,1)S(1)}, bf16[1,4,32,1024]{3,2,1,0:T(8,128)(2,1)S(1)}, u32[]{:S(2)}, u32[]{:S(2)}) %collective-permute-start.6) | collective-permute-done | bytes 262176 | tf_op jit(solution)/shard_map/ppermute | solution.py:56
  53.9 1.1 pad_maximum_fusion.7.refs_5_
  55.0 1.5 %collective-permute-start.26 = (bf16[2,4,32,1024]{3,2,1,0:T(8,128)(2,1)S(1)}, bf16[2,4,32,1024]{3,2,1,0:T(8,128)(2,1)S(1)}, u32[]{:S(2)}, u32[]{:S(2)}) collective-permute-start(bf16[2,4,32,1024]{3,2,1,0:T(8,128)(2,1)S(1)} %pad_maximum_fusion.7.refs_5_), channel_id=1, source_target_pairs={{0,16},{16,0},{1,17},{17,1},{2,18},{18,2},{3,19},{19,3},{4,20},{20... | collective-permute-start | bytes 1572872 | tf_op jit(solution)/shard_map/ppermute | solution.py:56
  56.5 1.0 pad_maximum_fusion.6.refs_1_
  57.5 1.7 %collective-permute-start.23 = (bf16[2,4,32,1024]{3,2,1,0:T(8,128)(2,1)S(1)}, bf16[2,4,32,1024]{3,2,1,0:T(8,128)(2,1)S(1)}, u32[]{:S(2)}, u32[]{:S(2)}) collective-permute-start(bf16[2,4,32,1024]{3,2,1,0:T(8,128)(2,1)S(1)} %pad_maximum_fusion.6.refs_1_), channel_id=1, source_target_pairs={{0,2},{1,3},{2,0},{3,1},{4,6},{5,7},{6,4},{7,5},{8,10},{9,11},{10,... | collective-permute-start | bytes 1572872 | tf_op jit(solution)/shard_map/ppermute | solution.py:52
  59.2 1.9 %copy-done = bf16[1,768,2048]{2,1,0:T(8,128)(2,1)S(1)} copy-done((bf16[1,768,2048]{2,1,0:T(8,128)(2,1)S(1)}, bf16[1,768,2048]{2,1,0:T(8,128)(2,1)}, u32[]{:S(2)}) %copy-start) | copy-done | bytes 3145752
  61.1 13.5 %ffn.2 = (bf16[2,4,2,32,1024]{4,3,2,1,0:T(8,128)(2,1)S(1)}, bf16[2,4,2,32,1024]{4,3,2,1,0:T(8,128)(2,1)S(1)}, bf16[4,2,32,1024]{3,2,1,0:T(8,128)(2,1)S(1)}, bf16...) custom-call(s32[1]{0:T(128)} %bitcast.refs_0_, bf16[2,4,32,1024]{3,2,1,0:T(8,128)(2,1)S(1)} %pad_maximum_fusion.3.refs_1_, ...), custom_call_target="tpu_custom_call" | custom-call | flops 10000000000 | bytes 20000000 | tf_op jit(solution)/shard_map/ffn/pallas_call | solution.py:136
  75.8 0.8 collective-permute-done.15
  76.7 0.6 collective-permute-done.17
  79.6 0.7 collective-permute-done.24.refs_3_
  80.3 12.1 %ffn.3 = (bf16[2,2,4,32,1024]{4,3,2,1,0:T(8,128)(2,1)S(1)}, bf16[2,2,4,32,1024]{4,3,2,1,0:T(8,128)(2,1)S(1)}, bf16[2,4,32,1024]{3,2,1,0:T(8,128)(2,1)S(1)}, bf16...) custom-call(s32[1]{0:T(128)} %bitcast.refs_0_, bf16[2,4,32,1024]{3,2,1,0:T(8,128)(2,1)S(1)} %pad_maximum_fusion.6.refs_1_, ...), custom_call_target="tpu_custom_call" | custom-call | flops 10000000000 | bytes 20000000 | tf_op jit(solution)/shard_map/ffn/pallas_call | solution.py:136
  93.3 1.4 %collective-permute-done.30 = bf16[2,4,32,1024]{3,2,1,0:T(8,128)(2,1)S(1)} collective-permute-done((bf16[2,4,32,1024]{3,2,1,0:T(8,128)(2,1)S(1)}, bf16[2,4,32,1024]{3,2,1,0:T(8,128)(2,1)S(1)}, u32[]{:S(2)}, u32[]{:S(2)}) %collective-permute-start.30) | collective-permute-done | bytes 524320 | tf_op jit(solution)/shard_map/ppermute | solution.py:52
  94.7 0.7 collective-permute-done.33
  95.9 1.2 collective-permute-start.31
  97.6 0.6 bitcast_add_fusion.2
  98.3 1.5 %collective-permute-start.19 = (bf16[2,4,32,1024]{3,2,1,0:T(8,128)(2,1)S(1)}, bf16[2,4,32,1024]{3,2,1,0:T(8,128)(2,1)S(1)}, u32[]{:S(2)}, u32[]{:S(2)}) collective-permute-start(bf16[2,4,32,1024]{3,2,1,0:T(8,128)(2,1)S(1)} %fusion.2), channel_id=1, source_target_pairs={{0,4},{1,5},{2,6},{3,7},{4,0},{5,1},{6,2},{7,3},{8,12},{9,13},{10,... | collective-permute-start | bytes 1572872 | tf_op jit(solution)/shard_map/ppermute | solution.py:52
  99.8 10.1 %collective-permute-done.31 = bf16[2,4,32,1024]{3,2,1,0:T(8,128)(2,1)S(1)} collective-permute-done((bf16[2,4,32,1024]{3,2,1,0:T(8,128)(2,1)S(1)}, bf16[2,4,32,1024]{3,2,1,0:T(8,128)(2,1)S(1)}, u32[]{:S(2)}, u32[]{:S(2)}) %collective-permute-start.31) | collective-permute-done | bytes 524320 | tf_op jit(solution)/shard_map/ppermute | solution.py:52
  109.9 0.8 collective-permute-done.34
  111.4 1.0 collective-permute-start.35
  112.4 0.6 collective-permute-start.32
  113.2 2.4 %collective-permute-start.20 = (bf16[1,4,32,1024]{3,2,1,0:T(8,128)(2,1)S(1)}, bf16[1,4,32,1024]{3,2,1,0:T(8,128)(2,1)S(1)}, u32[]{:S(2)}, u32[]{:S(2)}) collective-permute-start(bf16[1,4,32,1024]{3,2,1,0:T(8,128)(2,1)S(1)} %slice.248), channel_id=1, source_target_pairs={{0,8},{1,9},{2,10},{3,11},{4,12},{5,13},{6,14},{7,15},{8,0},{9,1},... | collective-permute-start | bytes 786440 | tf_op jit(solution)/shard_map/ppermute | solution.py:52
  115.7 3.0 %collective-permute-done.35 = bf16[4,32,1024]{2,1,0:T(8,128)(2,1)S(1)} collective-permute-done((bf16[4,32,1024]{2,1,0:T(8,128)(2,1)S(1)}, bf16[4,32,1024]{2,1,0:T(8,128)(2,1)S(1)}, u32[]{:S(2)}, u32[]{:S(2)}) %collective-permute-start.35) | collective-permute-done | bytes 262176 | tf_op jit(solution)/shard_map/ppermute | solution.py:52
  118.7 0.7 collective-permute-done.32
  119.5 1.5 %collective-permute-start.36 = (bf16[2,64,1024]{2,1,0:T(8,128)(2,1)S(1)}, bf16[2,64,1024]{2,1,0:T(8,128)(2,1)S(1)}, u32[]{:S(2)}, u32[]{:S(2)}) collective-permute-start(bf16[2,64,1024]{2,1,0:T(8,128)(2,1)S(1)} %fusion.9), channel_id=1, source_target_pairs={{0,4},{1,5},{2,6},{3,7},{4,0},{5,1},{6,2},{7,3},{8,12},{9,13},{10,... | collective-permute-start | bytes 786440 | tf_op jit(solution)/shard_map/ppermute | solution.py:52
  121.0 5.6 %collective-permute-done.20 = bf16[1,4,32,1024]{3,2,1,0:T(8,128)(2,1)S(1)} collective-permute-done((bf16[1,4,32,1024]{3,2,1,0:T(8,128)(2,1)S(1)}, bf16[1,4,32,1024]{3,2,1,0:T(8,128)(2,1)S(1)}, u32[]{:S(2)}, u32[]{:S(2)}) %collective-permute-start.20) | collective-permute-done | bytes 262176 | tf_op jit(solution)/shard_map/ppermute | solution.py:52
  126.7 1.5 %collective-permute-start.21 = (bf16[32,1024]{1,0:T(8,128)(2,1)S(1)}, bf16[32,1024]{1,0:T(8,128)(2,1)S(1)}, u32[]{:S(2)}, u32[]{:S(2)}) collective-permute-start(bf16[32,1024]{1,0:T(8,128)(2,1)S(1)} %get-tuple-element.61), channel_id=1, source_target_pairs={{0,16},{16,0},{1,17},{17,1},{2,18},{18,2},{3,19},{19,3},{4,20},{20... | collective-permute-start | bytes 196616 | tf_op jit(solution)/shard_map/ppermute | solution.py:56
  128.2 1.1 collective-permute-start.22
  129.3 0.8 collective-permute-done.36
  130.2 2.4 %collective-permute-start.37 = (bf16[1,64,1024]{2,1,0:T(8,128)(2,1)S(1)}, bf16[1,64,1024]{2,1,0:T(8,128)(2,1)S(1)}, u32[]{:S(2)}, u32[]{:S(2)}) collective-permute-start(bf16[1,64,1024]{2,1,0:T(8,128)(2,1)S(1)} %slice.249), channel_id=1, source_target_pairs={{0,8},{1,9},{2,10},{3,11},{4,12},{5,13},{6,14},{7,15},{8,0},{9,1},... | collective-permute-start | bytes 393224 | tf_op jit(solution)/shard_map/ppermute | solution.py:52
  132.6 5.9 %collective-permute-done.37 = bf16[1,64,1024]{2,1,0:T(8,128)(2,1)S(1)} collective-permute-done((bf16[1,64,1024]{2,1,0:T(8,128)(2,1)S(1)}, bf16[1,64,1024]{2,1,0:T(8,128)(2,1)S(1)}, u32[]{:S(2)}, u32[]{:S(2)}) %collective-permute-start.37) | collective-permute-done | bytes 131104 | tf_op jit(solution)/shard_map/ppermute | solution.py:52
  138.6 0.7 pad_maximum_fusion.10
  (86 shorter events, 9.5 us)
Async XLA Ops:
  0.0 26.7 %copy-start.5 = (f32[128,8]{0,1:T(8,128)S(1)}, f32[128,8]{0,1:T(8,128)}, u32[]{:S(2)}) copy-start(f32[128,8]{0,1:T(8,128)} %param.9) | copy-start | bytes 12292
  0.0 28.2 %copy-start.6 = (s32[128,8]{0,1:T(8,128)S(1)}, s32[128,8]{0,1:T(8,128)}, u32[]{:S(2)}) copy-start(s32[128,8]{0,1:T(8,128)} %param.8) | copy-start | bytes 12292
  1.0 10.4 %collective-permute-start = (bf16[1,64,1024]{2,1,0:T(8,128)(2,1)S(1)}, bf16[1,64,1024]{2,1,0:T(8,128)(2,1)S(1)}, u32[]{:S(2)}, u32[]{:S(2)}) collective-permute-start(bf16[1,64,1024]{2,1,0:T(8,128)(2,1)S(1)} %get-tuple-element.63), channel_id=1, source_target_pairs={{0,8},{1,9},{2,10},{3,11},{4,12},{5,13},{6,14},{7,15},{8,0},{9,1},... | collective-permute-start | bytes 393224 | tf_op jit(solution)/shard_map/ppermute | solution.py:52
  11.5 13.6 %collective-permute-start.1 = (bf16[2,64,1024]{2,1,0:T(8,128)(2,1)S(1)}, bf16[2,64,1024]{2,1,0:T(8,128)(2,1)S(1)}, u32[]{:S(2)}, u32[]{:S(2)}) collective-permute-start(bf16[2,64,1024]{2,1,0:T(8,128)(2,1)S(1)} %pad_maximum_fusion.8), channel_id=1, source_target_pairs={{0,4},{1,5},{2,6},{3,7},{4,0},{5,1},{6,2},{7,3},{8,12},{9,13},{10,... | collective-permute-start | bytes 786440 | tf_op jit(solution)/shard_map/ppermute | solution.py:52
  12.2 8.6 %collective-permute-start.4 = (bf16[1,64,1024]{2,1,0:T(8,128)(2,1)S(1)}, bf16[1,64,1024]{2,1,0:T(8,128)(2,1)S(1)}, u32[]{:S(2)}, u32[]{:S(2)}) collective-permute-start(bf16[1,64,1024]{2,1,0:T(8,128)(2,1)S(1)} %get-tuple-element.25), channel_id=1, source_target_pairs={{0,8},{1,9},{2,10},{3,11},{4,12},{5,13},{6,14},{7,15},{8,0},{9,1},... | collective-permute-start | bytes 393224 | tf_op jit(solution)/shard_map/ppermute | solution.py:52
  20.8 16.8 %copy-start.7 = (s32[16]{0:T(128)S(1)}, s32[16]{0:T(128)}, u32[]{:S(2)}) copy-start(s32[16]{0:T(128)} %constant.17.clone) | copy-start | bytes 196
  20.8 11.5 %collective-permute-start.5 = (bf16[2,64,1024]{2,1,0:T(8,128)(2,1)S(1)}, bf16[2,64,1024]{2,1,0:T(8,128)(2,1)S(1)}, u32[]{:S(2)}, u32[]{:S(2)}) collective-permute-start(bf16[2,64,1024]{2,1,0:T(8,128)(2,1)S(1)} %pad_maximum_fusion.9), channel_id=1, source_target_pairs={{0,4},{1,5},{2,6},{3,7},{4,0},{5,1},{6,2},{7,3},{8,12},{9,13},{10,... | collective-permute-start | bytes 786440 | tf_op jit(solution)/shard_map/ppermute | solution.py:52
  25.1 7.5 %collective-permute-start.10 = (bf16[1,4,32,1024]{3,2,1,0:T(8,128)(2,1)S(1)}, bf16[1,4,32,1024]{3,2,1,0:T(8,128)(2,1)S(1)}, u32[]{:S(2)}, u32[]{:S(2)}) collective-permute-start(bf16[1,4,32,1024]{3,2,1,0:T(8,128)(2,1)S(1)} %get-tuple-element.57), channel_id=1, source_target_pairs={{0,2},{1,3},{2,0},{3,1},{4,6},{5,7},{6,4},{7,5},{8,10},{9,11},{10,... | collective-permute-start | bytes 786440 | tf_op jit(solution)/shard_map/ppermute | solution.py:52
  26.7 7.5 %collective-permute-start.2 = (bf16[1,4,32,1024]{3,2,1,0:T(8,128)(2,1)S(1)}, bf16[1,4,32,1024]{3,2,1,0:T(8,128)(2,1)S(1)}, u32[]{:S(2)}, u32[]{:S(2)}) collective-permute-start(bf16[1,4,32,1024]{3,2,1,0:T(8,128)(2,1)S(1)} %get-tuple-element.58), channel_id=1, source_target_pairs={{0,16},{16,0},{1,17},{17,1},{2,18},{18,2},{3,19},{19,3},{4,20},{20... | collective-permute-start | bytes 786440 | tf_op jit(solution)/shard_map/ppermute | solution.py:56
  28.9 9.8 %all-to-all-start = ((f32[16,1,128]{2,1,0:T(1,128)}), f32[16,1,128]{2,1,0:T(1,128)S(1)}, u32[]{:S(2)}, u32[]{:S(2)}) async-start(f32[16,1,128]{2,1,0:T(1,128)} %bitcast.6), calls=%async_computation | async-start | bytes 16384 | tf_op jit(solution)/shard_map/all_to_all | solution.py:179
  32.7 20.1 %collective-permute-start.11 = (bf16[2,4,32,1024]{3,2,1,0:T(8,128)(2,1)S(1)}, bf16[2,4,32,1024]{3,2,1,0:T(8,128)(2,1)S(1)}, u32[]{:S(2)}, u32[]{:S(2)}) collective-permute-start(bf16[2,4,32,1024]{3,2,1,0:T(8,128)(2,1)S(1)} %pad_maximum_fusion.5.refs_5_), channel_id=1, source_target_pairs={{0,16},{16,0},{1,17},{17,1},{2,18},{18,2},{3,19},{19,3},{4,20},{20... | collective-permute-start | bytes 1572872 | tf_op jit(solution)/shard_map/ppermute | solution.py:56
  34.3 18.6 %collective-permute-start.3 = (bf16[2,4,32,1024]{3,2,1,0:T(8,128)(2,1)S(1)}, bf16[2,4,32,1024]{3,2,1,0:T(8,128)(2,1)S(1)}, u32[]{:S(2)}, u32[]{:S(2)}) collective-permute-start(bf16[2,4,32,1024]{3,2,1,0:T(8,128)(2,1)S(1)} %pad_maximum_fusion.3.refs_1_), channel_id=1, source_target_pairs={{0,2},{1,3},{2,0},{3,1},{4,6},{5,7},{6,4},{7,5},{8,10},{9,11},{10,... | collective-permute-start | bytes 1572872 | tf_op jit(solution)/shard_map/ppermute | solution.py:52
  36.0 17.3 %copy-start.2 = (bf16[1,4,32,1024]{3,2,1,0:T(8,128)(2,1)}, bf16[1,4,32,1024]{3,2,1,0:T(8,128)(2,1)S(1)}, u32[]{:S(2)}) copy-start(bf16[1,4,32,1024]{3,2,1,0:T(8,128)(2,1)S(1)} %get-tuple-element.59) | copy-start | bytes 786436
  36.0 16.3 %collective-permute-start.6 = (bf16[1,4,32,1024]{3,2,1,0:T(8,128)(2,1)S(1)}, bf16[1,4,32,1024]{3,2,1,0:T(8,128)(2,1)S(1)}, u32[]{:S(2)}, u32[]{:S(2)}) collective-permute-start(bf16[1,4,32,1024]{3,2,1,0:T(8,128)(2,1)S(1)} %get-tuple-element.60), channel_id=1, source_target_pairs={{0,16},{16,0},{1,17},{17,1},{2,18},{18,2},{3,19},{19,3},{4,20},{20... | collective-permute-start | bytes 786440 | tf_op jit(solution)/shard_map/ppermute | solution.py:56
  36.6 16.1 %collective-permute-start.7 = (bf16[1,4,32,1024]{3,2,1,0:T(8,128)(2,1)S(1)}, bf16[1,4,32,1024]{3,2,1,0:T(8,128)(2,1)S(1)}, u32[]{:S(2)}, u32[]{:S(2)}) collective-permute-start(bf16[1,4,32,1024]{3,2,1,0:T(8,128)(2,1)S(1)} %get-tuple-element.59), channel_id=1, source_target_pairs={{0,2},{1,3},{2,0},{3,1},{4,6},{5,7},{6,4},{7,5},{8,10},{9,11},{10,... | collective-permute-start | bytes 786440 | tf_op jit(solution)/shard_map/ppermute | solution.py:52
  39.3 18.2 %collective-permute-start.12 = (bf16[2,4,32,1024]{3,2,1,0:T(8,128)(2,1)S(1)}, bf16[2,4,32,1024]{3,2,1,0:T(8,128)(2,1)}, u32[]{:S(2)}, u32[]{:S(2)}) collective-permute-start(bf16[2,4,32,1024]{3,2,1,0:T(8,128)(2,1)S(1)} %pad_maximum_fusion.5.refs_5_), channel_id=1, source_target_pairs={{0,1},{1,0},{2,3},{3,2},{4,5},{5,4},{6,7},{7,6},{8,9},{9,8},{10,11... | collective-permute-start | bytes 1572872 | tf_op jit(solution)/shard_map/ppermute | solution.py:52
  52.3 1.0 copy-start.3
  52.3 6.9 %collective-permute-start.8 = (bf16[2,4,32,1024]{3,2,1,0:T(8,128)(2,1)S(1)}, bf16[2,4,32,1024]{3,2,1,0:T(8,128)(2,1)}, u32[]{:S(2)}, u32[]{:S(2)}) collective-permute-start(bf16[2,4,32,1024]{3,2,1,0:T(8,128)(2,1)S(1)} %pad_maximum_fusion.3.refs_1_), channel_id=1, source_target_pairs={{0,1},{1,0},{2,3},{3,2},{4,5},{5,4},{6,7},{7,6},{8,9},{9,8},{10,11... | collective-permute-start | bytes 1572872 | tf_op jit(solution)/shard_map/ppermute | solution.py:52
  52.7 0.7 copy-start.4
  52.7 6.5 %collective-permute-start.13 = (bf16[2,4,32,1024]{3,2,1,0:T(8,128)(2,1)S(1)}, bf16[2,4,32,1024]{3,2,1,0:T(8,128)(2,1)}, u32[]{:S(2)}, u32[]{:S(2)}) collective-permute-start(bf16[2,4,32,1024]{3,2,1,0:T(8,128)(2,1)S(1)} %collective-permute-done.11.refs_6_), channel_id=1, source_target_pairs={{0,1},{1,0},{2,3},{3,2},{4,5},{5,4},{6,7},{7,6},{8,9},{9,8},{10,11... | collective-permute-start | bytes 1572872 | tf_op jit(solution)/shard_map/ppermute | solution.py:52
  52.9 6.4 %collective-permute-start.9 = (bf16[2,4,32,1024]{3,2,1,0:T(8,128)(2,1)S(1)}, bf16[2,4,32,1024]{3,2,1,0:T(8,128)(2,1)}, u32[]{:S(2)}, u32[]{:S(2)}) collective-permute-start(bf16[2,4,32,1024]{3,2,1,0:T(8,128)(2,1)S(1)} %collective-permute-done.3.refs_2_), channel_id=1, source_target_pairs={{0,1},{1,0},{2,3},{3,2},{4,5},{5,4},{6,7},{7,6},{8,9},{9,8},{10,11... | collective-permute-start | bytes 1572872 | tf_op jit(solution)/shard_map/ppermute | solution.py:52
  55.0 20.2 %collective-permute-start.26 = (bf16[2,4,32,1024]{3,2,1,0:T(8,128)(2,1)S(1)}, bf16[2,4,32,1024]{3,2,1,0:T(8,128)(2,1)S(1)}, u32[]{:S(2)}, u32[]{:S(2)}) collective-permute-start(bf16[2,4,32,1024]{3,2,1,0:T(8,128)(2,1)S(1)} %pad_maximum_fusion.7.refs_5_), channel_id=1, source_target_pairs={{0,16},{16,0},{1,17},{17,1},{2,18},{18,2},{3,19},{19,3},{4,20},{20... | collective-permute-start | bytes 1572872 | tf_op jit(solution)/shard_map/ppermute | solution.py:56
  57.5 18.2 %collective-permute-start.23 = (bf16[2,4,32,1024]{3,2,1,0:T(8,128)(2,1)S(1)}, bf16[2,4,32,1024]{3,2,1,0:T(8,128)(2,1)S(1)}, u32[]{:S(2)}, u32[]{:S(2)}) collective-permute-start(bf16[2,4,32,1024]{3,2,1,0:T(8,128)(2,1)S(1)} %pad_maximum_fusion.6.refs_1_), channel_id=1, source_target_pairs={{0,2},{1,3},{2,0},{3,1},{4,6},{5,7},{6,4},{7,5},{8,10},{9,11},{10,... | collective-permute-start | bytes 1572872 | tf_op jit(solution)/shard_map/ppermute | solution.py:52
  59.2 1.9 %copy-start = (bf16[1,768,2048]{2,1,0:T(8,128)(2,1)S(1)}, bf16[1,768,2048]{2,1,0:T(8,128)(2,1)}, u32[]{:S(2)}) copy-start(bf16[1,768,2048]{2,1,0:T(8,128)(2,1)} %refs_10_.3) | copy-start | bytes 9437188
  74.6 5.7 %copy-start.1 = (bf16[1,768,2048]{2,1,0:T(8,128)(2,1)S(1)}, bf16[1,768,2048]{2,1,0:T(8,128)(2,1)}, u32[]{:S(2)}) copy-start(bf16[1,768,2048]{2,1,0:T(8,128)(2,1)} %refs_10_.3) | copy-start | bytes 9437188
  74.6 2.0 %collective-permute-start.15 = (bf16[4,2,32,1024]{3,2,1,0:T(8,128)(2,1)S(1)}, bf16[4,2,32,1024]{3,2,1,0:T(8,128)(2,1)S(1)}, u32[]{:S(2)}, u32[]{:S(2)}) collective-permute-start(bf16[4,2,32,1024]{3,2,1,0:T(8,128)(2,1)S(1)} %get-tuple-element.32), channel_id=1, source_target_pairs={{0,1},{1,0},{2,3},{3,2},{4,5},{5,4},{6,7},{7,6},{8,9},{9,8},{10,11... | collective-permute-start | bytes 1572872 | tf_op jit(solution)/shard_map/ppermute | solution.py:52
  74.7 2.6 %collective-permute-start.17 = (bf16[4,2,32,1024]{3,2,1,0:T(8,128)(2,1)S(1)}, bf16[4,2,32,1024]{3,2,1,0:T(8,128)(2,1)S(1)}, u32[]{:S(2)}, u32[]{:S(2)}) collective-permute-start(bf16[4,2,32,1024]{3,2,1,0:T(8,128)(2,1)S(1)} %get-tuple-element.33), channel_id=1, source_target_pairs={{0,1},{1,0},{2,3},{3,2},{4,5},{5,4},{6,7},{7,6},{8,9},{9,8},{10,11... | collective-permute-start | bytes 1572872 | tf_op jit(solution)/shard_map/ppermute | solution.py:52
  75.2 2.9 %collective-permute-start.28 = (bf16[2,4,32,1024]{3,2,1,0:T(8,128)(2,1)S(1)}, bf16[2,4,32,1024]{3,2,1,0:T(8,128)(2,1)S(1)}, u32[]{:S(2)}, u32[]{:S(2)}) collective-permute-start(bf16[2,4,32,1024]{3,2,1,0:T(8,128)(2,1)S(1)} %collective-permute-done.26.refs_6_), channel_id=1, source_target_pairs={{0,1},{1,0},{2,3},{3,2},{4,5},{5,4},{6,7},{7,6},{8,9},{9,8},{10,11... | collective-permute-start | bytes 1572872 | tf_op jit(solution)/shard_map/ppermute | solution.py:52
  75.3 3.6 %collective-permute-start.27 = (bf16[2,4,32,1024]{3,2,1,0:T(8,128)(2,1)S(1)}, bf16[2,4,32,1024]{3,2,1,0:T(8,128)(2,1)S(1)}, u32[]{:S(2)}, u32[]{:S(2)}) collective-permute-start(bf16[2,4,32,1024]{3,2,1,0:T(8,128)(2,1)S(1)} %pad_maximum_fusion.7.refs_5_), channel_id=1, source_target_pairs={{0,1},{1,0},{2,3},{3,2},{4,5},{5,4},{6,7},{7,6},{8,9},{9,8},{10,11... | collective-permute-start | bytes 1572872 | tf_op jit(solution)/shard_map/ppermute | solution.py:52
  75.7 3.9 %collective-permute-start.25 = (bf16[2,4,32,1024]{3,2,1,0:T(8,128)(2,1)S(1)}, bf16[2,4,32,1024]{3,2,1,0:T(8,128)(2,1)S(1)}, u32[]{:S(2)}, u32[]{:S(2)}) collective-permute-start(bf16[2,4,32,1024]{3,2,1,0:T(8,128)(2,1)S(1)} %collective-permute-done.23.refs_2_), channel_id=1, source_target_pairs={{0,1},{1,0},{2,3},{3,2},{4,5},{5,4},{6,7},{7,6},{8,9},{9,8},{10,11... | collective-permute-start | bytes 1572872 | tf_op jit(solution)/shard_map/ppermute | solution.py:52
  76.6 3.7 %collective-permute-start.24 = (bf16[2,4,32,1024]{3,2,1,0:T(8,128)(2,1)S(1)}, bf16[2,4,32,1024]{3,2,1,0:T(8,128)(2,1)S(1)}, u32[]{:S(2)}, u32[]{:S(2)}) collective-permute-start(bf16[2,4,32,1024]{3,2,1,0:T(8,128)(2,1)S(1)} %pad_maximum_fusion.6.refs_1_), channel_id=1, source_target_pairs={{0,1},{1,0},{2,3},{3,2},{4,5},{5,4},{6,7},{7,6},{8,9},{9,8},{10,11... | collective-permute-start | bytes 1572872 | tf_op jit(solution)/shard_map/ppermute | solution.py:52
  77.3 20.3 %collective-permute-start.14 = (bf16[2,4,2,32,1024]{4,3,2,1,0:T(8,128)(2,1)S(1)}, bf16[2,4,2,32,1024]{4,3,2,1,0:T(8,128)(2,1)S(1)}, u32[]{:S(2)}, u32[]{:S(2)}) collective-permute-start(bf16[2,4,2,32,1024]{4,3,2,1,0:T(8,128)(2,1)S(1)} %get-tuple-element.30), channel_id=1, source_target_pairs={{0,1},{1,0},{2,3},{3,2},{4,5},{5,4},{6,7},{7,6},{8,9},{9,8},{10,11... | collective-permute-start | bytes 3145736 | tf_op jit(solution)/shard_map/ppermute | solution.py:52
  78.1 14.4 %collective-permute-start.16 = (bf16[4,2,32,1024]{3,2,1,0:T(8,128)(2,1)S(1)}, bf16[4,2,32,1024]{3,2,1,0:T(8,128)(2,1)S(1)}, u32[]{:S(2)}, u32[]{:S(2)}) collective-permute-start(bf16[4,2,32,1024]{3,2,1,0:T(8,128)(2,1)S(1)} %get-tuple-element.54), channel_id=1, source_target_pairs={{0,2},{1,3},{2,0},{3,1},{4,6},{5,7},{6,4},{7,5},{8,10},{9,11},{10,... | collective-permute-start | bytes 1572872 | tf_op jit(solution)/shard_map/ppermute | solution.py:52
  78.8 14.0 %collective-permute-start.18 = (bf16[4,2,32,1024]{3,2,1,0:T(8,128)(2,1)S(1)}, bf16[4,2,32,1024]{3,2,1,0:T(8,128)(2,1)S(1)}, u32[]{:S(2)}, u32[]{:S(2)}) collective-permute-start(bf16[4,2,32,1024]{3,2,1,0:T(8,128)(2,1)S(1)} %get-tuple-element.53), channel_id=1, source_target_pairs={{0,16},{16,0},{1,17},{17,1},{2,18},{18,2},{3,19},{19,3},{4,20},{20... | collective-permute-start | bytes 1572872 | tf_op jit(solution)/shard_map/ppermute | solution.py:56
  92.8 1.9 %collective-permute-start.30 = (bf16[2,4,32,1024]{3,2,1,0:T(8,128)(2,1)S(1)}, bf16[2,4,32,1024]{3,2,1,0:T(8,128)(2,1)S(1)}, u32[]{:S(2)}, u32[]{:S(2)}) collective-permute-start(bf16[2,4,32,1024]{3,2,1,0:T(8,128)(2,1)S(1)} %get-tuple-element.42), channel_id=1, source_target_pairs={{0,1},{1,0},{2,3},{3,2},{4,5},{5,4},{6,7},{7,6},{8,9},{9,8},{10,11... | collective-permute-start | bytes 1572872 | tf_op jit(solution)/shard_map/ppermute | solution.py:52
  92.8 2.7 %collective-permute-start.33 = (bf16[2,4,32,1024]{3,2,1,0:T(8,128)(2,1)S(1)}, bf16[2,4,32,1024]{3,2,1,0:T(8,128)(2,1)S(1)}, u32[]{:S(2)}, u32[]{:S(2)}) collective-permute-start(bf16[2,4,32,1024]{3,2,1,0:T(8,128)(2,1)S(1)} %get-tuple-element.44), channel_id=1, source_target_pairs={{0,1},{1,0},{2,3},{3,2},{4,5},{5,4},{6,7},{7,6},{8,9},{9,8},{10,11... | collective-permute-start | bytes 1572872 | tf_op jit(solution)/shard_map/ppermute | solution.py:52
  93.3 6.5 %collective-permute-start.29 = (bf16[2,2,4,32,1024]{4,3,2,1,0:T(8,128)(2,1)S(1)}, bf16[2,2,4,32,1024]{4,3,2,1,0:T(8,128)(2,1)S(1)}, u32[]{:S(2)}, u32[]{:S(2)}) collective-permute-start(bf16[2,2,4,32,1024]{4,3,2,1,0:T(8,128)(2,1)S(1)} %get-tuple-element.39), channel_id=1, source_target_pairs={{0,1},{1,0},{2,3},{3,2},{4,5},{5,4},{6,7},{7,6},{8,9},{9,8},{10,11... | collective-permute-start | bytes 3145736 | tf_op jit(solution)/shard_map/ppermute | solution.py:52
  95.9 14.0 %collective-permute-start.31 = (bf16[2,4,32,1024]{3,2,1,0:T(8,128)(2,1)S(1)}, bf16[2,4,32,1024]{3,2,1,0:T(8,128)(2,1)S(1)}, u32[]{:S(2)}, u32[]{:S(2)}) collective-permute-start(bf16[2,4,32,1024]{3,2,1,0:T(8,128)(2,1)S(1)} %get-tuple-element.52), channel_id=1, source_target_pairs={{0,2},{1,3},{2,0},{3,1},{4,6},{5,7},{6,4},{7,5},{8,10},{9,11},{10,... | collective-permute-start | bytes 1572872 | tf_op jit(solution)/shard_map/ppermute | solution.py:52
  97.1 13.7 %collective-permute-start.34 = (bf16[2,4,32,1024]{3,2,1,0:T(8,128)(2,1)S(1)}, bf16[2,4,32,1024]{3,2,1,0:T(8,128)(2,1)S(1)}, u32[]{:S(2)}, u32[]{:S(2)}) collective-permute-start(bf16[2,4,32,1024]{3,2,1,0:T(8,128)(2,1)S(1)} %get-tuple-element.51), channel_id=1, source_target_pairs={{0,16},{16,0},{1,17},{17,1},{2,18},{18,2},{3,19},{19,3},{4,20},{20... | collective-permute-start | bytes 1572872 | tf_op jit(solution)/shard_map/ppermute | solution.py:56
  98.3 14.7 %collective-permute-start.19 = (bf16[2,4,32,1024]{3,2,1,0:T(8,128)(2,1)S(1)}, bf16[2,4,32,1024]{3,2,1,0:T(8,128)(2,1)S(1)}, u32[]{:S(2)}, u32[]{:S(2)}) collective-permute-start(bf16[2,4,32,1024]{3,2,1,0:T(8,128)(2,1)S(1)} %fusion.2), channel_id=1, source_target_pairs={{0,4},{1,5},{2,6},{3,7},{4,0},{5,1},{6,2},{7,3},{8,12},{9,13},{10,... | collective-permute-start | bytes 1572872 | tf_op jit(solution)/shard_map/ppermute | solution.py:52
  111.4 7.3 %collective-permute-start.35 = (bf16[4,32,1024]{2,1,0:T(8,128)(2,1)S(1)}, bf16[4,32,1024]{2,1,0:T(8,128)(2,1)S(1)}, u32[]{:S(2)}, u32[]{:S(2)}) collective-permute-start(bf16[4,32,1024]{2,1,0:T(8,128)(2,1)S(1)} %fusion.13), channel_id=1, source_target_pairs={{0,2},{1,3},{2,0},{3,1},{4,6},{5,7},{6,4},{7,5},{8,10},{9,11},{10,... | collective-permute-start | bytes 786440 | tf_op jit(solution)/shard_map/ppermute | solution.py:52
  112.4 7.0 %collective-permute-start.32 = (bf16[4,32,1024]{2,1,0:T(8,128)(2,1)S(1)}, bf16[4,32,1024]{2,1,0:T(8,128)(2,1)S(1)}, u32[]{:S(2)}, u32[]{:S(2)}) collective-permute-start(bf16[4,32,1024]{2,1,0:T(8,128)(2,1)S(1)} %fusion.12), channel_id=1, source_target_pairs={{0,16},{16,0},{1,17},{17,1},{2,18},{18,2},{3,19},{19,3},{4,20},{20... | collective-permute-start | bytes 786440 | tf_op jit(solution)/shard_map/ppermute | solution.py:56
  113.2 13.3 %collective-permute-start.20 = (bf16[1,4,32,1024]{3,2,1,0:T(8,128)(2,1)S(1)}, bf16[1,4,32,1024]{3,2,1,0:T(8,128)(2,1)S(1)}, u32[]{:S(2)}, u32[]{:S(2)}) collective-permute-start(bf16[1,4,32,1024]{3,2,1,0:T(8,128)(2,1)S(1)} %slice.248), channel_id=1, source_target_pairs={{0,8},{1,9},{2,10},{3,11},{4,12},{5,13},{6,14},{7,15},{8,0},{9,1},... | collective-permute-start | bytes 786440 | tf_op jit(solution)/shard_map/ppermute | solution.py:52
  119.5 10.7 %collective-permute-start.36 = (bf16[2,64,1024]{2,1,0:T(8,128)(2,1)S(1)}, bf16[2,64,1024]{2,1,0:T(8,128)(2,1)S(1)}, u32[]{:S(2)}, u32[]{:S(2)}) collective-permute-start(bf16[2,64,1024]{2,1,0:T(8,128)(2,1)S(1)} %fusion.9), channel_id=1, source_target_pairs={{0,4},{1,5},{2,6},{3,7},{4,0},{5,1},{6,2},{7,3},{8,12},{9,13},{10,... | collective-permute-start | bytes 786440 | tf_op jit(solution)/shard_map/ppermute | solution.py:52
  126.7 6.0 %collective-permute-start.21 = (bf16[32,1024]{1,0:T(8,128)(2,1)S(1)}, bf16[32,1024]{1,0:T(8,128)(2,1)S(1)}, u32[]{:S(2)}, u32[]{:S(2)}) collective-permute-start(bf16[32,1024]{1,0:T(8,128)(2,1)S(1)} %get-tuple-element.61), channel_id=1, source_target_pairs={{0,16},{16,0},{1,17},{17,1},{2,18},{18,2},{3,19},{19,3},{4,20},{20... | collective-permute-start | bytes 196616 | tf_op jit(solution)/shard_map/ppermute | solution.py:56
  128.2 4.4 %collective-permute-start.22 = (bf16[32,1024]{1,0:T(8,128)(2,1)S(1)}, bf16[32,1024]{1,0:T(8,128)(2,1)S(1)}, u32[]{:S(2)}, u32[]{:S(2)}) collective-permute-start(bf16[32,1024]{1,0:T(8,128)(2,1)S(1)} %get-tuple-element.62), channel_id=1, source_target_pairs={{0,2},{1,3},{2,0},{3,1},{4,6},{5,7},{6,4},{7,5},{8,10},{9,11},{10,... | collective-permute-start | bytes 196616 | tf_op jit(solution)/shard_map/ppermute | solution.py:52
  130.2 8.3 %collective-permute-start.37 = (bf16[1,64,1024]{2,1,0:T(8,128)(2,1)S(1)}, bf16[1,64,1024]{2,1,0:T(8,128)(2,1)S(1)}, u32[]{:S(2)}, u32[]{:S(2)}) collective-permute-start(bf16[1,64,1024]{2,1,0:T(8,128)(2,1)S(1)} %slice.249), channel_id=1, source_target_pairs={{0,8},{1,9},{2,10},{3,11},{4,12},{5,13},{6,14},{7,15},{8,0},{9,1},... | collective-permute-start | bytes 393224 | tf_op jit(solution)/shard_map/ppermute | solution.py:52

commit v3 on v2

--- a/solution.py
+++ b/solution.py
@@ -188,6 +188,8 @@
         for m in line:
             gots.append(swap(after(v, *events), m))
             v = jnp.concatenate([v, gots[-1]], axis=0)
+        if not events:
+            v = after(v, weights)
         a, b = v[None, :, :rows], v[None, :, rows:]
         gots += [along["x"](a), along["y"](b)]
         a = jnp.concatenate([a, gots[-2]], axis=0)
@@ -196,7 +198,7 @@
 
     a, b, gots = spread(tokens[None, :2 * rows])
     c, d, late = spread(tokens[None, 2 * rows:], gots[0])
-    a, b = (a[0], after(a[1], weights, *late[-2:])), (b[0], after(b[1], weights, *late[-2:]))
+    a, b = (a[0], after(a[1], *late[-2:])), (b[0], after(b[1], *late[-2:]))
 
     def run(z_first, a, b, k):
         pieces = []

time: 140 us -> 136 us (0.971)
  starting transfers between devices: 44.4 us -> 40.4 us
  other arithmetic: 6.97 us -> 9 us
  waiting for transfers between devices: 57.6 us -> 55.8 us
    ppermute x30, starting transfers between devices: 32.4 us -> 26.1 us  [swap(): return lax.ppermute(value, 'expert', [(i, i ^ mask) for i in range(n)])]
    all_to_all x1, waiting for transfers between devices: 0.98 us -> 3.7 us  [gather_all(): lax.all_to_all(dense, 'expert', split_axis=0, concat_axis=0, tiled=True)]
    ppermute x8, waiting for transfers between devices: 14.7 us -> 12.3 us  [swap_dp(): return lax.ppermute(value, 'dp', [(0, 1), (1, 0)])]
    ppermute x30, waiting for transfers between devices: 41.9 us -> 39.8 us  [swap(): return lax.ppermute(value, 'expert', [(i, i ^ mask) for i in range(n)])]
    ppermute x8, starting transfers between devices: 8.48 us -> 10.3 us  [swap_dp(): return lax.ppermute(value, 'dp', [(0, 1), (1, 0)])]
  transfers between devices with their start and end apart: 39 -> 39, of which waited for: 22 -> 21; matrix products, arithmetic and copies ran while one was open for 5% -> 7% of each run, Pallas kernels for 18% -> 19%
where the time goes in v3:
time: 136 us; the launch traced here: 135 us
  waiting for transfers between devices  55.8 us (41%)
  starting transfers between devices  40.4 us (30%)
  Pallas kernels  25.6 us (19%)
  other arithmetic  9 us (7%)
  local copies, waits for them, and re-layouts  4.35 us (3%)
    ppermute x30, waiting for transfers between devices, swap(): return lax.ppermute(value, 'expert', [(i, i ^ mask) for i in range(n)])  39.8 us
    ppermute x30, starting transfers between devices, swap(): return lax.ppermute(value, 'expert', [(i, i ^ mask) for i in range(n)])  26.1 us
    pallas_call x2, Pallas kernels, ffn(): pl.pallas_call(lambda *refs: ffn_kernel(half, z_first, *refs), out_shape=...  25.6 us
    ppermute x8, waiting for transfers between devices, swap_dp(): return lax.ppermute(value, 'dp', [(0, 1), (1, 0)])  12.3 us
    ppermute x8, starting transfers between devices, swap_dp(): return lax.ppermute(value, 'dp', [(0, 1), (1, 0)])  10.3 us
    all_to_all x1, starting transfers between devices, gather_all(): lax.all_to_all(dense, 'expert', split_axis=0, concat_axis=0, tiled=True)  3.91 us
    all_to_all x1, waiting for transfers between devices, gather_all(): lax.all_to_all(dense, 'expert', split_axis=0, concat_axis=0, tiled=True)  3.7 us
  transfers between devices with their start and end apart: 39, of which 21 were waited for; matrix products, arithmetic and copies ran while one was open for 7% of the time, Pallas kernels for 19%

profile of v3, /device:TPU:0, one launch (start us, length us, event | category | flops | bytes accessed | tf_op | source)
XLA Modules:
  0.0 135.5 jit_solution(6028471280543785919)
XLA Ops:
  0.0 1.0 slice_bitcast_fusion.9
  1.0 4.1 %collective-permute-start = (bf16[1,64,1024]{2,1,0:T(8,128)(2,1)S(1)}, bf16[1,64,1024]{2,1,0:T(8,128)(2,1)S(1)}, u32[]{:S(2)}, u32[]{:S(2)}) collective-permute-start(bf16[1,64,1024]{2,1,0:T(8,128)(2,1)S(1)} %get-tuple-element.65), channel_id=1, source_target_pairs={{0,8},{1,9},{2,10},{3,11},{4,12},{5,13},{6,14},{7,15},{8,0},{9,1},... | collective-permute-start | bytes 393224 | tf_op jit(solution)/shard_map/ppermute | solution.py:52
  5.1 0.7 reduce_sum.18
  5.8 0.7 divide_bitcast_fusion
  6.5 1.3 select_reduce_fusion
  7.8 3.9 %all-to-all-start = ((f32[16,1,128]{2,1,0:T(1,128)}), f32[16,1,128]{2,1,0:T(1,128)S(1)}, u32[]{:S(2)}, u32[]{:S(2)}) async-start(f32[16,1,128]{2,1,0:T(1,128)} %bitcast.5), calls=%async_computation | async-start | bytes 16384 | tf_op jit(solution)/shard_map/all_to_all | solution.py:179
  11.8 2.0 %collective-permute-start.1 = (bf16[2,64,1024]{2,1,0:T(8,128)(2,1)S(1)}, bf16[2,64,1024]{2,1,0:T(8,128)(2,1)S(1)}, u32[]{:S(2)}, u32[]{:S(2)}) collective-permute-start(bf16[2,64,1024]{2,1,0:T(8,128)(2,1)S(1)} %pad_maximum_fusion.8), channel_id=1, source_target_pairs={{0,4},{1,5},{2,6},{3,7},{4,0},{5,1},{6,2},{7,3},{8,12},{9,13},{10,... | collective-permute-start | bytes 786440 | tf_op jit(solution)/shard_map/ppermute | solution.py:52
  13.7 0.7 compare_select_fusion
  14.4 3.7 %all-to-all-done = f32[16,1,128]{2,1,0:T(1,128)S(1)} async-done(((f32[16,1,128]{2,1,0:T(1,128)}), f32[16,1,128]{2,1,0:T(1,128)S(1)}, u32[]{:S(2)}, u32[]{:S(2)}) %all-to-all-start) | async-done | bytes 8224 | tf_op jit(solution)/shard_map/all_to_all | solution.py:179
  18.8 1.8 %collective-permute-done.1 = bf16[2,64,1024]{2,1,0:T(8,128)(2,1)S(1)} collective-permute-done((bf16[2,64,1024]{2,1,0:T(8,128)(2,1)S(1)}, bf16[2,64,1024]{2,1,0:T(8,128)(2,1)S(1)}, u32[]{:S(2)}, u32[]{:S(2)}) %collective-permute-start.1) | collective-permute-done | bytes 262176 | tf_op jit(solution)/shard_map/ppermute | solution.py:52
  20.7 1.7 %collective-permute-start.10 = (bf16[1,4,32,1024]{3,2,1,0:T(8,128)(2,1)S(1)}, bf16[1,4,32,1024]{3,2,1,0:T(8,128)(2,1)S(1)}, u32[]{:S(2)}, u32[]{:S(2)}) collective-permute-start(bf16[1,4,32,1024]{3,2,1,0:T(8,128)(2,1)S(1)} %get-tuple-element.59), channel_id=1, source_target_pairs={{0,2},{1,3},{2,0},{3,1},{4,6},{5,7},{6,4},{7,5},{8,10},{9,11},{10,... | collective-permute-start | bytes 786440 | tf_op jit(solution)/shard_map/ppermute | solution.py:52
  22.4 2.3 %collective-permute-start.4 = (bf16[1,64,1024]{2,1,0:T(8,128)(2,1)S(1)}, bf16[1,64,1024]{2,1,0:T(8,128)(2,1)S(1)}, u32[]{:S(2)}, u32[]{:S(2)}) collective-permute-start(bf16[1,64,1024]{2,1,0:T(8,128)(2,1)S(1)} %get-tuple-element.27), channel_id=1, source_target_pairs={{0,8},{1,9},{2,10},{3,11},{4,12},{5,13},{6,14},{7,15},{8,0},{9,1},... | collective-permute-start | bytes 393224 | tf_op jit(solution)/shard_map/ppermute | solution.py:52
  24.7 1.5 %collective-permute-start.2 = (bf16[1,4,32,1024]{3,2,1,0:T(8,128)(2,1)S(1)}, bf16[1,4,32,1024]{3,2,1,0:T(8,128)(2,1)S(1)}, u32[]{:S(2)}, u32[]{:S(2)}) collective-permute-start(bf16[1,4,32,1024]{3,2,1,0:T(8,128)(2,1)S(1)} %get-tuple-element.60), channel_id=1, source_target_pairs={{0,16},{16,0},{1,17},{17,1},{2,18},{18,2},{3,19},{19,3},{4,20},{20... | collective-permute-start | bytes 786440 | tf_op jit(solution)/shard_map/ppermute | solution.py:56
  26.2 4.4 %collective-permute-done.4 = bf16[1,64,1024]{2,1,0:T(8,128)(2,1)S(1)} collective-permute-done((bf16[1,64,1024]{2,1,0:T(8,128)(2,1)S(1)}, bf16[1,64,1024]{2,1,0:T(8,128)(2,1)S(1)}, u32[]{:S(2)}, u32[]{:S(2)}) %collective-permute-start.4) | collective-permute-done | bytes 131104 | tf_op jit(solution)/shard_map/ppermute | solution.py:52
  31.0 1.6 %collective-permute-start.11 = (bf16[2,4,32,1024]{3,2,1,0:T(8,128)(2,1)S(1)}, bf16[2,4,32,1024]{3,2,1,0:T(8,128)(2,1)S(1)}, u32[]{:S(2)}, u32[]{:S(2)}) collective-permute-start(bf16[2,4,32,1024]{3,2,1,0:T(8,128)(2,1)S(1)} %pad_maximum_fusion.5.refs_5_), channel_id=1, source_target_pairs={{0,16},{16,0},{1,17},{17,1},{2,18},{18,2},{3,19},{19,3},{4,20},{20... | collective-permute-start | bytes 1572872 | tf_op jit(solution)/shard_map/ppermute | solution.py:56
  32.6 0.6 collective-permute-start.3
  33.3 4.8 %collective-permute-done.5 = bf16[2,64,1024]{2,1,0:T(8,128)(2,1)S(1)} collective-permute-done((bf16[2,64,1024]{2,1,0:T(8,128)(2,1)S(1)}, bf16[2,64,1024]{2,1,0:T(8,128)(2,1)S(1)}, u32[]{:S(2)}, u32[]{:S(2)}) %collective-permute-start.5) | collective-permute-done | bytes 262176 | tf_op jit(solution)/shard_map/ppermute | solution.py:52
  38.2 1.6 %collective-permute-start.6 = (bf16[1,4,32,1024]{3,2,1,0:T(8,128)(2,1)S(1)}, bf16[1,4,32,1024]{3,2,1,0:T(8,128)(2,1)S(1)}, u32[]{:S(2)}, u32[]{:S(2)}) collective-permute-start(bf16[1,4,32,1024]{3,2,1,0:T(8,128)(2,1)S(1)} %get-tuple-element.62), channel_id=1, source_target_pairs={{0,16},{16,0},{1,17},{17,1},{2,18},{18,2},{3,19},{19,3},{4,20},{20... | collective-permute-start | bytes 786440 | tf_op jit(solution)/shard_map/ppermute | solution.py:56
  39.8 0.8 collective-permute-start.7
  40.6 9.2 %collective-permute-done.6 = bf16[1,4,32,1024]{3,2,1,0:T(8,128)(2,1)S(1)} collective-permute-done((bf16[1,4,32,1024]{3,2,1,0:T(8,128)(2,1)S(1)}, bf16[1,4,32,1024]{3,2,1,0:T(8,128)(2,1)S(1)}, u32[]{:S(2)}, u32[]{:S(2)}) %collective-permute-start.6) | collective-permute-done | bytes 262176 | tf_op jit(solution)/shard_map/ppermute | solution.py:56
  49.8 1.3 collective-permute-done.7
  52.3 1.1 pad_maximum_fusion.7.refs_5_
  54.0 1.0 pad_maximum_fusion.6.refs_1_
  55.6 1.9 %copy-done = bf16[1,768,2048]{2,1,0:T(8,128)(2,1)S(1)} copy-done((bf16[1,768,2048]{2,1,0:T(8,128)(2,1)S(1)}, bf16[1,768,2048]{2,1,0:T(8,128)(2,1)}, u32[]{:S(2)}) %copy-start) | copy-done | bytes 3145752
  57.5 13.5 %ffn.2 = (bf16[2,4,2,32,1024]{4,3,2,1,0:T(8,128)(2,1)S(1)}, bf16[2,4,2,32,1024]{4,3,2,1,0:T(8,128)(2,1)S(1)}, bf16[4,2,32,1024]{3,2,1,0:T(8,128)(2,1)S(1)}, bf16...) custom-call(s32[1]{0:T(128)} %bitcast.refs_0_, bf16[2,4,32,1024]{3,2,1,0:T(8,128)(2,1)S(1)} %pad_maximum_fusion.3.refs_1_, ...), custom_call_target="tpu_custom_call" | custom-call | flops 10000000000 | bytes 20000000 | tf_op jit(solution)/shard_map/ffn/pallas_call | solution.py:136
  72.2 0.8 collective-permute-done.15
  74.5 1.5 %collective-permute-start.16 = (bf16[4,2,32,1024]{3,2,1,0:T(8,128)(2,1)S(1)}, bf16[4,2,32,1024]{3,2,1,0:T(8,128)(2,1)S(1)}, u32[]{:S(2)}, u32[]{:S(2)}) collective-permute-start(bf16[4,2,32,1024]{3,2,1,0:T(8,128)(2,1)S(1)} %get-tuple-element.56), channel_id=1, source_target_pairs={{0,2},{1,3},{2,0},{3,1},{4,6},{5,7},{6,4},{7,5},{8,10},{9,11},{10,... | collective-permute-start | bytes 1572872 | tf_op jit(solution)/shard_map/ppermute | solution.py:52
  75.9 1.5 %collective-permute-start.18 = (bf16[4,2,32,1024]{3,2,1,0:T(8,128)(2,1)S(1)}, bf16[4,2,32,1024]{3,2,1,0:T(8,128)(2,1)S(1)}, u32[]{:S(2)}, u32[]{:S(2)}) collective-permute-start(bf16[4,2,32,1024]{3,2,1,0:T(8,128)(2,1)S(1)} %get-tuple-element.55), channel_id=1, source_target_pairs={{0,16},{16,0},{1,17},{17,1},{2,18},{18,2},{3,19},{19,3},{4,20},{20... | collective-permute-start | bytes 1572872 | tf_op jit(solution)/shard_map/ppermute | solution.py:56
  77.4 12.2 %ffn.3 = (bf16[2,2,4,32,1024]{4,3,2,1,0:T(8,128)(2,1)S(1)}, bf16[2,2,4,32,1024]{4,3,2,1,0:T(8,128)(2,1)S(1)}, bf16[2,4,32,1024]{3,2,1,0:T(8,128)(2,1)S(1)}, bf16...) custom-call(s32[1]{0:T(128)} %bitcast.refs_0_, bf16[2,4,32,1024]{3,2,1,0:T(8,128)(2,1)S(1)} %pad_maximum_fusion.6.refs_1_, ...), custom_call_target="tpu_custom_call" | custom-call | flops 10000000000 | bytes 20000000 | tf_op jit(solution)/shard_map/ffn/pallas_call | solution.py:136
  90.3 1.4 %collective-permute-done.30 = bf16[2,4,32,1024]{3,2,1,0:T(8,128)(2,1)S(1)} collective-permute-done((bf16[2,4,32,1024]{3,2,1,0:T(8,128)(2,1)S(1)}, bf16[2,4,32,1024]{3,2,1,0:T(8,128)(2,1)S(1)}, u32[]{:S(2)}, u32[]{:S(2)}) %collective-permute-start.30) | collective-permute-done | bytes 524320 | tf_op jit(solution)/shard_map/ppermute | solution.py:52
  91.6 0.7 collective-permute-done.33
  92.8 1.0 collective-permute-start.31
  93.8 1.5 %collective-permute-start.34 = (bf16[2,4,32,1024]{3,2,1,0:T(8,128)(2,1)S(1)}, bf16[2,4,32,1024]{3,2,1,0:T(8,128)(2,1)S(1)}, u32[]{:S(2)}, u32[]{:S(2)}) collective-permute-start(bf16[2,4,32,1024]{3,2,1,0:T(8,128)(2,1)S(1)} %get-tuple-element.53), channel_id=1, source_target_pairs={{0,16},{16,0},{1,17},{17,1},{2,18},{18,2},{3,19},{19,3},{4,20},{20... | collective-permute-start | bytes 1572872 | tf_op jit(solution)/shard_map/ppermute | solution.py:56
  96.0 1.5 %collective-permute-start.19 = (bf16[2,4,32,1024]{3,2,1,0:T(8,128)(2,1)S(1)}, bf16[2,4,32,1024]{3,2,1,0:T(8,128)(2,1)S(1)}, u32[]{:S(2)}, u32[]{:S(2)}) collective-permute-start(bf16[2,4,32,1024]{3,2,1,0:T(8,128)(2,1)S(1)} %fusion.2), channel_id=1, source_target_pairs={{0,4},{1,5},{2,6},{3,7},{4,0},{5,1},{6,2},{7,3},{8,12},{9,13},{10,... | collective-permute-start | bytes 1572872 | tf_op jit(solution)/shard_map/ppermute | solution.py:52
  97.4 9.4 %collective-permute-done.31 = bf16[2,4,32,1024]{3,2,1,0:T(8,128)(2,1)S(1)} collective-permute-done((bf16[2,4,32,1024]{3,2,1,0:T(8,128)(2,1)S(1)}, bf16[2,4,32,1024]{3,2,1,0:T(8,128)(2,1)S(1)}, u32[]{:S(2)}, u32[]{:S(2)}) %collective-permute-start.31) | collective-permute-done | bytes 524320 | tf_op jit(solution)/shard_map/ppermute | solution.py:52
  106.8 0.6 collective-permute-done.34
  108.1 1.2 collective-permute-start.35
  109.3 1.6 %collective-permute-start.32 = (bf16[4,32,1024]{2,1,0:T(8,128)(2,1)S(1)}, bf16[4,32,1024]{2,1,0:T(8,128)(2,1)S(1)}, u32[]{:S(2)}, u32[]{:S(2)}) collective-permute-start(bf16[4,32,1024]{2,1,0:T(8,128)(2,1)S(1)} %fusion.12), channel_id=1, source_target_pairs={{0,16},{16,0},{1,17},{17,1},{2,18},{18,2},{3,19},{19,3},{4,20},{20... | collective-permute-start | bytes 786440 | tf_op jit(solution)/shard_map/ppermute | solution.py:56
  111.1 3.4 %collective-permute-start.20 = (bf16[1,4,32,1024]{3,2,1,0:T(8,128)(2,1)S(1)}, bf16[1,4,32,1024]{3,2,1,0:T(8,128)(2,1)S(1)}, u32[]{:S(2)}, u32[]{:S(2)}) collective-permute-start(bf16[1,4,32,1024]{3,2,1,0:T(8,128)(2,1)S(1)} %slice.246), channel_id=1, source_target_pairs={{0,8},{1,9},{2,10},{3,11},{4,12},{5,13},{6,14},{7,15},{8,0},{9,1},... | collective-permute-start | bytes 786440 | tf_op jit(solution)/shard_map/ppermute | solution.py:52
  114.5 0.8 collective-permute-done.35
  115.4 0.9 collective-permute-done.32
  116.4 1.5 %collective-permute-start.36 = (bf16[2,64,1024]{2,1,0:T(8,128)(2,1)S(1)}, bf16[2,64,1024]{2,1,0:T(8,128)(2,1)S(1)}, u32[]{:S(2)}, u32[]{:S(2)}) collective-permute-start(bf16[2,64,1024]{2,1,0:T(8,128)(2,1)S(1)} %fusion.9), channel_id=1, source_target_pairs={{0,4},{1,5},{2,6},{3,7},{4,0},{5,1},{6,2},{7,3},{8,12},{9,13},{10,... | collective-permute-start | bytes 786440 | tf_op jit(solution)/shard_map/ppermute | solution.py:52
  117.9 7.3 %collective-permute-done.20 = bf16[1,4,32,1024]{3,2,1,0:T(8,128)(2,1)S(1)} collective-permute-done((bf16[1,4,32,1024]{3,2,1,0:T(8,128)(2,1)S(1)}, bf16[1,4,32,1024]{3,2,1,0:T(8,128)(2,1)S(1)}, u32[]{:S(2)}, u32[]{:S(2)}) %collective-permute-start.20) | collective-permute-done | bytes 262176 | tf_op jit(solution)/shard_map/ppermute | solution.py:52
  125.9 0.9 collective-permute-start.22
  126.8 1.1 collective-permute-done.36
  128.2 1.4 %collective-permute-done.21 = bf16[32,1024]{1,0:T(8,128)(2,1)S(1)} collective-permute-done((bf16[32,1024]{1,0:T(8,128)(2,1)S(1)}, bf16[32,1024]{1,0:T(8,128)(2,1)S(1)}, u32[]{:S(2)}, u32[]{:S(2)}) %collective-permute-start.21) | collective-permute-done | bytes 65568 | tf_op jit(solution)/shard_map/ppermute | solution.py:56
  130.2 4.6 %collective-permute-done.37 = bf16[1,64,1024]{2,1,0:T(8,128)(2,1)S(1)} collective-permute-done((bf16[1,64,1024]{2,1,0:T(8,128)(2,1)S(1)}, bf16[1,64,1024]{2,1,0:T(8,128)(2,1)S(1)}, u32[]{:S(2)}, u32[]{:S(2)}) %collective-permute-start.37) | collective-permute-done | bytes 131104 | tf_op jit(solution)/shard_map/ppermute | solution.py:52
  134.7 0.7 pad_maximum_fusion.10
  (80 shorter events, 10.7 us)
Async XLA Ops:
  1.0 10.7 %collective-permute-start = (bf16[1,64,1024]{2,1,0:T(8,128)(2,1)S(1)}, bf16[1,64,1024]{2,1,0:T(8,128)(2,1)S(1)}, u32[]{:S(2)}, u32[]{:S(2)}) collective-permute-start(bf16[1,64,1024]{2,1,0:T(8,128)(2,1)S(1)} %get-tuple-element.65), channel_id=1, source_target_pairs={{0,8},{1,9},{2,10},{3,11},{4,12},{5,13},{6,14},{7,15},{8,0},{9,1},... | collective-permute-start | bytes 393224 | tf_op jit(solution)/shard_map/ppermute | solution.py:52
  7.8 10.3 %all-to-all-start = ((f32[16,1,128]{2,1,0:T(1,128)}), f32[16,1,128]{2,1,0:T(1,128)S(1)}, u32[]{:S(2)}, u32[]{:S(2)}) async-start(f32[16,1,128]{2,1,0:T(1,128)} %bitcast.5), calls=%async_computation | async-start | bytes 16384 | tf_op jit(solution)/shard_map/all_to_all | solution.py:179
  11.8 8.8 %collective-permute-start.1 = (bf16[2,64,1024]{2,1,0:T(8,128)(2,1)S(1)}, bf16[2,64,1024]{2,1,0:T(8,128)(2,1)S(1)}, u32[]{:S(2)}, u32[]{:S(2)}) collective-permute-start(bf16[2,64,1024]{2,1,0:T(8,128)(2,1)S(1)} %pad_maximum_fusion.8), channel_id=1, source_target_pairs={{0,4},{1,5},{2,6},{3,7},{4,0},{5,1},{6,2},{7,3},{8,12},{9,13},{10,... | collective-permute-start | bytes 786440 | tf_op jit(solution)/shard_map/ppermute | solution.py:52
  20.7 10.3 %collective-permute-start.10 = (bf16[1,4,32,1024]{3,2,1,0:T(8,128)(2,1)S(1)}, bf16[1,4,32,1024]{3,2,1,0:T(8,128)(2,1)S(1)}, u32[]{:S(2)}, u32[]{:S(2)}) collective-permute-start(bf16[1,4,32,1024]{3,2,1,0:T(8,128)(2,1)S(1)} %get-tuple-element.59), channel_id=1, source_target_pairs={{0,2},{1,3},{2,0},{3,1},{4,6},{5,7},{6,4},{7,5},{8,10},{9,11},{10,... | collective-permute-start | bytes 786440 | tf_op jit(solution)/shard_map/ppermute | solution.py:52
  22.4 8.2 %collective-permute-start.4 = (bf16[1,64,1024]{2,1,0:T(8,128)(2,1)S(1)}, bf16[1,64,1024]{2,1,0:T(8,128)(2,1)S(1)}, u32[]{:S(2)}, u32[]{:S(2)}) collective-permute-start(bf16[1,64,1024]{2,1,0:T(8,128)(2,1)S(1)} %get-tuple-element.27), channel_id=1, source_target_pairs={{0,8},{1,9},{2,10},{3,11},{4,12},{5,13},{6,14},{7,15},{8,0},{9,1},... | collective-permute-start | bytes 393224 | tf_op jit(solution)/shard_map/ppermute | solution.py:52
  24.7 7.9 %collective-permute-start.2 = (bf16[1,4,32,1024]{3,2,1,0:T(8,128)(2,1)S(1)}, bf16[1,4,32,1024]{3,2,1,0:T(8,128)(2,1)S(1)}, u32[]{:S(2)}, u32[]{:S(2)}) collective-permute-start(bf16[1,4,32,1024]{3,2,1,0:T(8,128)(2,1)S(1)} %get-tuple-element.60), channel_id=1, source_target_pairs={{0,16},{16,0},{1,17},{17,1},{2,18},{18,2},{3,19},{19,3},{4,20},{20... | collective-permute-start | bytes 786440 | tf_op jit(solution)/shard_map/ppermute | solution.py:56
  30.6 7.5 %collective-permute-start.5 = (bf16[2,64,1024]{2,1,0:T(8,128)(2,1)S(1)}, bf16[2,64,1024]{2,1,0:T(8,128)(2,1)S(1)}, u32[]{:S(2)}, u32[]{:S(2)}) collective-permute-start(bf16[2,64,1024]{2,1,0:T(8,128)(2,1)S(1)} %pad_maximum_fusion.9), channel_id=1, source_target_pairs={{0,4},{1,5},{2,6},{3,7},{4,0},{5,1},{6,2},{7,3},{8,12},{9,13},{10,... | collective-permute-start | bytes 786440 | tf_op jit(solution)/shard_map/ppermute | solution.py:52
  31.0 20.1 %collective-permute-start.11 = (bf16[2,4,32,1024]{3,2,1,0:T(8,128)(2,1)S(1)}, bf16[2,4,32,1024]{3,2,1,0:T(8,128)(2,1)S(1)}, u32[]{:S(2)}, u32[]{:S(2)}) collective-permute-start(bf16[2,4,32,1024]{3,2,1,0:T(8,128)(2,1)S(1)} %pad_maximum_fusion.5.refs_5_), channel_id=1, source_target_pairs={{0,16},{16,0},{1,17},{17,1},{2,18},{18,2},{3,19},{19,3},{4,20},{20... | collective-permute-start | bytes 1572872 | tf_op jit(solution)/shard_map/ppermute | solution.py:56
  32.6 18.5 %collective-permute-start.3 = (bf16[2,4,32,1024]{3,2,1,0:T(8,128)(2,1)S(1)}, bf16[2,4,32,1024]{3,2,1,0:T(8,128)(2,1)S(1)}, u32[]{:S(2)}, u32[]{:S(2)}) collective-permute-start(bf16[2,4,32,1024]{3,2,1,0:T(8,128)(2,1)S(1)} %pad_maximum_fusion.3.refs_1_), channel_id=1, source_target_pairs={{0,2},{1,3},{2,0},{3,1},{4,6},{5,7},{6,4},{7,5},{8,10},{9,11},{10,... | collective-permute-start | bytes 1572872 | tf_op jit(solution)/shard_map/ppermute | solution.py:52
  38.2 13.5 %copy-start.2 = (bf16[1,4,32,1024]{3,2,1,0:T(8,128)(2,1)}, bf16[1,4,32,1024]{3,2,1,0:T(8,128)(2,1)S(1)}, u32[]{:S(2)}) copy-start(bf16[1,4,32,1024]{3,2,1,0:T(8,128)(2,1)S(1)} %get-tuple-element.61) | copy-start | bytes 786436
  38.2 11.6 %collective-permute-start.6 = (bf16[1,4,32,1024]{3,2,1,0:T(8,128)(2,1)S(1)}, bf16[1,4,32,1024]{3,2,1,0:T(8,128)(2,1)S(1)}, u32[]{:S(2)}, u32[]{:S(2)}) collective-permute-start(bf16[1,4,32,1024]{3,2,1,0:T(8,128)(2,1)S(1)} %get-tuple-element.62), channel_id=1, source_target_pairs={{0,16},{16,0},{1,17},{17,1},{2,18},{18,2},{3,19},{19,3},{4,20},{20... | collective-permute-start | bytes 786440 | tf_op jit(solution)/shard_map/ppermute | solution.py:56
  39.8 11.4 %collective-permute-start.7 = (bf16[1,4,32,1024]{3,2,1,0:T(8,128)(2,1)S(1)}, bf16[1,4,32,1024]{3,2,1,0:T(8,128)(2,1)S(1)}, u32[]{:S(2)}, u32[]{:S(2)}) collective-permute-start(bf16[1,4,32,1024]{3,2,1,0:T(8,128)(2,1)S(1)} %get-tuple-element.61), channel_id=1, source_target_pairs={{0,2},{1,3},{2,0},{3,1},{4,6},{5,7},{6,4},{7,5},{8,10},{9,11},{10,... | collective-permute-start | bytes 786440 | tf_op jit(solution)/shard_map/ppermute | solution.py:52
  40.6 14.4 %collective-permute-start.12 = (bf16[2,4,32,1024]{3,2,1,0:T(8,128)(2,1)S(1)}, bf16[2,4,32,1024]{3,2,1,0:T(8,128)(2,1)}, u32[]{:S(2)}, u32[]{:S(2)}) collective-permute-start(bf16[2,4,32,1024]{3,2,1,0:T(8,128)(2,1)S(1)} %pad_maximum_fusion.5.refs_5_), channel_id=1, source_target_pairs={{0,1},{1,0},{2,3},{3,2},{4,5},{5,4},{6,7},{7,6},{8,9},{9,8},{10,11... | collective-permute-start | bytes 1572872 | tf_op jit(solution)/shard_map/ppermute | solution.py:52
  49.8 1.9 %copy-start.3 = (bf16[1,4,32,1024]{3,2,1,0:T(8,128)(2,1)}, bf16[1,4,32,1024]{3,2,1,0:T(8,128)(2,1)S(1)}, u32[]{:S(2)}) copy-start(bf16[1,4,32,1024]{3,2,1,0:T(8,128)(2,1)S(1)} %collective-permute-done.6) | copy-start | bytes 786436
  49.8 5.8 %collective-permute-start.8 = (bf16[2,4,32,1024]{3,2,1,0:T(8,128)(2,1)S(1)}, bf16[2,4,32,1024]{3,2,1,0:T(8,128)(2,1)}, u32[]{:S(2)}, u32[]{:S(2)}) collective-permute-start(bf16[2,4,32,1024]{3,2,1,0:T(8,128)(2,1)S(1)} %pad_maximum_fusion.3.refs_1_), channel_id=1, source_target_pairs={{0,1},{1,0},{2,3},{3,2},{4,5},{5,4},{6,7},{7,6},{8,9},{9,8},{10,11... | collective-permute-start | bytes 1572872 | tf_op jit(solution)/shard_map/ppermute | solution.py:52
  51.1 0.7 copy-start.4
  51.1 4.5 %collective-permute-start.13 = (bf16[2,4,32,1024]{3,2,1,0:T(8,128)(2,1)S(1)}, bf16[2,4,32,1024]{3,2,1,0:T(8,128)(2,1)}, u32[]{:S(2)}, u32[]{:S(2)}) collective-permute-start(bf16[2,4,32,1024]{3,2,1,0:T(8,128)(2,1)S(1)} %collective-permute-done.11.refs_6_), channel_id=1, source_target_pairs={{0,1},{1,0},{2,3},{3,2},{4,5},{5,4},{6,7},{7,6},{8,9},{9,8},{10,11... | collective-permute-start | bytes 1572872 | tf_op jit(solution)/shard_map/ppermute | solution.py:52
  51.1 4.5 %collective-permute-start.9 = (bf16[2,4,32,1024]{3,2,1,0:T(8,128)(2,1)S(1)}, bf16[2,4,32,1024]{3,2,1,0:T(8,128)(2,1)}, u32[]{:S(2)}, u32[]{:S(2)}) collective-permute-start(bf16[2,4,32,1024]{3,2,1,0:T(8,128)(2,1)S(1)} %collective-permute-done.3.refs_2_), channel_id=1, source_target_pairs={{0,1},{1,0},{2,3},{3,2},{4,5},{5,4},{6,7},{7,6},{8,9},{9,8},{10,11... | collective-permute-start | bytes 1572872 | tf_op jit(solution)/shard_map/ppermute | solution.py:52
  53.4 18.2 %collective-permute-start.26 = (bf16[2,4,32,1024]{3,2,1,0:T(8,128)(2,1)S(1)}, bf16[2,4,32,1024]{3,2,1,0:T(8,128)(2,1)S(1)}, u32[]{:S(2)}, u32[]{:S(2)}) collective-permute-start(bf16[2,4,32,1024]{3,2,1,0:T(8,128)(2,1)S(1)} %pad_maximum_fusion.7.refs_5_), channel_id=1, source_target_pairs={{0,16},{16,0},{1,17},{17,1},{2,18},{18,2},{3,19},{19,3},{4,20},{20... | collective-permute-start | bytes 1572872 | tf_op jit(solution)/shard_map/ppermute | solution.py:56
  55.0 17.1 %collective-permute-start.23 = (bf16[2,4,32,1024]{3,2,1,0:T(8,128)(2,1)S(1)}, bf16[2,4,32,1024]{3,2,1,0:T(8,128)(2,1)S(1)}, u32[]{:S(2)}, u32[]{:S(2)}) collective-permute-start(bf16[2,4,32,1024]{3,2,1,0:T(8,128)(2,1)S(1)} %pad_maximum_fusion.6.refs_1_), channel_id=1, source_target_pairs={{0,2},{1,3},{2,0},{3,1},{4,6},{5,7},{6,4},{7,5},{8,10},{9,11},{10,... | collective-permute-start | bytes 1572872 | tf_op jit(solution)/shard_map/ppermute | solution.py:52
  55.6 1.9 %copy-start = (bf16[1,768,2048]{2,1,0:T(8,128)(2,1)S(1)}, bf16[1,768,2048]{2,1,0:T(8,128)(2,1)}, u32[]{:S(2)}) copy-start(bf16[1,768,2048]{2,1,0:T(8,128)(2,1)} %refs_10_.3) | copy-start | bytes 9437188
  71.0 6.5 %copy-start.1 = (bf16[1,768,2048]{2,1,0:T(8,128)(2,1)S(1)}, bf16[1,768,2048]{2,1,0:T(8,128)(2,1)}, u32[]{:S(2)}) copy-start(bf16[1,768,2048]{2,1,0:T(8,128)(2,1)} %refs_10_.3) | copy-start | bytes 9437188
  71.0 2.0 %collective-permute-start.15 = (bf16[4,2,32,1024]{3,2,1,0:T(8,128)(2,1)S(1)}, bf16[4,2,32,1024]{3,2,1,0:T(8,128)(2,1)S(1)}, u32[]{:S(2)}, u32[]{:S(2)}) collective-permute-start(bf16[4,2,32,1024]{3,2,1,0:T(8,128)(2,1)S(1)} %get-tuple-element.34), channel_id=1, source_target_pairs={{0,1},{1,0},{2,3},{3,2},{4,5},{5,4},{6,7},{7,6},{8,9},{9,8},{10,11... | collective-permute-start | bytes 1572872 | tf_op jit(solution)/shard_map/ppermute | solution.py:52
  71.1 2.6 %collective-permute-start.17 = (bf16[4,2,32,1024]{3,2,1,0:T(8,128)(2,1)S(1)}, bf16[4,2,32,1024]{3,2,1,0:T(8,128)(2,1)S(1)}, u32[]{:S(2)}, u32[]{:S(2)}) collective-permute-start(bf16[4,2,32,1024]{3,2,1,0:T(8,128)(2,1)S(1)} %get-tuple-element.35), channel_id=1, source_target_pairs={{0,1},{1,0},{2,3},{3,2},{4,5},{5,4},{6,7},{7,6},{8,9},{9,8},{10,11... | collective-permute-start | bytes 1572872 | tf_op jit(solution)/shard_map/ppermute | solution.py:52
  71.6 2.9 %collective-permute-start.28 = (bf16[2,4,32,1024]{3,2,1,0:T(8,128)(2,1)S(1)}, bf16[2,4,32,1024]{3,2,1,0:T(8,128)(2,1)S(1)}, u32[]{:S(2)}, u32[]{:S(2)}) collective-permute-start(bf16[2,4,32,1024]{3,2,1,0:T(8,128)(2,1)S(1)} %collective-permute-done.26.refs_6_), channel_id=1, source_target_pairs={{0,1},{1,0},{2,3},{3,2},{4,5},{5,4},{6,7},{7,6},{8,9},{9,8},{10,11... | collective-permute-start | bytes 1572872 | tf_op jit(solution)/shard_map/ppermute | solution.py:52
  71.7 4.3 %collective-permute-start.27 = (bf16[2,4,32,1024]{3,2,1,0:T(8,128)(2,1)S(1)}, bf16[2,4,32,1024]{3,2,1,0:T(8,128)(2,1)S(1)}, u32[]{:S(2)}, u32[]{:S(2)}) collective-permute-start(bf16[2,4,32,1024]{3,2,1,0:T(8,128)(2,1)S(1)} %pad_maximum_fusion.7.refs_5_), channel_id=1, source_target_pairs={{0,1},{1,0},{2,3},{3,2},{4,5},{5,4},{6,7},{7,6},{8,9},{9,8},{10,11... | collective-permute-start | bytes 1572872 | tf_op jit(solution)/shard_map/ppermute | solution.py:52
  72.1 5.3 %collective-permute-start.25 = (bf16[2,4,32,1024]{3,2,1,0:T(8,128)(2,1)S(1)}, bf16[2,4,32,1024]{3,2,1,0:T(8,128)(2,1)S(1)}, u32[]{:S(2)}, u32[]{:S(2)}) collective-permute-start(bf16[2,4,32,1024]{3,2,1,0:T(8,128)(2,1)S(1)} %collective-permute-done.23.refs_2_), channel_id=1, source_target_pairs={{0,1},{1,0},{2,3},{3,2},{4,5},{5,4},{6,7},{7,6},{8,9},{9,8},{10,11... | collective-permute-start | bytes 1572872 | tf_op jit(solution)/shard_map/ppermute | solution.py:52
  73.0 4.5 %collective-permute-start.24 = (bf16[2,4,32,1024]{3,2,1,0:T(8,128)(2,1)S(1)}, bf16[2,4,32,1024]{3,2,1,0:T(8,128)(2,1)S(1)}, u32[]{:S(2)}, u32[]{:S(2)}) collective-permute-start(bf16[2,4,32,1024]{3,2,1,0:T(8,128)(2,1)S(1)} %pad_maximum_fusion.6.refs_1_), channel_id=1, source_target_pairs={{0,1},{1,0},{2,3},{3,2},{4,5},{5,4},{6,7},{7,6},{8,9},{9,8},{10,11... | collective-permute-start | bytes 1572872 | tf_op jit(solution)/shard_map/ppermute | solution.py:52
  73.7 21.6 %collective-permute-start.14 = (bf16[2,4,2,32,1024]{4,3,2,1,0:T(8,128)(2,1)S(1)}, bf16[2,4,2,32,1024]{4,3,2,1,0:T(8,128)(2,1)S(1)}, u32[]{:S(2)}, u32[]{:S(2)}) collective-permute-start(bf16[2,4,2,32,1024]{4,3,2,1,0:T(8,128)(2,1)S(1)} %get-tuple-element.32), channel_id=1, source_target_pairs={{0,1},{1,0},{2,3},{3,2},{4,5},{5,4},{6,7},{7,6},{8,9},{9,8},{10,11... | collective-permute-start | bytes 3145736 | tf_op jit(solution)/shard_map/ppermute | solution.py:52
  74.5 15.1 %collective-permute-start.16 = (bf16[4,2,32,1024]{3,2,1,0:T(8,128)(2,1)S(1)}, bf16[4,2,32,1024]{3,2,1,0:T(8,128)(2,1)S(1)}, u32[]{:S(2)}, u32[]{:S(2)}) collective-permute-start(bf16[4,2,32,1024]{3,2,1,0:T(8,128)(2,1)S(1)} %get-tuple-element.56), channel_id=1, source_target_pairs={{0,2},{1,3},{2,0},{3,1},{4,6},{5,7},{6,4},{7,5},{8,10},{9,11},{10,... | collective-permute-start | bytes 1572872 | tf_op jit(solution)/shard_map/ppermute | solution.py:52
  75.9 13.8 %collective-permute-start.18 = (bf16[4,2,32,1024]{3,2,1,0:T(8,128)(2,1)S(1)}, bf16[4,2,32,1024]{3,2,1,0:T(8,128)(2,1)S(1)}, u32[]{:S(2)}, u32[]{:S(2)}) collective-permute-start(bf16[4,2,32,1024]{3,2,1,0:T(8,128)(2,1)S(1)} %get-tuple-element.55), channel_id=1, source_target_pairs={{0,16},{16,0},{1,17},{17,1},{2,18},{18,2},{3,19},{19,3},{4,20},{20... | collective-permute-start | bytes 1572872 | tf_op jit(solution)/shard_map/ppermute | solution.py:56
  89.7 1.9 %collective-permute-start.30 = (bf16[2,4,32,1024]{3,2,1,0:T(8,128)(2,1)S(1)}, bf16[2,4,32,1024]{3,2,1,0:T(8,128)(2,1)S(1)}, u32[]{:S(2)}, u32[]{:S(2)}) collective-permute-start(bf16[2,4,32,1024]{3,2,1,0:T(8,128)(2,1)S(1)} %get-tuple-element.44), channel_id=1, source_target_pairs={{0,1},{1,0},{2,3},{3,2},{4,5},{5,4},{6,7},{7,6},{8,9},{9,8},{10,11... | collective-permute-start | bytes 1572872 | tf_op jit(solution)/shard_map/ppermute | solution.py:52
  89.7 2.7 %collective-permute-start.33 = (bf16[2,4,32,1024]{3,2,1,0:T(8,128)(2,1)S(1)}, bf16[2,4,32,1024]{3,2,1,0:T(8,128)(2,1)S(1)}, u32[]{:S(2)}, u32[]{:S(2)}) collective-permute-start(bf16[2,4,32,1024]{3,2,1,0:T(8,128)(2,1)S(1)} %get-tuple-element.46), channel_id=1, source_target_pairs={{0,1},{1,0},{2,3},{3,2},{4,5},{5,4},{6,7},{7,6},{8,9},{9,8},{10,11... | collective-permute-start | bytes 1572872 | tf_op jit(solution)/shard_map/ppermute | solution.py:52
  90.2 7.2 %collective-permute-start.29 = (bf16[2,2,4,32,1024]{4,3,2,1,0:T(8,128)(2,1)S(1)}, bf16[2,2,4,32,1024]{4,3,2,1,0:T(8,128)(2,1)S(1)}, u32[]{:S(2)}, u32[]{:S(2)}) collective-permute-start(bf16[2,2,4,32,1024]{4,3,2,1,0:T(8,128)(2,1)S(1)} %get-tuple-element.41), channel_id=1, source_target_pairs={{0,1},{1,0},{2,3},{3,2},{4,5},{5,4},{6,7},{7,6},{8,9},{9,8},{10,11... | collective-permute-start | bytes 3145736 | tf_op jit(solution)/shard_map/ppermute | solution.py:52
  92.8 14.0 %collective-permute-start.31 = (bf16[2,4,32,1024]{3,2,1,0:T(8,128)(2,1)S(1)}, bf16[2,4,32,1024]{3,2,1,0:T(8,128)(2,1)S(1)}, u32[]{:S(2)}, u32[]{:S(2)}) collective-permute-start(bf16[2,4,32,1024]{3,2,1,0:T(8,128)(2,1)S(1)} %get-tuple-element.54), channel_id=1, source_target_pairs={{0,2},{1,3},{2,0},{3,1},{4,6},{5,7},{6,4},{7,5},{8,10},{9,11},{10,... | collective-permute-start | bytes 1572872 | tf_op jit(solution)/shard_map/ppermute | solution.py:52
  93.8 13.7 %collective-permute-start.34 = (bf16[2,4,32,1024]{3,2,1,0:T(8,128)(2,1)S(1)}, bf16[2,4,32,1024]{3,2,1,0:T(8,128)(2,1)S(1)}, u32[]{:S(2)}, u32[]{:S(2)}) collective-permute-start(bf16[2,4,32,1024]{3,2,1,0:T(8,128)(2,1)S(1)} %get-tuple-element.53), channel_id=1, source_target_pairs={{0,16},{16,0},{1,17},{17,1},{2,18},{18,2},{3,19},{19,3},{4,20},{20... | collective-permute-start | bytes 1572872 | tf_op jit(solution)/shard_map/ppermute | solution.py:56
  96.0 14.9 %collective-permute-start.19 = (bf16[2,4,32,1024]{3,2,1,0:T(8,128)(2,1)S(1)}, bf16[2,4,32,1024]{3,2,1,0:T(8,128)(2,1)S(1)}, u32[]{:S(2)}, u32[]{:S(2)}) collective-permute-start(bf16[2,4,32,1024]{3,2,1,0:T(8,128)(2,1)S(1)} %fusion.2), channel_id=1, source_target_pairs={{0,4},{1,5},{2,6},{3,7},{4,0},{5,1},{6,2},{7,3},{8,12},{9,13},{10,... | collective-permute-start | bytes 1572872 | tf_op jit(solution)/shard_map/ppermute | solution.py:52
  108.1 7.3 %collective-permute-start.35 = (bf16[4,32,1024]{2,1,0:T(8,128)(2,1)S(1)}, bf16[4,32,1024]{2,1,0:T(8,128)(2,1)S(1)}, u32[]{:S(2)}, u32[]{:S(2)}) collective-permute-start(bf16[4,32,1024]{2,1,0:T(8,128)(2,1)S(1)} %fusion.13), channel_id=1, source_target_pairs={{0,2},{1,3},{2,0},{3,1},{4,6},{5,7},{6,4},{7,5},{8,10},{9,11},{10,... | collective-permute-start | bytes 786440 | tf_op jit(solution)/shard_map/ppermute | solution.py:52
  109.3 7.0 %collective-permute-start.32 = (bf16[4,32,1024]{2,1,0:T(8,128)(2,1)S(1)}, bf16[4,32,1024]{2,1,0:T(8,128)(2,1)S(1)}, u32[]{:S(2)}, u32[]{:S(2)}) collective-permute-start(bf16[4,32,1024]{2,1,0:T(8,128)(2,1)S(1)} %fusion.12), channel_id=1, source_target_pairs={{0,16},{16,0},{1,17},{17,1},{2,18},{18,2},{3,19},{19,3},{4,20},{20... | collective-permute-start | bytes 786440 | tf_op jit(solution)/shard_map/ppermute | solution.py:56
  111.1 14.1 %collective-permute-start.20 = (bf16[1,4,32,1024]{3,2,1,0:T(8,128)(2,1)S(1)}, bf16[1,4,32,1024]{3,2,1,0:T(8,128)(2,1)S(1)}, u32[]{:S(2)}, u32[]{:S(2)}) collective-permute-start(bf16[1,4,32,1024]{3,2,1,0:T(8,128)(2,1)S(1)} %slice.246), channel_id=1, source_target_pairs={{0,8},{1,9},{2,10},{3,11},{4,12},{5,13},{6,14},{7,15},{8,0},{9,1},... | collective-permute-start | bytes 786440 | tf_op jit(solution)/shard_map/ppermute | solution.py:52
  116.4 11.5 %collective-permute-start.36 = (bf16[2,64,1024]{2,1,0:T(8,128)(2,1)S(1)}, bf16[2,64,1024]{2,1,0:T(8,128)(2,1)S(1)}, u32[]{:S(2)}, u32[]{:S(2)}) collective-permute-start(bf16[2,64,1024]{2,1,0:T(8,128)(2,1)S(1)} %fusion.9), channel_id=1, source_target_pairs={{0,4},{1,5},{2,6},{3,7},{4,0},{5,1},{6,2},{7,3},{8,12},{9,13},{10,... | collective-permute-start | bytes 786440 | tf_op jit(solution)/shard_map/ppermute | solution.py:52
  125.3 4.3 %collective-permute-start.21 = (bf16[32,1024]{1,0:T(8,128)(2,1)S(1)}, bf16[32,1024]{1,0:T(8,128)(2,1)S(1)}, u32[]{:S(2)}, u32[]{:S(2)}) collective-permute-start(bf16[32,1024]{1,0:T(8,128)(2,1)S(1)} %get-tuple-element.63), channel_id=1, source_target_pairs={{0,16},{16,0},{1,17},{17,1},{2,18},{18,2},{3,19},{19,3},{4,20},{20... | collective-permute-start | bytes 196616 | tf_op jit(solution)/shard_map/ppermute | solution.py:56
  125.9 4.3 %collective-permute-start.22 = (bf16[32,1024]{1,0:T(8,128)(2,1)S(1)}, bf16[32,1024]{1,0:T(8,128)(2,1)S(1)}, u32[]{:S(2)}, u32[]{:S(2)}) collective-permute-start(bf16[32,1024]{1,0:T(8,128)(2,1)S(1)} %get-tuple-element.64), channel_id=1, source_target_pairs={{0,2},{1,3},{2,0},{3,1},{4,6},{5,7},{6,4},{7,5},{8,10},{9,11},{10,... | collective-permute-start | bytes 196616 | tf_op jit(solution)/shard_map/ppermute | solution.py:52
  128.0 6.8 %collective-permute-start.37 = (bf16[1,64,1024]{2,1,0:T(8,128)(2,1)S(1)}, bf16[1,64,1024]{2,1,0:T(8,128)(2,1)S(1)}, u32[]{:S(2)}, u32[]{:S(2)}) collective-permute-start(bf16[1,64,1024]{2,1,0:T(8,128)(2,1)S(1)} %slice.247), channel_id=1, source_target_pairs={{0,8},{1,9},{2,10},{3,11},{4,12},{5,13},{6,14},{7,15},{8,0},{9,1},... | collective-permute-start | bytes 393224 | tf_op jit(solution)/shard_map/ppermute | solution.py:52

commit v4 on v3

--- a/solution.py
+++ b/solution.py
@@ -73,7 +73,7 @@
         for h in range(2):
             at = pl.ds(h * (ff // 2), ff // 2)
             copies.append(pltpu.make_async_copy(src.at[0, at], dst.at[at], sems.at[2 * k + h]))
-    for copy in copies:
+    for copy in copies[:2]:
         copy.start()
     mine = half_ref[0]
     here = [pl.ds(pl.multiple_of((mine if s == 0 else 1 - mine) * part, part), part) for s in range(2)]
@@ -101,6 +101,8 @@
         if p == 0:
             copies[0].wait()
             copies[1].wait()
+            for copy in copies[2:]:
+                copy.start()
         gate = project(p, gate_ref)
         if p == 0:
             copies[2].wait()
@@ -194,6 +196,7 @@
         gots += [along["x"](a), along["y"](b)]
         a = jnp.concatenate([a, gots[-2]], axis=0)
         b = jnp.concatenate([b, gots[-1]], axis=0)
+        a, b = lax.optimization_barrier((a, b))
         return (a, along["y"](a)), (b, along["x"](b)), gots
 
     a, b, gots = spread(tokens[None, :2 * rows])

time: 136 us -> 136 us (level)
  transfers between devices with their start and end apart: 39 -> 39, of which waited for: 21 -> 22; matrix products, arithmetic and copies ran while one was open for 7% -> 7% of each run, Pallas kernels for 19% -> 19%
where the time goes in v4:
time: 136 us; the launch traced here: 135 us
  waiting for transfers between devices  55.8 us (41%)
  starting transfers between devices  40.3 us (30%)
  Pallas kernels  25.6 us (19%)
  other arithmetic  9 us (7%)
  local copies, waits for them, and re-layouts  4.35 us (3%)
    ppermute x30, waiting for transfers between devices, swap(): return lax.ppermute(value, 'expert', [(i, i ^ mask) for i in range(n)])  39 us
    ppermute x30, starting transfers between devices, swap(): return lax.ppermute(value, 'expert', [(i, i ^ mask) for i in range(n)])  26 us
    pallas_call x2, Pallas kernels, ffn(): pl.pallas_call(lambda *refs: ffn_kernel(half, z_first, *refs), out_shape=...  25.6 us
    ppermute x8, waiting for transfers between devices, swap_dp(): return lax.ppermute(value, 'dp', [(0, 1), (1, 0)])  13 us
    ppermute x8, starting transfers between devices, swap_dp(): return lax.ppermute(value, 'dp', [(0, 1), (1, 0)])  10.3 us
    all_to_all x1, starting transfers between devices, gather_all(): lax.all_to_all(dense, 'expert', split_axis=0, concat_axis=0, tiled=True)  3.91 us
    all_to_all x1, waiting for transfers between devices, gather_all(): lax.all_to_all(dense, 'expert', split_axis=0, concat_axis=0, tiled=True)  3.7 us
  transfers between devices with their start and end apart: 39, of which 22 were waited for; matrix products, arithmetic and copies ran while one was open for 7% of the time, Pallas kernels for 19%

profile of v4, /device:TPU:0, one launch (start us, length us, event | category | flops | bytes accessed | tf_op | source)
XLA Modules:
  0.0 135.3 jit_solution(15658407333990073942)
XLA Ops:
  0.0 1.0 slice_bitcast_fusion.9
  1.0 4.1 %collective-permute-start = (bf16[1,64,1024]{2,1,0:T(8,128)(2,1)S(1)}, bf16[1,64,1024]{2,1,0:T(8,128)(2,1)S(1)}, u32[]{:S(2)}, u32[]{:S(2)}) collective-permute-start(bf16[1,64,1024]{2,1,0:T(8,128)(2,1)S(1)} %get-tuple-element.73), channel_id=1, source_target_pairs={{0,8},{1,9},{2,10},{3,11},{4,12},{5,13},{6,14},{7,15},{8,0},{9,1},... | collective-permute-start | bytes 393224 | tf_op jit(solution)/shard_map/ppermute | solution.py:52
  5.1 0.7 reduce_sum.18
  5.8 0.7 divide_bitcast_fusion
  6.5 1.3 select_reduce_fusion
  7.8 3.9 %all-to-all-start = ((f32[16,1,128]{2,1,0:T(1,128)}), f32[16,1,128]{2,1,0:T(1,128)S(1)}, u32[]{:S(2)}, u32[]{:S(2)}) async-start(f32[16,1,128]{2,1,0:T(1,128)} %bitcast.5), calls=%async_computation | async-start | bytes 16384 | tf_op jit(solution)/shard_map/all_to_all | solution.py:181
  11.8 2.0 %collective-permute-start.1 = (bf16[2,64,1024]{2,1,0:T(8,128)(2,1)S(1)}, bf16[2,64,1024]{2,1,0:T(8,128)(2,1)S(1)}, u32[]{:S(2)}, u32[]{:S(2)}) collective-permute-start(bf16[2,64,1024]{2,1,0:T(8,128)(2,1)S(1)} %pad_maximum_fusion.8), channel_id=1, source_target_pairs={{0,4},{1,5},{2,6},{3,7},{4,0},{5,1},{6,2},{7,3},{8,12},{9,13},{10,... | collective-permute-start | bytes 786440 | tf_op jit(solution)/shard_map/ppermute | solution.py:52
  13.7 0.7 compare_select_fusion
  14.4 3.7 %all-to-all-done = f32[16,1,128]{2,1,0:T(1,128)S(1)} async-done(((f32[16,1,128]{2,1,0:T(1,128)}), f32[16,1,128]{2,1,0:T(1,128)S(1)}, u32[]{:S(2)}, u32[]{:S(2)}) %all-to-all-start) | async-done | bytes 8224 | tf_op jit(solution)/shard_map/all_to_all | solution.py:181
  18.8 1.8 %collective-permute-done.1 = bf16[2,64,1024]{2,1,0:T(8,128)(2,1)S(1)} collective-permute-done((bf16[2,64,1024]{2,1,0:T(8,128)(2,1)S(1)}, bf16[2,64,1024]{2,1,0:T(8,128)(2,1)S(1)}, u32[]{:S(2)}, u32[]{:S(2)}) %collective-permute-start.1) | collective-permute-done | bytes 262176 | tf_op jit(solution)/shard_map/ppermute | solution.py:52
  20.7 1.7 %collective-permute-start.3 = (bf16[1,4,32,1024]{3,2,1,0:T(8,128)(2,1)S(1)}, bf16[1,4,32,1024]{3,2,1,0:T(8,128)(2,1)S(1)}, u32[]{:S(2)}, u32[]{:S(2)}) collective-permute-start(bf16[1,4,32,1024]{3,2,1,0:T(8,128)(2,1)S(1)} %get-tuple-element.67), channel_id=1, source_target_pairs={{0,2},{1,3},{2,0},{3,1},{4,6},{5,7},{6,4},{7,5},{8,10},{9,11},{10,... | collective-permute-start | bytes 786440 | tf_op jit(solution)/shard_map/ppermute | solution.py:52
  22.4 2.3 %collective-permute-start.5 = (bf16[1,64,1024]{2,1,0:T(8,128)(2,1)S(1)}, bf16[1,64,1024]{2,1,0:T(8,128)(2,1)S(1)}, u32[]{:S(2)}, u32[]{:S(2)}) collective-permute-start(bf16[1,64,1024]{2,1,0:T(8,128)(2,1)S(1)} %get-tuple-element.32), channel_id=1, source_target_pairs={{0,8},{1,9},{2,10},{3,11},{4,12},{5,13},{6,14},{7,15},{8,0},{9,1},... | collective-permute-start | bytes 393224 | tf_op jit(solution)/shard_map/ppermute | solution.py:52
  24.7 1.5 %collective-permute-start.2 = (bf16[1,4,32,1024]{3,2,1,0:T(8,128)(2,1)S(1)}, bf16[1,4,32,1024]{3,2,1,0:T(8,128)(2,1)S(1)}, u32[]{:S(2)}, u32[]{:S(2)}) collective-permute-start(bf16[1,4,32,1024]{3,2,1,0:T(8,128)(2,1)S(1)} %get-tuple-element.68), channel_id=1, source_target_pairs={{0,16},{16,0},{1,17},{17,1},{2,18},{18,2},{3,19},{19,3},{4,20},{20... | collective-permute-start | bytes 786440 | tf_op jit(solution)/shard_map/ppermute | solution.py:56
  26.2 4.4 %collective-permute-done.5 = bf16[1,64,1024]{2,1,0:T(8,128)(2,1)S(1)} collective-permute-done((bf16[1,64,1024]{2,1,0:T(8,128)(2,1)S(1)}, bf16[1,64,1024]{2,1,0:T(8,128)(2,1)S(1)}, u32[]{:S(2)}, u32[]{:S(2)}) %collective-permute-start.5) | collective-permute-done | bytes 131104 | tf_op jit(solution)/shard_map/ppermute | solution.py:52
  31.0 0.7 collective-permute-done.2
  31.8 1.6 %collective-permute-start.11 = (bf16[2,4,32,1024]{3,2,1,0:T(8,128)(2,1)S(1)}, bf16[2,4,32,1024]{3,2,1,0:T(8,128)(2,1)S(1)}, u32[]{:S(2)}, u32[]{:S(2)}) collective-permute-start(bf16[2,4,32,1024]{3,2,1,0:T(8,128)(2,1)S(1)} %pad_maximum_fusion.4.refs_5_), channel_id=1, source_target_pairs={{0,16},{16,0},{1,17},{17,1},{2,18},{18,2},{3,19},{19,3},{4,20},{20... | collective-permute-start | bytes 1572872 | tf_op jit(solution)/shard_map/ppermute | solution.py:56
  33.9 4.2 %collective-permute-done.6 = bf16[2,64,1024]{2,1,0:T(8,128)(2,1)S(1)} collective-permute-done((bf16[2,64,1024]{2,1,0:T(8,128)(2,1)S(1)}, bf16[2,64,1024]{2,1,0:T(8,128)(2,1)S(1)}, u32[]{:S(2)}, u32[]{:S(2)}) %collective-permute-start.6) | collective-permute-done | bytes 262176 | tf_op jit(solution)/shard_map/ppermute | solution.py:52
  38.2 1.6 %collective-permute-start.7 = (bf16[1,4,32,1024]{3,2,1,0:T(8,128)(2,1)S(1)}, bf16[1,4,32,1024]{3,2,1,0:T(8,128)(2,1)S(1)}, u32[]{:S(2)}, u32[]{:S(2)}) collective-permute-start(bf16[1,4,32,1024]{3,2,1,0:T(8,128)(2,1)S(1)} %get-tuple-element.70), channel_id=1, source_target_pairs={{0,16},{16,0},{1,17},{17,1},{2,18},{18,2},{3,19},{19,3},{4,20},{20... | collective-permute-start | bytes 786440 | tf_op jit(solution)/shard_map/ppermute | solution.py:56
  39.8 0.8 collective-permute-start.8
  40.6 9.3 %collective-permute-done.7 = bf16[1,4,32,1024]{3,2,1,0:T(8,128)(2,1)S(1)} collective-permute-done((bf16[1,4,32,1024]{3,2,1,0:T(8,128)(2,1)S(1)}, bf16[1,4,32,1024]{3,2,1,0:T(8,128)(2,1)S(1)}, u32[]{:S(2)}, u32[]{:S(2)}) %collective-permute-start.7) | collective-permute-done | bytes 262176 | tf_op jit(solution)/shard_map/ppermute | solution.py:56
  49.9 1.2 collective-permute-done.8
  52.2 1.1 pad_maximum_fusion.7.refs_5_
  53.3 1.0 pad_maximum_fusion.6.refs_1_
  55.5 1.9 %copy-done = bf16[1,768,2048]{2,1,0:T(8,128)(2,1)S(1)} copy-done((bf16[1,768,2048]{2,1,0:T(8,128)(2,1)S(1)}, bf16[1,768,2048]{2,1,0:T(8,128)(2,1)}, u32[]{:S(2)}) %copy-start) | copy-done | bytes 3145752
  57.4 13.5 %ffn.2 = (bf16[2,4,2,32,1024]{4,3,2,1,0:T(8,128)(2,1)S(1)}, bf16[2,4,2,32,1024]{4,3,2,1,0:T(8,128)(2,1)S(1)}, bf16[4,2,32,1024]{3,2,1,0:T(8,128)(2,1)S(1)}, bf16...) custom-call(s32[1]{0:T(128)} %bitcast.refs_0_, bf16[2,4,32,1024]{3,2,1,0:T(8,128)(2,1)S(1)} %pad_maximum_fusion.3.refs_1_, ...), custom_call_target="tpu_custom_call" | custom-call | flops 10000000000 | bytes 20000000 | tf_op jit(solution)/shard_map/ffn/pallas_call | solution.py:138
  72.0 0.8 collective-permute-done.15
  74.3 1.5 %collective-permute-start.16 = (bf16[4,2,32,1024]{3,2,1,0:T(8,128)(2,1)S(1)}, bf16[4,2,32,1024]{3,2,1,0:T(8,128)(2,1)S(1)}, u32[]{:S(2)}, u32[]{:S(2)}) collective-permute-start(bf16[4,2,32,1024]{3,2,1,0:T(8,128)(2,1)S(1)} %get-tuple-element.64), channel_id=1, source_target_pairs={{0,2},{1,3},{2,0},{3,1},{4,6},{5,7},{6,4},{7,5},{8,10},{9,11},{10,... | collective-permute-start | bytes 1572872 | tf_op jit(solution)/shard_map/ppermute | solution.py:52
  75.8 1.5 %collective-permute-start.18 = (bf16[4,2,32,1024]{3,2,1,0:T(8,128)(2,1)S(1)}, bf16[4,2,32,1024]{3,2,1,0:T(8,128)(2,1)S(1)}, u32[]{:S(2)}, u32[]{:S(2)}) collective-permute-start(bf16[4,2,32,1024]{3,2,1,0:T(8,128)(2,1)S(1)} %get-tuple-element.63), channel_id=1, source_target_pairs={{0,16},{16,0},{1,17},{17,1},{2,18},{18,2},{3,19},{19,3},{4,20},{20... | collective-permute-start | bytes 1572872 | tf_op jit(solution)/shard_map/ppermute | solution.py:56
  77.3 12.2 %ffn.3 = (bf16[2,2,4,32,1024]{4,3,2,1,0:T(8,128)(2,1)S(1)}, bf16[2,2,4,32,1024]{4,3,2,1,0:T(8,128)(2,1)S(1)}, bf16[2,4,32,1024]{3,2,1,0:T(8,128)(2,1)S(1)}, bf16...) custom-call(s32[1]{0:T(128)} %bitcast.refs_0_, bf16[2,4,32,1024]{3,2,1,0:T(8,128)(2,1)S(1)} %pad_maximum_fusion.6.refs_1_, ...), custom_call_target="tpu_custom_call" | custom-call | flops 10000000000 | bytes 20000000 | tf_op jit(solution)/shard_map/ffn/pallas_call | solution.py:138
  90.2 1.4 %collective-permute-done.30 = bf16[2,4,32,1024]{3,2,1,0:T(8,128)(2,1)S(1)} collective-permute-done((bf16[2,4,32,1024]{3,2,1,0:T(8,128)(2,1)S(1)}, bf16[2,4,32,1024]{3,2,1,0:T(8,128)(2,1)S(1)}, u32[]{:S(2)}, u32[]{:S(2)}) %collective-permute-start.30) | collective-permute-done | bytes 524320 | tf_op jit(solution)/shard_map/ppermute | solution.py:52
  91.5 0.7 collective-permute-done.33
  92.7 1.0 collective-permute-start.31
  93.7 1.5 %collective-permute-start.34 = (bf16[2,4,32,1024]{3,2,1,0:T(8,128)(2,1)S(1)}, bf16[2,4,32,1024]{3,2,1,0:T(8,128)(2,1)S(1)}, u32[]{:S(2)}, u32[]{:S(2)}) collective-permute-start(bf16[2,4,32,1024]{3,2,1,0:T(8,128)(2,1)S(1)} %get-tuple-element.61), channel_id=1, source_target_pairs={{0,16},{16,0},{1,17},{17,1},{2,18},{18,2},{3,19},{19,3},{4,20},{20... | collective-permute-start | bytes 1572872 | tf_op jit(solution)/shard_map/ppermute | solution.py:56
  95.8 1.5 %collective-permute-start.19 = (bf16[2,4,32,1024]{3,2,1,0:T(8,128)(2,1)S(1)}, bf16[2,4,32,1024]{3,2,1,0:T(8,128)(2,1)S(1)}, u32[]{:S(2)}, u32[]{:S(2)}) collective-permute-start(bf16[2,4,32,1024]{3,2,1,0:T(8,128)(2,1)S(1)} %fusion.2), channel_id=1, source_target_pairs={{0,4},{1,5},{2,6},{3,7},{4,0},{5,1},{6,2},{7,3},{8,12},{9,13},{10,... | collective-permute-start | bytes 1572872 | tf_op jit(solution)/shard_map/ppermute | solution.py:52
  97.3 9.4 %collective-permute-done.31 = bf16[2,4,32,1024]{3,2,1,0:T(8,128)(2,1)S(1)} collective-permute-done((bf16[2,4,32,1024]{3,2,1,0:T(8,128)(2,1)S(1)}, bf16[2,4,32,1024]{3,2,1,0:T(8,128)(2,1)S(1)}, u32[]{:S(2)}, u32[]{:S(2)}) %collective-permute-start.31) | collective-permute-done | bytes 524320 | tf_op jit(solution)/shard_map/ppermute | solution.py:52
  106.7 0.6 collective-permute-done.34
  108.0 1.2 collective-permute-start.35
  109.2 1.6 %collective-permute-start.32 = (bf16[4,32,1024]{2,1,0:T(8,128)(2,1)S(1)}, bf16[4,32,1024]{2,1,0:T(8,128)(2,1)S(1)}, u32[]{:S(2)}, u32[]{:S(2)}) collective-permute-start(bf16[4,32,1024]{2,1,0:T(8,128)(2,1)S(1)} %fusion.12), channel_id=1, source_target_pairs={{0,16},{16,0},{1,17},{17,1},{2,18},{18,2},{3,19},{19,3},{4,20},{20... | collective-permute-start | bytes 786440 | tf_op jit(solution)/shard_map/ppermute | solution.py:56
  111.0 3.4 %collective-permute-start.20 = (bf16[1,4,32,1024]{3,2,1,0:T(8,128)(2,1)S(1)}, bf16[1,4,32,1024]{3,2,1,0:T(8,128)(2,1)S(1)}, u32[]{:S(2)}, u32[]{:S(2)}) collective-permute-start(bf16[1,4,32,1024]{3,2,1,0:T(8,128)(2,1)S(1)} %slice.246), channel_id=1, source_target_pairs={{0,8},{1,9},{2,10},{3,11},{4,12},{5,13},{6,14},{7,15},{8,0},{9,1},... | collective-permute-start | bytes 786440 | tf_op jit(solution)/shard_map/ppermute | solution.py:52
  114.4 0.8 collective-permute-done.35
  115.3 0.9 collective-permute-done.32
  116.3 1.5 %collective-permute-start.36 = (bf16[2,64,1024]{2,1,0:T(8,128)(2,1)S(1)}, bf16[2,64,1024]{2,1,0:T(8,128)(2,1)S(1)}, u32[]{:S(2)}, u32[]{:S(2)}) collective-permute-start(bf16[2,64,1024]{2,1,0:T(8,128)(2,1)S(1)} %fusion.9), channel_id=1, source_target_pairs={{0,4},{1,5},{2,6},{3,7},{4,0},{5,1},{6,2},{7,3},{8,12},{9,13},{10,... | collective-permute-start | bytes 786440 | tf_op jit(solution)/shard_map/ppermute | solution.py:52
  117.7 7.3 %collective-permute-done.20 = bf16[1,4,32,1024]{3,2,1,0:T(8,128)(2,1)S(1)} collective-permute-done((bf16[1,4,32,1024]{3,2,1,0:T(8,128)(2,1)S(1)}, bf16[1,4,32,1024]{3,2,1,0:T(8,128)(2,1)S(1)}, u32[]{:S(2)}, u32[]{:S(2)}) %collective-permute-start.20) | collective-permute-done | bytes 262176 | tf_op jit(solution)/shard_map/ppermute | solution.py:52
  125.7 0.9 collective-permute-start.22
  126.6 1.1 collective-permute-done.36
  128.1 1.4 %collective-permute-done.21 = bf16[32,1024]{1,0:T(8,128)(2,1)S(1)} collective-permute-done((bf16[32,1024]{1,0:T(8,128)(2,1)S(1)}, bf16[32,1024]{1,0:T(8,128)(2,1)S(1)}, u32[]{:S(2)}, u32[]{:S(2)}) %collective-permute-start.21) | collective-permute-done | bytes 65568 | tf_op jit(solution)/shard_map/ppermute | solution.py:56
  130.0 4.6 %collective-permute-done.37 = bf16[1,64,1024]{2,1,0:T(8,128)(2,1)S(1)} collective-permute-done((bf16[1,64,1024]{2,1,0:T(8,128)(2,1)S(1)}, bf16[1,64,1024]{2,1,0:T(8,128)(2,1)S(1)}, u32[]{:S(2)}, u32[]{:S(2)}) %collective-permute-start.37) | collective-permute-done | bytes 131104 | tf_op jit(solution)/shard_map/ppermute | solution.py:52
  134.6 0.7 pad_maximum_fusion.10
  (80 shorter events, 11.2 us)
Async XLA Ops:
  1.0 10.7 %collective-permute-start = (bf16[1,64,1024]{2,1,0:T(8,128)(2,1)S(1)}, bf16[1,64,1024]{2,1,0:T(8,128)(2,1)S(1)}, u32[]{:S(2)}, u32[]{:S(2)}) collective-permute-start(bf16[1,64,1024]{2,1,0:T(8,128)(2,1)S(1)} %get-tuple-element.73), channel_id=1, source_target_pairs={{0,8},{1,9},{2,10},{3,11},{4,12},{5,13},{6,14},{7,15},{8,0},{9,1},... | collective-permute-start | bytes 393224 | tf_op jit(solution)/shard_map/ppermute | solution.py:52
  7.8 10.3 %all-to-all-start = ((f32[16,1,128]{2,1,0:T(1,128)}), f32[16,1,128]{2,1,0:T(1,128)S(1)}, u32[]{:S(2)}, u32[]{:S(2)}) async-start(f32[16,1,128]{2,1,0:T(1,128)} %bitcast.5), calls=%async_computation | async-start | bytes 16384 | tf_op jit(solution)/shard_map/all_to_all | solution.py:181
  11.8 8.8 %collective-permute-start.1 = (bf16[2,64,1024]{2,1,0:T(8,128)(2,1)S(1)}, bf16[2,64,1024]{2,1,0:T(8,128)(2,1)S(1)}, u32[]{:S(2)}, u32[]{:S(2)}) collective-permute-start(bf16[2,64,1024]{2,1,0:T(8,128)(2,1)S(1)} %pad_maximum_fusion.8), channel_id=1, source_target_pairs={{0,4},{1,5},{2,6},{3,7},{4,0},{5,1},{6,2},{7,3},{8,12},{9,13},{10,... | collective-permute-start | bytes 786440 | tf_op jit(solution)/shard_map/ppermute | solution.py:52
  20.7 10.3 %collective-permute-start.3 = (bf16[1,4,32,1024]{3,2,1,0:T(8,128)(2,1)S(1)}, bf16[1,4,32,1024]{3,2,1,0:T(8,128)(2,1)S(1)}, u32[]{:S(2)}, u32[]{:S(2)}) collective-permute-start(bf16[1,4,32,1024]{3,2,1,0:T(8,128)(2,1)S(1)} %get-tuple-element.67), channel_id=1, source_target_pairs={{0,2},{1,3},{2,0},{3,1},{4,6},{5,7},{6,4},{7,5},{8,10},{9,11},{10,... | collective-permute-start | bytes 786440 | tf_op jit(solution)/shard_map/ppermute | solution.py:52
  22.4 8.2 %collective-permute-start.5 = (bf16[1,64,1024]{2,1,0:T(8,128)(2,1)S(1)}, bf16[1,64,1024]{2,1,0:T(8,128)(2,1)S(1)}, u32[]{:S(2)}, u32[]{:S(2)}) collective-permute-start(bf16[1,64,1024]{2,1,0:T(8,128)(2,1)S(1)} %get-tuple-element.32), channel_id=1, source_target_pairs={{0,8},{1,9},{2,10},{3,11},{4,12},{5,13},{6,14},{7,15},{8,0},{9,1},... | collective-permute-start | bytes 393224 | tf_op jit(solution)/shard_map/ppermute | solution.py:52
  24.7 7.0 %collective-permute-start.2 = (bf16[1,4,32,1024]{3,2,1,0:T(8,128)(2,1)S(1)}, bf16[1,4,32,1024]{3,2,1,0:T(8,128)(2,1)S(1)}, u32[]{:S(2)}, u32[]{:S(2)}) collective-permute-start(bf16[1,4,32,1024]{3,2,1,0:T(8,128)(2,1)S(1)} %get-tuple-element.68), channel_id=1, source_target_pairs={{0,16},{16,0},{1,17},{17,1},{2,18},{18,2},{3,19},{19,3},{4,20},{20... | collective-permute-start | bytes 786440 | tf_op jit(solution)/shard_map/ppermute | solution.py:56
  30.6 7.5 %collective-permute-start.6 = (bf16[2,64,1024]{2,1,0:T(8,128)(2,1)S(1)}, bf16[2,64,1024]{2,1,0:T(8,128)(2,1)S(1)}, u32[]{:S(2)}, u32[]{:S(2)}) collective-permute-start(bf16[2,64,1024]{2,1,0:T(8,128)(2,1)S(1)} %pad_maximum_fusion.9), channel_id=1, source_target_pairs={{0,4},{1,5},{2,6},{3,7},{4,0},{5,1},{6,2},{7,3},{8,12},{9,13},{10,... | collective-permute-start | bytes 786440 | tf_op jit(solution)/shard_map/ppermute | solution.py:52
  31.8 19.3 %collective-permute-start.11 = (bf16[2,4,32,1024]{3,2,1,0:T(8,128)(2,1)S(1)}, bf16[2,4,32,1024]{3,2,1,0:T(8,128)(2,1)S(1)}, u32[]{:S(2)}, u32[]{:S(2)}) collective-permute-start(bf16[2,4,32,1024]{3,2,1,0:T(8,128)(2,1)S(1)} %pad_maximum_fusion.4.refs_5_), channel_id=1, source_target_pairs={{0,16},{16,0},{1,17},{17,1},{2,18},{18,2},{3,19},{19,3},{4,20},{20... | collective-permute-start | bytes 1572872 | tf_op jit(solution)/shard_map/ppermute | solution.py:56
  33.4 17.7 %collective-permute-start.4 = (bf16[2,4,32,1024]{3,2,1,0:T(8,128)(2,1)S(1)}, bf16[2,4,32,1024]{3,2,1,0:T(8,128)(2,1)S(1)}, u32[]{:S(2)}, u32[]{:S(2)}) collective-permute-start(bf16[2,4,32,1024]{3,2,1,0:T(8,128)(2,1)S(1)} %pad_maximum_fusion.3.refs_1_), channel_id=1, source_target_pairs={{0,2},{1,3},{2,0},{3,1},{4,6},{5,7},{6,4},{7,5},{8,10},{9,11},{10,... | collective-permute-start | bytes 1572872 | tf_op jit(solution)/shard_map/ppermute | solution.py:52
  38.2 13.4 %copy-start.2 = (bf16[1,4,32,1024]{3,2,1,0:T(8,128)(2,1)}, bf16[1,4,32,1024]{3,2,1,0:T(8,128)(2,1)S(1)}, u32[]{:S(2)}) copy-start(bf16[1,4,32,1024]{3,2,1,0:T(8,128)(2,1)S(1)} %get-tuple-element.69) | copy-start | bytes 786436
  38.2 11.7 %collective-permute-start.7 = (bf16[1,4,32,1024]{3,2,1,0:T(8,128)(2,1)S(1)}, bf16[1,4,32,1024]{3,2,1,0:T(8,128)(2,1)S(1)}, u32[]{:S(2)}, u32[]{:S(2)}) collective-permute-start(bf16[1,4,32,1024]{3,2,1,0:T(8,128)(2,1)S(1)} %get-tuple-element.70), channel_id=1, source_target_pairs={{0,16},{16,0},{1,17},{17,1},{2,18},{18,2},{3,19},{19,3},{4,20},{20... | collective-permute-start | bytes 786440 | tf_op jit(solution)/shard_map/ppermute | solution.py:56
  39.8 11.3 %collective-permute-start.8 = (bf16[1,4,32,1024]{3,2,1,0:T(8,128)(2,1)S(1)}, bf16[1,4,32,1024]{3,2,1,0:T(8,128)(2,1)S(1)}, u32[]{:S(2)}, u32[]{:S(2)}) collective-permute-start(bf16[1,4,32,1024]{3,2,1,0:T(8,128)(2,1)S(1)} %get-tuple-element.69), channel_id=1, source_target_pairs={{0,2},{1,3},{2,0},{3,1},{4,6},{5,7},{6,4},{7,5},{8,10},{9,11},{10,... | collective-permute-start | bytes 786440 | tf_op jit(solution)/shard_map/ppermute | solution.py:52
  40.6 14.3 %collective-permute-start.12 = (bf16[2,4,32,1024]{3,2,1,0:T(8,128)(2,1)S(1)}, bf16[2,4,32,1024]{3,2,1,0:T(8,128)(2,1)}, u32[]{:S(2)}, u32[]{:S(2)}) collective-permute-start(bf16[2,4,32,1024]{3,2,1,0:T(8,128)(2,1)S(1)} %pad_maximum_fusion.4.refs_5_), channel_id=1, source_target_pairs={{0,1},{1,0},{2,3},{3,2},{4,5},{5,4},{6,7},{7,6},{8,9},{9,8},{10,11... | collective-permute-start | bytes 1572872 | tf_op jit(solution)/shard_map/ppermute | solution.py:52
  49.9 1.7 %copy-start.3 = (bf16[1,4,32,1024]{3,2,1,0:T(8,128)(2,1)}, bf16[1,4,32,1024]{3,2,1,0:T(8,128)(2,1)S(1)}, u32[]{:S(2)}) copy-start(bf16[1,4,32,1024]{3,2,1,0:T(8,128)(2,1)S(1)} %collective-permute-done.7) | copy-start | bytes 786436
  49.9 5.6 %collective-permute-start.9 = (bf16[2,4,32,1024]{3,2,1,0:T(8,128)(2,1)S(1)}, bf16[2,4,32,1024]{3,2,1,0:T(8,128)(2,1)}, u32[]{:S(2)}, u32[]{:S(2)}) collective-permute-start(bf16[2,4,32,1024]{3,2,1,0:T(8,128)(2,1)S(1)} %pad_maximum_fusion.3.refs_1_), channel_id=1, source_target_pairs={{0,1},{1,0},{2,3},{3,2},{4,5},{5,4},{6,7},{7,6},{8,9},{9,8},{10,11... | collective-permute-start | bytes 1572872 | tf_op jit(solution)/shard_map/ppermute | solution.py:52
  51.1 0.7 copy-start.4
  51.1 4.4 %collective-permute-start.13 = (bf16[2,4,32,1024]{3,2,1,0:T(8,128)(2,1)S(1)}, bf16[2,4,32,1024]{3,2,1,0:T(8,128)(2,1)}, u32[]{:S(2)}, u32[]{:S(2)}) collective-permute-start(bf16[2,4,32,1024]{3,2,1,0:T(8,128)(2,1)S(1)} %collective-permute-done.11.refs_6_), channel_id=1, source_target_pairs={{0,1},{1,0},{2,3},{3,2},{4,5},{5,4},{6,7},{7,6},{8,9},{9,8},{10,11... | collective-permute-start | bytes 1572872 | tf_op jit(solution)/shard_map/ppermute | solution.py:52
  51.1 4.4 %collective-permute-start.10 = (bf16[2,4,32,1024]{3,2,1,0:T(8,128)(2,1)S(1)}, bf16[2,4,32,1024]{3,2,1,0:T(8,128)(2,1)}, u32[]{:S(2)}, u32[]{:S(2)}) collective-permute-start(bf16[2,4,32,1024]{3,2,1,0:T(8,128)(2,1)S(1)} %collective-permute-done.4.refs_2_), channel_id=1, source_target_pairs={{0,1},{1,0},{2,3},{3,2},{4,5},{5,4},{6,7},{7,6},{8,9},{9,8},{10,11... | collective-permute-start | bytes 1572872 | tf_op jit(solution)/shard_map/ppermute | solution.py:52
  54.3 17.1 %collective-permute-start.26 = (bf16[2,4,32,1024]{3,2,1,0:T(8,128)(2,1)S(1)}, bf16[2,4,32,1024]{3,2,1,0:T(8,128)(2,1)S(1)}, u32[]{:S(2)}, u32[]{:S(2)}) collective-permute-start(bf16[2,4,32,1024]{3,2,1,0:T(8,128)(2,1)S(1)} %pad_maximum_fusion.7.refs_5_), channel_id=1, source_target_pairs={{0,16},{16,0},{1,17},{17,1},{2,18},{18,2},{3,19},{19,3},{4,20},{20... | collective-permute-start | bytes 1572872 | tf_op jit(solution)/shard_map/ppermute | solution.py:56
  54.9 17.1 %collective-permute-start.23 = (bf16[2,4,32,1024]{3,2,1,0:T(8,128)(2,1)S(1)}, bf16[2,4,32,1024]{3,2,1,0:T(8,128)(2,1)S(1)}, u32[]{:S(2)}, u32[]{:S(2)}) collective-permute-start(bf16[2,4,32,1024]{3,2,1,0:T(8,128)(2,1)S(1)} %pad_maximum_fusion.6.refs_1_), channel_id=1, source_target_pairs={{0,2},{1,3},{2,0},{3,1},{4,6},{5,7},{6,4},{7,5},{8,10},{9,11},{10,... | collective-permute-start | bytes 1572872 | tf_op jit(solution)/shard_map/ppermute | solution.py:52
  55.5 1.9 %copy-start = (bf16[1,768,2048]{2,1,0:T(8,128)(2,1)S(1)}, bf16[1,768,2048]{2,1,0:T(8,128)(2,1)}, u32[]{:S(2)}) copy-start(bf16[1,768,2048]{2,1,0:T(8,128)(2,1)} %refs_10_.3) | copy-start | bytes 9437188
  70.9 6.5 %copy-start.1 = (bf16[1,768,2048]{2,1,0:T(8,128)(2,1)S(1)}, bf16[1,768,2048]{2,1,0:T(8,128)(2,1)}, u32[]{:S(2)}) copy-start(bf16[1,768,2048]{2,1,0:T(8,128)(2,1)} %refs_10_.3) | copy-start | bytes 9437188
  70.9 2.0 %collective-permute-start.15 = (bf16[4,2,32,1024]{3,2,1,0:T(8,128)(2,1)S(1)}, bf16[4,2,32,1024]{3,2,1,0:T(8,128)(2,1)S(1)}, u32[]{:S(2)}, u32[]{:S(2)}) collective-permute-start(bf16[4,2,32,1024]{3,2,1,0:T(8,128)(2,1)S(1)} %get-tuple-element.40), channel_id=1, source_target_pairs={{0,1},{1,0},{2,3},{3,2},{4,5},{5,4},{6,7},{7,6},{8,9},{9,8},{10,11... | collective-permute-start | bytes 1572872 | tf_op jit(solution)/shard_map/ppermute | solution.py:52
  70.9 2.6 %collective-permute-start.17 = (bf16[4,2,32,1024]{3,2,1,0:T(8,128)(2,1)S(1)}, bf16[4,2,32,1024]{3,2,1,0:T(8,128)(2,1)S(1)}, u32[]{:S(2)}, u32[]{:S(2)}) collective-permute-start(bf16[4,2,32,1024]{3,2,1,0:T(8,128)(2,1)S(1)} %get-tuple-element.41), channel_id=1, source_target_pairs={{0,1},{1,0},{2,3},{3,2},{4,5},{5,4},{6,7},{7,6},{8,9},{9,8},{10,11... | collective-permute-start | bytes 1572872 | tf_op jit(solution)/shard_map/ppermute | solution.py:52
  71.5 2.9 %collective-permute-start.28 = (bf16[2,4,32,1024]{3,2,1,0:T(8,128)(2,1)S(1)}, bf16[2,4,32,1024]{3,2,1,0:T(8,128)(2,1)S(1)}, u32[]{:S(2)}, u32[]{:S(2)}) collective-permute-start(bf16[2,4,32,1024]{3,2,1,0:T(8,128)(2,1)S(1)} %collective-permute-done.26.refs_6_), channel_id=1, source_target_pairs={{0,1},{1,0},{2,3},{3,2},{4,5},{5,4},{6,7},{7,6},{8,9},{9,8},{10,11... | collective-permute-start | bytes 1572872 | tf_op jit(solution)/shard_map/ppermute | solution.py:52
  71.5 4.3 %collective-permute-start.27 = (bf16[2,4,32,1024]{3,2,1,0:T(8,128)(2,1)S(1)}, bf16[2,4,32,1024]{3,2,1,0:T(8,128)(2,1)S(1)}, u32[]{:S(2)}, u32[]{:S(2)}) collective-permute-start(bf16[2,4,32,1024]{3,2,1,0:T(8,128)(2,1)S(1)} %pad_maximum_fusion.7.refs_5_), channel_id=1, source_target_pairs={{0,1},{1,0},{2,3},{3,2},{4,5},{5,4},{6,7},{7,6},{8,9},{9,8},{10,11... | collective-permute-start | bytes 1572872 | tf_op jit(solution)/shard_map/ppermute | solution.py:52
  72.0 5.3 %collective-permute-start.25 = (bf16[2,4,32,1024]{3,2,1,0:T(8,128)(2,1)S(1)}, bf16[2,4,32,1024]{3,2,1,0:T(8,128)(2,1)S(1)}, u32[]{:S(2)}, u32[]{:S(2)}) collective-permute-start(bf16[2,4,32,1024]{3,2,1,0:T(8,128)(2,1)S(1)} %collective-permute-done.23.refs_2_), channel_id=1, source_target_pairs={{0,1},{1,0},{2,3},{3,2},{4,5},{5,4},{6,7},{7,6},{8,9},{9,8},{10,11... | collective-permute-start | bytes 1572872 | tf_op jit(solution)/shard_map/ppermute | solution.py:52
  72.8 4.5 %collective-permute-start.24 = (bf16[2,4,32,1024]{3,2,1,0:T(8,128)(2,1)S(1)}, bf16[2,4,32,1024]{3,2,1,0:T(8,128)(2,1)S(1)}, u32[]{:S(2)}, u32[]{:S(2)}) collective-permute-start(bf16[2,4,32,1024]{3,2,1,0:T(8,128)(2,1)S(1)} %pad_maximum_fusion.6.refs_1_), channel_id=1, source_target_pairs={{0,1},{1,0},{2,3},{3,2},{4,5},{5,4},{6,7},{7,6},{8,9},{9,8},{10,11... | collective-permute-start | bytes 1572872 | tf_op jit(solution)/shard_map/ppermute | solution.py:52
  73.6 21.6 %collective-permute-start.14 = (bf16[2,4,2,32,1024]{4,3,2,1,0:T(8,128)(2,1)S(1)}, bf16[2,4,2,32,1024]{4,3,2,1,0:T(8,128)(2,1)S(1)}, u32[]{:S(2)}, u32[]{:S(2)}) collective-permute-start(bf16[2,4,2,32,1024]{4,3,2,1,0:T(8,128)(2,1)S(1)} %get-tuple-element.38), channel_id=1, source_target_pairs={{0,1},{1,0},{2,3},{3,2},{4,5},{5,4},{6,7},{7,6},{8,9},{9,8},{10,11... | collective-permute-start | bytes 3145736 | tf_op jit(solution)/shard_map/ppermute | solution.py:52
  74.3 15.1 %collective-permute-start.16 = (bf16[4,2,32,1024]{3,2,1,0:T(8,128)(2,1)S(1)}, bf16[4,2,32,1024]{3,2,1,0:T(8,128)(2,1)S(1)}, u32[]{:S(2)}, u32[]{:S(2)}) collective-permute-start(bf16[4,2,32,1024]{3,2,1,0:T(8,128)(2,1)S(1)} %get-tuple-element.64), channel_id=1, source_target_pairs={{0,2},{1,3},{2,0},{3,1},{4,6},{5,7},{6,4},{7,5},{8,10},{9,11},{10,... | collective-permute-start | bytes 1572872 | tf_op jit(solution)/shard_map/ppermute | solution.py:52
  75.8 13.8 %collective-permute-start.18 = (bf16[4,2,32,1024]{3,2,1,0:T(8,128)(2,1)S(1)}, bf16[4,2,32,1024]{3,2,1,0:T(8,128)(2,1)S(1)}, u32[]{:S(2)}, u32[]{:S(2)}) collective-permute-start(bf16[4,2,32,1024]{3,2,1,0:T(8,128)(2,1)S(1)} %get-tuple-element.63), channel_id=1, source_target_pairs={{0,16},{16,0},{1,17},{17,1},{2,18},{18,2},{3,19},{19,3},{4,20},{20... | collective-permute-start | bytes 1572872 | tf_op jit(solution)/shard_map/ppermute | solution.py:56
  89.6 1.9 %collective-permute-start.30 = (bf16[2,4,32,1024]{3,2,1,0:T(8,128)(2,1)S(1)}, bf16[2,4,32,1024]{3,2,1,0:T(8,128)(2,1)S(1)}, u32[]{:S(2)}, u32[]{:S(2)}) collective-permute-start(bf16[2,4,32,1024]{3,2,1,0:T(8,128)(2,1)S(1)} %get-tuple-element.52), channel_id=1, source_target_pairs={{0,1},{1,0},{2,3},{3,2},{4,5},{5,4},{6,7},{7,6},{8,9},{9,8},{10,11... | collective-permute-start | bytes 1572872 | tf_op jit(solution)/shard_map/ppermute | solution.py:52
  89.6 2.7 %collective-permute-start.33 = (bf16[2,4,32,1024]{3,2,1,0:T(8,128)(2,1)S(1)}, bf16[2,4,32,1024]{3,2,1,0:T(8,128)(2,1)S(1)}, u32[]{:S(2)}, u32[]{:S(2)}) collective-permute-start(bf16[2,4,32,1024]{3,2,1,0:T(8,128)(2,1)S(1)} %get-tuple-element.54), channel_id=1, source_target_pairs={{0,1},{1,0},{2,3},{3,2},{4,5},{5,4},{6,7},{7,6},{8,9},{9,8},{10,11... | collective-permute-start | bytes 1572872 | tf_op jit(solution)/shard_map/ppermute | solution.py:52
  90.1 7.2 %collective-permute-start.29 = (bf16[2,2,4,32,1024]{4,3,2,1,0:T(8,128)(2,1)S(1)}, bf16[2,2,4,32,1024]{4,3,2,1,0:T(8,128)(2,1)S(1)}, u32[]{:S(2)}, u32[]{:S(2)}) collective-permute-start(bf16[2,2,4,32,1024]{4,3,2,1,0:T(8,128)(2,1)S(1)} %get-tuple-element.49), channel_id=1, source_target_pairs={{0,1},{1,0},{2,3},{3,2},{4,5},{5,4},{6,7},{7,6},{8,9},{9,8},{10,11... | collective-permute-start | bytes 3145736 | tf_op jit(solution)/shard_map/ppermute | solution.py:52
  92.7 14.0 %collective-permute-start.31 = (bf16[2,4,32,1024]{3,2,1,0:T(8,128)(2,1)S(1)}, bf16[2,4,32,1024]{3,2,1,0:T(8,128)(2,1)S(1)}, u32[]{:S(2)}, u32[]{:S(2)}) collective-permute-start(bf16[2,4,32,1024]{3,2,1,0:T(8,128)(2,1)S(1)} %get-tuple-element.62), channel_id=1, source_target_pairs={{0,2},{1,3},{2,0},{3,1},{4,6},{5,7},{6,4},{7,5},{8,10},{9,11},{10,... | collective-permute-start | bytes 1572872 | tf_op jit(solution)/shard_map/ppermute | solution.py:52
  93.7 13.7 %collective-permute-start.34 = (bf16[2,4,32,1024]{3,2,1,0:T(8,128)(2,1)S(1)}, bf16[2,4,32,1024]{3,2,1,0:T(8,128)(2,1)S(1)}, u32[]{:S(2)}, u32[]{:S(2)}) collective-permute-start(bf16[2,4,32,1024]{3,2,1,0:T(8,128)(2,1)S(1)} %get-tuple-element.61), channel_id=1, source_target_pairs={{0,16},{16,0},{1,17},{17,1},{2,18},{18,2},{3,19},{19,3},{4,20},{20... | collective-permute-start | bytes 1572872 | tf_op jit(solution)/shard_map/ppermute | solution.py:56
  95.8 14.9 %collective-permute-start.19 = (bf16[2,4,32,1024]{3,2,1,0:T(8,128)(2,1)S(1)}, bf16[2,4,32,1024]{3,2,1,0:T(8,128)(2,1)S(1)}, u32[]{:S(2)}, u32[]{:S(2)}) collective-permute-start(bf16[2,4,32,1024]{3,2,1,0:T(8,128)(2,1)S(1)} %fusion.2), channel_id=1, source_target_pairs={{0,4},{1,5},{2,6},{3,7},{4,0},{5,1},{6,2},{7,3},{8,12},{9,13},{10,... | collective-permute-start | bytes 1572872 | tf_op jit(solution)/shard_map/ppermute | solution.py:52
  108.0 7.3 %collective-permute-start.35 = (bf16[4,32,1024]{2,1,0:T(8,128)(2,1)S(1)}, bf16[4,32,1024]{2,1,0:T(8,128)(2,1)S(1)}, u32[]{:S(2)}, u32[]{:S(2)}) collective-permute-start(bf16[4,32,1024]{2,1,0:T(8,128)(2,1)S(1)} %fusion.13), channel_id=1, source_target_pairs={{0,2},{1,3},{2,0},{3,1},{4,6},{5,7},{6,4},{7,5},{8,10},{9,11},{10,... | collective-permute-start | bytes 786440 | tf_op jit(solution)/shard_map/ppermute | solution.py:52
  109.2 7.0 %collective-permute-start.32 = (bf16[4,32,1024]{2,1,0:T(8,128)(2,1)S(1)}, bf16[4,32,1024]{2,1,0:T(8,128)(2,1)S(1)}, u32[]{:S(2)}, u32[]{:S(2)}) collective-permute-start(bf16[4,32,1024]{2,1,0:T(8,128)(2,1)S(1)} %fusion.12), channel_id=1, source_target_pairs={{0,16},{16,0},{1,17},{17,1},{2,18},{18,2},{3,19},{19,3},{4,20},{20... | collective-permute-start | bytes 786440 | tf_op jit(solution)/shard_map/ppermute | solution.py:56
  111.0 14.1 %collective-permute-start.20 = (bf16[1,4,32,1024]{3,2,1,0:T(8,128)(2,1)S(1)}, bf16[1,4,32,1024]{3,2,1,0:T(8,128)(2,1)S(1)}, u32[]{:S(2)}, u32[]{:S(2)}) collective-permute-start(bf16[1,4,32,1024]{3,2,1,0:T(8,128)(2,1)S(1)} %slice.246), channel_id=1, source_target_pairs={{0,8},{1,9},{2,10},{3,11},{4,12},{5,13},{6,14},{7,15},{8,0},{9,1},... | collective-permute-start | bytes 786440 | tf_op jit(solution)/shard_map/ppermute | solution.py:52
  116.3 11.5 %collective-permute-start.36 = (bf16[2,64,1024]{2,1,0:T(8,128)(2,1)S(1)}, bf16[2,64,1024]{2,1,0:T(8,128)(2,1)S(1)}, u32[]{:S(2)}, u32[]{:S(2)}) collective-permute-start(bf16[2,64,1024]{2,1,0:T(8,128)(2,1)S(1)} %fusion.9), channel_id=1, source_target_pairs={{0,4},{1,5},{2,6},{3,7},{4,0},{5,1},{6,2},{7,3},{8,12},{9,13},{10,... | collective-permute-start | bytes 786440 | tf_op jit(solution)/shard_map/ppermute | solution.py:52
  125.1 4.3 %collective-permute-start.21 = (bf16[32,1024]{1,0:T(8,128)(2,1)S(1)}, bf16[32,1024]{1,0:T(8,128)(2,1)S(1)}, u32[]{:S(2)}, u32[]{:S(2)}) collective-permute-start(bf16[32,1024]{1,0:T(8,128)(2,1)S(1)} %get-tuple-element.71), channel_id=1, source_target_pairs={{0,16},{16,0},{1,17},{17,1},{2,18},{18,2},{3,19},{19,3},{4,20},{20... | collective-permute-start | bytes 196616 | tf_op jit(solution)/shard_map/ppermute | solution.py:56
  125.7 4.3 %collective-permute-start.22 = (bf16[32,1024]{1,0:T(8,128)(2,1)S(1)}, bf16[32,1024]{1,0:T(8,128)(2,1)S(1)}, u32[]{:S(2)}, u32[]{:S(2)}) collective-permute-start(bf16[32,1024]{1,0:T(8,128)(2,1)S(1)} %get-tuple-element.72), channel_id=1, source_target_pairs={{0,2},{1,3},{2,0},{3,1},{4,6},{5,7},{6,4},{7,5},{8,10},{9,11},{10,... | collective-permute-start | bytes 196616 | tf_op jit(solution)/shard_map/ppermute | solution.py:52
  127.8 6.8 %collective-permute-start.37 = (bf16[1,64,1024]{2,1,0:T(8,128)(2,1)S(1)}, bf16[1,64,1024]{2,1,0:T(8,128)(2,1)S(1)}, u32[]{:S(2)}, u32[]{:S(2)}) collective-permute-start(bf16[1,64,1024]{2,1,0:T(8,128)(2,1)S(1)} %slice.247), channel_id=1, source_target_pairs={{0,8},{1,9},{2,10},{3,11},{4,12},{5,13},{6,14},{7,15},{8,0},{9,1},... | collective-permute-start | bytes 393224 | tf_op jit(solution)/shard_map/ppermute | solution.py:52
